TPU v7x, 32 devices: a whole 2x2x4 slice. The times are simulated.
32 devices in a mesh: sect: 4 (over y, core), dir: 8 (over z, x).
Axes of the slice: x: 2, y: 2, z: 4, core: 2. Of those that a mesh axis runs over, the one named last changes fastest.
Arguments:
- unknowns: bfloat16 [2, 8, 16, 128, 256], P(None, 'sect', 'dir'), may hold values from -6 to 6
- leaf_live: int32 [8, 16], P('sect', 'dir'), may hold values from 0 to 1, as said below
- near_blocks: bfloat16 [2, 8, 16, 9, 128, 128], P(None, 'sect', 'dir'), may hold values from -0.125 to 0.125
- aggregate: bfloat16 [2, 8, 16, 512, 128], P(None, 'sect', 'dir'), may hold values from -0.1875 to 0.1875
- disaggregate: bfloat16 [2, 8, 16, 128, 512], P(None, 'sect', 'dir'), may hold values from -0.1875 to 0.1875
- translate: float32 [16, 2, 512], P(None, None, 'dir'), may hold values from -1.2 to 1.2
Outputs:
- field: float32 [2, 8, 16, 128, 256], P(None, 'sect', 'dir')
Inputs may be any that keep to these rules, and one draw needn't show every extreme that they name: `leaf_live`: every 2 x 2 block of leaves (one coarse box) has its first leaf live; in every draw some box has all four leaves live.
All inputs are finite; a program needn't handle non-finite values.
Results may differ from a plain program's by a relative error of at most 0.0036.
Values may be sent and summed in bfloat16 or wider, within the bound.
No kernel may reach another device: no remote copies, remote signals or barrier semaphores. Data moves between devices by JAX's collectives and lax.ppermute only.
A program may use at most 64 MiB of HBM per device.

v0:
```python
import jax
import jax.numpy as jnp
from jax import lax
from jax.sharding import PartitionSpec as P

far_offsets = [
    (row_step, col_step)
    for row_step in range(-2, 3)
    for col_step in range(-2, 3)
    if max(abs(row_step), abs(col_step)) == 2
]


def with_halo(cells, sides, width):
    for axis, dim in sides:
        count = lax.axis_size(axis)
        ends = count - 1
        head = lax.slice_in_dim(cells, 0, width, axis=dim)
        tail = lax.slice_in_dim(cells, cells.shape[dim] - width, cells.shape[dim], axis=dim)
        cells = jnp.concatenate(
            [
                lax.ppermute(tail, axis, [(i, (i + 1) % count) for i in range(ends)]),
                cells,
                lax.ppermute(head, axis, [((i + 1) % count, i) for i in range(ends)]),
            ],
            axis=dim,
        )
    return cells


def complex_product(form, left, right):
    real = jnp.einsum(form, left[0], right[0], preferred_element_type=jnp.float32) - jnp.einsum(
        form, left[1], right[1], preferred_element_type=jnp.float32
    )
    imag = jnp.einsum(form, left[0], right[1], preferred_element_type=jnp.float32) + jnp.einsum(
        form, left[1], right[0], preferred_element_type=jnp.float32
    )
    return jnp.stack([real, imag])


def translate_grid(sources, coefs):
    box_rows = sources.shape[0]
    box_cols = sources.shape[1]
    widened = jnp.pad(sources.astype(jnp.float32), ((2, 2), (2, 2), (0, 0), (0, 0), (0, 0)))
    accum = jnp.zeros(sources.shape, jnp.float32)
    for row_step in range(-2, 3):
        total = jnp.zeros(sources.shape, jnp.float32)
        for index, (step_row, step_col) in enumerate(far_offsets):
            if step_row == row_step:
                shifted = widened[
                    2 + step_row : 2 + step_row + box_rows, 2 + step_col : 2 + step_col + box_cols
                ]
                coef_real = coefs[index, 0][None, None, :, None]
                coef_imag = coefs[index, 1][None, None, :, None]
                real = coef_real * shifted[:, :, 0] - coef_imag * shifted[:, :, 1]
                imag = coef_real * shifted[:, :, 1] + coef_imag * shifted[:, :, 0]
                total = total + jnp.stack([real, imag], axis=2)
        rounded = lax.optimization_barrier(total.astype(jnp.bfloat16))
        accum = accum + rounded.astype(jnp.float32)
    return accum.astype(jnp.bfloat16)


def shards(unknowns, leaf_live, near_blocks, aggregate, disaggregate, translate):
    live = leaf_live.astype(jnp.float32)[None, :, :, None, None]
    masked = (unknowns.astype(jnp.float32) * live).astype(jnp.bfloat16)
    base = complex_product("uvqn,uvnr->qr", aggregate, masked).astype(jnp.bfloat16)
    padded = with_halo(masked, (("sect", 1), ("dir", 2)), 1)
    pieces = []
    for row_step in range(-1, 2):
        for col_step in range(-1, 2):
            pieces.append(padded[:, 1 + row_step : 3 + row_step, 1 + col_step : 3 + col_step])
    beside = jnp.stack(pieces, axis=3)
    near = complex_product("uvkmn,uvknr->uvmr", near_blocks, beside)
    sect_count = lax.axis_size("sect")
    dir_count = lax.axis_size("dir")
    total_dirs = base.shape[1]
    sides = base.shape[2]
    narrow = total_dirs // (sect_count * dir_count)
    reordered = (
        base.reshape(2, dir_count, sect_count, narrow, sides)
        .transpose(0, 2, 1, 3, 4)
        .reshape(2, total_dirs, sides)[None, None]
    )
    spread = lax.all_to_all(
        lax.all_to_all(reordered, "sect", split_axis=3, concat_axis=0, tiled=True),
        "dir",
        split_axis=3,
        concat_axis=1,
        tiled=True,
    )
    coefs = lax.dynamic_slice_in_dim(translate, lax.axis_index("sect") * narrow, narrow, 2)
    incoming_all = translate_grid(spread, coefs)
    returned = lax.all_to_all(
        lax.all_to_all(incoming_all, "sect", split_axis=0, concat_axis=3, tiled=True),
        "dir",
        split_axis=1,
        concat_axis=3,
        tiled=True,
    )[0, 0]
    far = complex_product("uvmq,qr->uvmr", disaggregate, returned)
    return (near + far) * live


def solution(mesh):
    in_specs = (
        P(None, "sect", "dir", None, None),
        P("sect", "dir"),
        P(None, "sect", "dir", None, None, None),
        P(None, "sect", "dir", None, None),
        P(None, "sect", "dir", None, None),
        P(None, None, "dir"),
    )
    out_specs = P(None, "sect", "dir", None, None)
    return jax.shard_map(shards, mesh=mesh, in_specs=in_specs, out_specs=out_specs, check_vma=False)
```

profile of v0, /device:TPU:0, one launch (start us, length us, event | category | flops | bytes accessed | tf_op | source)
XLA Modules:
  0.0 98.9 jit_solution(5334588564130951844)
XLA Ops:
  0.0 1.4 %copy.36 = bf16[2,2,2,128,256]{3,4,2,1,0:T(8,128)(2,1)S(1)} copy(bf16[2,2,2,128,256]{4,3,2,1,0:T(8,128)(2,1)} %param.6) | data formatting | bytes 1048576 | tf_op args[0]
  2.3 1.3 %collective-permute-start.1 = (bf16[2,1,2,128,256]{3,4,2,1,0:T(8,128)(2,1)S(1)}, bf16[2,1,2,128,256]{3,4,2,1,0:T(8,128)(2,1)S(1)}, u32[]{:S(2)}, u32[]{:S(2)}) collective-permute-start(bf16[2,1,2,128,256]{3,4,2,1,0:T(8,128)(2,1)S(1)} %get-tuple-element.64), channel_id=1, source_target_pairs={{8,0},{16,8},{24,16},{9,1},{17,9},{25,17},{10,2},{18,10},{26,18},{... | collective-permute-start | bytes 786440 | tf_op jit(solution)/shard_map/ppermute | solution.py:24
  3.6 3.0 %collective-permute-start = (bf16[2,1,2,128,256]{3,4,2,1,0:T(8,128)(2,1)S(1)}, bf16[2,1,2,128,256]{3,4,2,1,0:T(8,128)(2,1)S(1)}, u32[]{:S(2)}, u32[]{:S(2)}) collective-permute-start(bf16[2,1,2,128,256]{3,4,2,1,0:T(8,128)(2,1)S(1)} %get-tuple-element.63), channel_id=1, source_target_pairs={{0,8},{8,16},{16,24},{1,9},{9,17},{17,25},{2,10},{10,18},{18,26},{... | collective-permute-start | bytes 786440 | tf_op jit(solution)/shard_map/ppermute | solution.py:22
  7.9 1.1 %fusion.85 = (bf16[2,4,1,128,256]{3,4,2,1,0:T(8,128)(2,1)}, bf16[2,4,1,128,256]{3,4,2,1,0:T(8,128)(2,1)}) fusion(bf16[2,4,2,128,256]{3,4,2,1,0:T(8,128)(2,1)S(1)} %pad_maximum_fusion.1), kind=kLoop, calls=%fused_computation.183 | loop fusion | bytes 2097152 | tf_op jit(solution)/shard_map/slice | solution.py:18
  9.0 1.3 %collective-permute-start.3 = (bf16[2,4,1,128,256]{3,4,2,1,0:T(8,128)(2,1)}, bf16[2,4,1,128,256]{3,4,2,1,0:T(8,128)(2,1)}, u32[]{:S(2)}, u32[]{:S(2)}) collective-permute-start(bf16[2,4,1,128,256]{3,4,2,1,0:T(8,128)(2,1)} %get-tuple-element.59), channel_id=1, source_target_pairs={{1,0},{2,1},{3,2},{4,3},{5,4},{6,5},{7,6},{9,8},{10,9},{11,10},{12... | collective-permute-start | bytes 1572872 | tf_op jit(solution)/shard_map/ppermute | solution.py:24
  10.3 6.3 %collective-permute-start.2 = (bf16[2,4,1,128,256]{3,4,2,1,0:T(8,128)(2,1)}, bf16[2,4,1,128,256]{3,4,2,1,0:T(8,128)(2,1)}, u32[]{:S(2)}, u32[]{:S(2)}) collective-permute-start(bf16[2,4,1,128,256]{3,4,2,1,0:T(8,128)(2,1)} %get-tuple-element.60), channel_id=1, source_target_pairs={{0,1},{1,2},{2,3},{3,4},{4,5},{5,6},{6,7},{8,9},{9,10},{10,11},{11... | collective-permute-start | bytes 1572872 | tf_op jit(solution)/shard_map/ppermute | solution.py:22
  16.6 1.1 %fusion.22 = bf16[512,256]{0,1:T(8,128)(2,1)} fusion(f32[256,512]{1,0:T(8,128)S(1)} %convolution_bitcast_fusion.2, bf16[2,2,2,512,128]{4,3,2,1,0:T(8,128)(2,1)S(1)} %copy-done, bf16[2,2,2,128,256]{3,4,2,1,0:T(8,128)(2,1)S(1)} %multiply_convert_fusion), kind=kOutput, calls=%fused_computation.33 | convolution fusion | flops 134479872 | bytes 1572864 | tf_op jit(solution)/shard_map/uvqn,uvnr->qr/dot_general | solution.py:32
  17.8 1.1 %copy.45 = bf16[512,256]{1,0:T(8,128)(2,1)S(1)} copy(bf16[512,256]{0,1:T(8,128)(2,1)} %fusion.22) | data formatting | bytes 524288 | tf_op jit(solution)/shard_map/sub | solution.py:32
  19.0 1.3 %copy.48 = bf16[1,1,2,512,256]{4,2,1,0,3:T(2,128)(2,1)} copy(bf16[1,1,2,512,256]{4,3,2,1,0:T(8,128)(2,1)S(1)} %bitcast.291) | data formatting | bytes 1048576 | tf_op jit(solution)/shard_map/broadcast_in_dim;reshape | solution.py:80
  20.3 7.4 %all-to-all-start = ((bf16[1,1,2,512,256]{4,2,1,0,3:T(2,128)(2,1)}), bf16[1,1,2,512,256]{4,2,1,0,3:T(2,128)(2,1)S(1)}, u32[]{:S(2)}, u32[]{:S(2)}) async-start(bf16[1,1,2,512,256]{4,2,1,0,3:T(2,128)(2,1)} %copy.48), calls=%async_computation | async-start | bytes 1048576 | tf_op jit(solution)/shard_map/all_to_all | solution.py:85
  27.9 8.7 %all-to-all-done = bf16[1,1,2,512,256]{4,2,1,0,3:T(2,128)(2,1)S(1)} async-done(((bf16[1,1,2,512,256]{4,2,1,0,3:T(2,128)(2,1)}), bf16[1,1,2,512,256]{4,2,1,0,3:T(2,128)(2,1)S(1)}, u32[]{:S(2)}, u32[]{:S(2)}) %all-to-all-start) | async-done | bytes 524320 | tf_op jit(solution)/shard_map/all_to_all | solution.py:85
  36.6 1.2 %copy.78 = bf16[1,1,2,4,128,256]{5,2,3,4,1,0:T(2,128)(2,1)} copy(bf16[1,1,2,4,128,256]{5,2,4,3,1,0:T(2,128)(2,1)S(1)} %bitcast.288) | data formatting | bytes 1048576 | tf_op jit(solution)/shard_map/all_to_all | solution.py:85
  37.8 4.9 %all-to-all-start.1 = ((bf16[4,1,2,128,256]{4,2,0,1,3:T(2,128)(2,1)}), bf16[4,1,2,128,256]{4,2,0,1,3:T(2,128)(2,1)}, u32[]{:S(2)}, u32[]{:S(2)}) async-start(bf16[4,1,2,128,256]{4,2,0,1,3:T(2,128)(2,1)} %bitcast.282), calls=%async_computation.1 | async-start | bytes 1048576 | tf_op jit(solution)/shard_map/all_to_all | solution.py:84
  42.7 1.5 %pad_maximum_fusion = (bf16[2,4,3,128,256]{3,4,2,1,0:T(8,128)(2,1)S(1)}, bf16[2,4,3,128,256]{3,4,2,1,0:T(8,128)(2,1)S(1)}) fusion(bf16[2,4,1,128,256]{3,4,2,1,0:T(8,128)(2,1)} %collective-permute-done.3, bf16[2,1,2,128,256]{3,4,2,1,0:T(8,128)(2,1)S(1)} %collective-permute-done.1, bf16[2,2,2,128,256]{3,4,2,1,0:T(8,128)(2,1)S(1)} %multiply_convert_fusion, ...), kind=kLoop, calls=%fused_computation.7 | loop fusion | flops 4718592 | bytes 5242880 | tf_op jit(solution)/shard_map/concatenate | solution.py:20
  45.1 0.9 fusion.48
  46.9 0.9 fusion.45
  47.8 1.0 bitcast_dynamic-update-slice_fusion
  48.8 0.9 fusion.44
  51.5 5.6 %all-to-all-done.1 = bf16[4,1,2,128,256]{4,2,0,1,3:T(2,128)(2,1)} async-done(((bf16[4,1,2,128,256]{4,2,0,1,3:T(2,128)(2,1)}), bf16[4,1,2,128,256]{4,2,0,1,3:T(2,128)(2,1)}, u32[]{:S(2)}, u32[]{:S(2)}) %all-to-all-start.1) | async-done | bytes 524320 | tf_op jit(solution)/shard_map/all_to_all | solution.py:84
  57.1 1.1 %copy.50 = bf16[4,1,2,128,256]{4,3,2,0,1:T(8,128)(2,1)S(1)} copy(bf16[4,1,2,128,256]{4,2,0,1,3:T(2,128)(2,1)} %all-to-all-done.1) | data formatting | bytes 1048576 | tf_op jit(solution)/shard_map/all_to_all | solution.py:84
  61.7 1.0 fusion.28
  63.5 1.2 %add_convert_fusion = bf16[4,8,2,16,256]{4,3,1,2,0:T(8,128)(2,1)} fusion(bf16[4,8,2,16,256]{4,3,1,2,0:T(8,128)(2,1)S(1)} %fusion.35, bf16[4,8,2,16,256]{4,3,1,2,0:T(8,128)(2,1)S(1)} %get-tuple-element.98, bf16[4,8,2,16,256]{4,3,1,2,0:T(8,128)(2,1)S(1)} %get-tuple-element.100, bf16[4,8,2,16,256]{4,3,1,2,0:T(8,128)(2,1)S(1)} %get-tuple-element.99, ...), kind=kLoop, calls=%fused_computation.54 | loop fusion | flops 2621440 | bytes 3145728 | tf_op jit(solution)/shard_map/convert_element_type | solution.py:60
  64.7 3.5 %all-to-all-start.2 = ((bf16[4,8,2,16,256]{4,3,1,2,0:T(8,128)(2,1)}), bf16[4,8,2,16,256]{4,3,1,2,0:T(8,128)(2,1)S(1)}, u32[]{:S(2)}, u32[]{:S(2)}) async-start(bf16[4,8,2,16,256]{4,3,1,2,0:T(8,128)(2,1)} %add_convert_fusion), calls=%async_computation.2 | async-start | bytes 1048576 | tf_op jit(solution)/shard_map/all_to_all | solution.py:94
  68.2 0.9 fusion.40
  69.1 2.7 %fusion.7 = f32[2,2,256,128]{3,2,1,0:T(8,128)S(1)} fusion(bf16[2,2,2,9,128,256]{4,5,3,2,1,0:T(8,128)(2,1)} %fusion.40, bf16[2,2,2,9,128,128]{5,4,3,2,1,0:T(8,128)(2,1)} %param.8), kind=kOutput, calls=%fused_computation.12 | convolution fusion | flops 301989888 | bytes 4063232 | tf_op jit(solution)/shard_map/uvkmn,uvknr->uvmr/dot_general | solution.py:35
  71.9 5.1 %all-to-all-done.2 = bf16[4,8,2,16,256]{4,3,1,2,0:T(8,128)(2,1)S(1)} async-done(((bf16[4,8,2,16,256]{4,3,1,2,0:T(8,128)(2,1)}), bf16[4,8,2,16,256]{4,3,1,2,0:T(8,128)(2,1)S(1)}, u32[]{:S(2)}, u32[]{:S(2)}) %all-to-all-start.2) | async-done | bytes 524320 | tf_op jit(solution)/shard_map/all_to_all | solution.py:94
  77.9 3.7 %all-to-all-start.3 = ((bf16[1,8,2,64,256]{4,3,2,0,1:T(8,128)(2,1)}), bf16[1,8,2,64,256]{4,3,2,0,1:T(8,128)(2,1)S(1)}, u32[]{:S(2)}, u32[]{:S(2)}) async-start(bf16[1,8,2,64,256]{4,3,2,0,1:T(8,128)(2,1)} %bitcast.92), calls=%async_computation.3 | async-start | bytes 1048576 | tf_op jit(solution)/shard_map/all_to_all | solution.py:93
  81.6 2.9 %fusion.4 = f32[2,2,256,128]{3,2,1,0:T(8,128)S(1)} fusion(bf16[2,2,2,9,128,256]{4,5,3,2,1,0:T(8,128)(2,1)} %fusion.40, bf16[2,2,2,9,128,128]{5,4,3,2,1,0:T(8,128)(2,1)} %param.8), kind=kOutput, calls=%fused_computation.9 | convolution fusion | flops 301989888 | bytes 4063232 | tf_op jit(solution)/shard_map/uvkmn,uvknr->uvmr/dot_general | solution.py:32
  84.5 2.5 %fusion.13 = f32[1,2,2,128,256]{3,4,2,1,0:T(8,128)S(1)} fusion(f32[2,2,256,128]{3,2,1,0:T(8,128)S(1)} %fusion.7, bf16[2,2,2,9,128,256]{4,5,3,2,1,0:T(8,128)(2,1)} %fusion.40, bf16[2,2,2,9,128,128]{5,4,3,2,1,0:T(8,128)(2,1)S(1)} %copy-done.3), kind=kOutput, calls=%fused_computation.24 | convolution fusion | flops 302120960 | bytes 4587520 | tf_op jit(solution)/shard_map/uvkmn,uvknr->uvmr/dot_general | solution.py:35
  86.9 2.5 %fusion.11 = f32[1,2,2,128,256]{3,4,2,1,0:T(8,128)S(1)} fusion(f32[2,2,256,128]{3,2,1,0:T(8,128)S(1)} %fusion.4, bf16[2,2,2,9,128,256]{4,5,3,2,1,0:T(8,128)(2,1)} %fusion.40, bf16[2,2,2,9,128,128]{5,4,3,2,1,0:T(8,128)(2,1)S(1)} %copy-done.3), kind=kOutput, calls=%fused_computation.22 | convolution fusion | flops 302120960 | bytes 4587520 | tf_op jit(solution)/shard_map/uvkmn,uvknr->uvmr/dot_general | solution.py:32
  89.5 6.4 %all-to-all-done.3 = bf16[1,8,2,64,256]{4,3,2,0,1:T(8,128)(2,1)S(1)} async-done(((bf16[1,8,2,64,256]{4,3,2,0,1:T(8,128)(2,1)}), bf16[1,8,2,64,256]{4,3,2,0,1:T(8,128)(2,1)S(1)}, u32[]{:S(2)}, u32[]{:S(2)}) %all-to-all-start.3) | async-done | bytes 524320 | tf_op jit(solution)/shard_map/all_to_all | solution.py:93
  97.6 1.3 %copy.58 = f32[2,2,2,128,256]{4,3,2,1,0:T(8,128)} copy(f32[2,2,2,128,256]{3,4,2,1,0:T(8,128)S(1)} %fusion.24) | data formatting | bytes 2097152 | tf_op jit(solution)/shard_map/mul | solution.py:101
  (44 shorter events, 12.8 us)
Async XLA Ops:
  0.0 6.7 %copy-start = (bf16[2,2,2,512,128]{4,3,2,1,0:T(8,128)(2,1)S(1)}, bf16[2,2,2,512,128]{4,3,2,1,0:T(8,128)(2,1)}, u32[]{:S(2)}) copy-start(bf16[2,2,2,512,128]{4,3,2,1,0:T(8,128)(2,1)} %param.9) | copy-start | bytes 3145732
  2.3 5.4 %collective-permute-start.1 = (bf16[2,1,2,128,256]{3,4,2,1,0:T(8,128)(2,1)S(1)}, bf16[2,1,2,128,256]{3,4,2,1,0:T(8,128)(2,1)S(1)}, u32[]{:S(2)}, u32[]{:S(2)}) collective-permute-start(bf16[2,1,2,128,256]{3,4,2,1,0:T(8,128)(2,1)S(1)} %get-tuple-element.64), channel_id=1, source_target_pairs={{8,0},{16,8},{24,16},{9,1},{17,9},{25,17},{10,2},{18,10},{26,18},{... | collective-permute-start | bytes 786440 | tf_op jit(solution)/shard_map/ppermute | solution.py:24
  3.6 4.2 %collective-permute-start = (bf16[2,1,2,128,256]{3,4,2,1,0:T(8,128)(2,1)S(1)}, bf16[2,1,2,128,256]{3,4,2,1,0:T(8,128)(2,1)S(1)}, u32[]{:S(2)}, u32[]{:S(2)}) collective-permute-start(bf16[2,1,2,128,256]{3,4,2,1,0:T(8,128)(2,1)S(1)} %get-tuple-element.63), channel_id=1, source_target_pairs={{0,8},{8,16},{16,24},{1,9},{9,17},{17,25},{2,10},{10,18},{18,26},{... | collective-permute-start | bytes 786440 | tf_op jit(solution)/shard_map/ppermute | solution.py:22
  9.0 33.7 %collective-permute-start.3 = (bf16[2,4,1,128,256]{3,4,2,1,0:T(8,128)(2,1)}, bf16[2,4,1,128,256]{3,4,2,1,0:T(8,128)(2,1)}, u32[]{:S(2)}, u32[]{:S(2)}) collective-permute-start(bf16[2,4,1,128,256]{3,4,2,1,0:T(8,128)(2,1)} %get-tuple-element.59), channel_id=1, source_target_pairs={{1,0},{2,1},{3,2},{4,3},{5,4},{6,5},{7,6},{9,8},{10,9},{11,10},{12... | collective-permute-start | bytes 1572872 | tf_op jit(solution)/shard_map/ppermute | solution.py:24
  10.3 32.4 %collective-permute-start.2 = (bf16[2,4,1,128,256]{3,4,2,1,0:T(8,128)(2,1)}, bf16[2,4,1,128,256]{3,4,2,1,0:T(8,128)(2,1)}, u32[]{:S(2)}, u32[]{:S(2)}) collective-permute-start(bf16[2,4,1,128,256]{3,4,2,1,0:T(8,128)(2,1)} %get-tuple-element.60), channel_id=1, source_target_pairs={{0,1},{1,2},{2,3},{3,4},{4,5},{5,6},{6,7},{8,9},{9,10},{10,11},{11... | collective-permute-start | bytes 1572872 | tf_op jit(solution)/shard_map/ppermute | solution.py:22
  17.8 10.0 %copy-start.2 = (f32[16,2,64]{2,1,0:T(2,128)S(1)}, f32[16,2,64]{2,1,0:T(2,128)}, u32[]{:S(2)}) copy-start(f32[16,2,64]{2,1,0:T(2,128)} %param.11) | copy-start | bytes 24580
  20.3 16.3 %all-to-all-start = ((bf16[1,1,2,512,256]{4,2,1,0,3:T(2,128)(2,1)}), bf16[1,1,2,512,256]{4,2,1,0,3:T(2,128)(2,1)S(1)}, u32[]{:S(2)}, u32[]{:S(2)}) async-start(bf16[1,1,2,512,256]{4,2,1,0,3:T(2,128)(2,1)} %copy.48), calls=%async_computation | async-start | bytes 1048576 | tf_op jit(solution)/shard_map/all_to_all | solution.py:85
  37.8 19.3 %all-to-all-start.1 = ((bf16[4,1,2,128,256]{4,2,0,1,3:T(2,128)(2,1)}), bf16[4,1,2,128,256]{4,2,0,1,3:T(2,128)(2,1)}, u32[]{:S(2)}, u32[]{:S(2)}) async-start(bf16[4,1,2,128,256]{4,2,0,1,3:T(2,128)(2,1)} %bitcast.282), calls=%async_computation.1 | async-start | bytes 1048576 | tf_op jit(solution)/shard_map/all_to_all | solution.py:84
  64.7 12.3 %all-to-all-start.2 = ((bf16[4,8,2,16,256]{4,3,1,2,0:T(8,128)(2,1)}), bf16[4,8,2,16,256]{4,3,1,2,0:T(8,128)(2,1)S(1)}, u32[]{:S(2)}, u32[]{:S(2)}) async-start(bf16[4,8,2,16,256]{4,3,1,2,0:T(8,128)(2,1)} %add_convert_fusion), calls=%async_computation.2 | async-start | bytes 1048576 | tf_op jit(solution)/shard_map/all_to_all | solution.py:94
  77.9 18.0 %all-to-all-start.3 = ((bf16[1,8,2,64,256]{4,3,2,0,1:T(8,128)(2,1)}), bf16[1,8,2,64,256]{4,3,2,0,1:T(8,128)(2,1)S(1)}, u32[]{:S(2)}, u32[]{:S(2)}) async-start(bf16[1,8,2,64,256]{4,3,2,0,1:T(8,128)(2,1)} %bitcast.92), calls=%async_computation.3 | async-start | bytes 1048576 | tf_op jit(solution)/shard_map/all_to_all | solution.py:93
  81.5 2.9 %copy-start.3 = (bf16[2,2,2,9,128,128]{5,4,3,2,1,0:T(8,128)(2,1)S(1)}, bf16[2,2,2,9,128,128]{5,4,3,2,1,0:T(8,128)(2,1)}, u32[]{:S(2)}) copy-start(bf16[2,2,2,9,128,128]{5,4,3,2,1,0:T(8,128)(2,1)} %param.8) | copy-start | bytes 7077892
  86.9 9.0 %copy-start.1 = (bf16[2,2,2,128,512]{4,3,2,1,0:T(8,128)(2,1)S(1)}, bf16[2,2,2,128,512]{4,3,2,1,0:T(8,128)(2,1)}, u32[]{:S(2)}) copy-start(bf16[2,2,2,128,512]{4,3,2,1,0:T(8,128)(2,1)} %param.10) | copy-start | bytes 3145732
where the time goes:
time: 99.5 us; the launch traced here: 98.9 us
  starting transfers between devices  31.4 us (32%)
  waiting for transfers between devices  25.9 us (26%)
  local copies, waits for them, and re-layouts  15.3 us (15%)
  matrix products  14.1 us (14%)
  other arithmetic  11.9 us (12%)
    ppermute x2, starting transfers between devices, with_halo(): lax.ppermute(tail, axis, [(i, (i + 1) % count) for i in range(ends)])  9.32 us
    all_to_all x1, waiting for transfers between devices, shards(): lax.all_to_all(reordered, 'sect', split_axis=3, concat_axis=0, tiled=True)  8.73 us
    all_to_all x1, starting transfers between devices, shards(): lax.all_to_all(reordered, 'sect', split_axis=3, concat_axis=0, tiled=True)  7.45 us
    all_to_all x1, waiting for transfers between devices, shards(): lax.all_to_all(lax.all_to_all(incoming_all, 'sect', split_axis=0, concat_...  6.36 us
    unnamed x14, local copies, waits for them, and re-layouts  5.94 us
    all_to_all x1, waiting for transfers between devices, shards(): lax.all_to_all(lax.all_to_all(reordered, 'sect', split_axis=3, concat_axi...  5.58 us
    all_to_all x1, waiting for transfers between devices, shards(): lax.all_to_all(incoming_all, 'sect', split_axis=0, concat_axis=3, tiled=T...  5.11 us
    all_to_all x1, starting transfers between devices, shards(): lax.all_to_all(lax.all_to_all(reordered, 'sect', split_axis=3, concat_axi...  4.91 us
  transfers between devices with their start and end apart: 8, of which 5 were waited for; matrix products, arithmetic and copies ran while one was open for 27% of the time, Pallas kernels for 0%

commit v1 on v0

v1 whole, which is shorter than its diff:
```python
import functools

import jax
import jax.numpy as jnp
from jax import lax
from jax.experimental import pallas as pl
from jax.experimental.pallas import tpu as pltpu
from jax.sharding import PartitionSpec as P

REACH = 2
PAIR = 2
MIB = 1 << 20
far_offsets = [
    (row_step, col_step)
    for row_step in range(-REACH, REACH + 1)
    for col_step in range(-REACH, REACH + 1)
    if max(abs(row_step), abs(col_step)) == REACH
]
VMEM = pl.BlockSpec(memory_space=pltpu.VMEM)
SMEM = pl.BlockSpec(memory_space=pltpu.SMEM)


def params(mib):
    return pltpu.CompilerParams(vmem_limit_bytes=mib * MIB)


def swap_pairs(count, first):
    pairs = []
    for i in range(count):
        partner = i + 1 if (i - first) % 2 == 0 else i - 1
        pairs.append((i, partner if 0 <= partner < count else i))
    return pairs


def column_kernel(live_ref, unknowns_ref, near_ref, cross_ref):
    odd = lax.rem(lax.axis_index("dir"), 2)
    for u in range(unknowns_ref.shape[1]):
        for out_ref, v in ((near_ref, 1 - odd), (cross_ref, odd)):
            keep = live_ref[u, v].astype(jnp.float32).astype(jnp.bfloat16)
            out_ref[:, u] = unknowns_ref[:, u, v] * keep


def complex_dot(left_real, left_imag, right):
    rows = left_real.shape[0]
    cols = right.shape[1] // 2
    both = jnp.dot(
        jnp.concatenate([left_real, left_imag], axis=0), right, preferred_element_type=jnp.float32
    )
    real = both[:rows, :cols] - both[rows:, cols:]
    imag = both[:rows, cols:] + both[rows:, :cols]
    return real, imag


def pattern_kernel(live_ref, unknowns_ref, aggregate_ref, out_ref, leaves_ref):
    parts, _, narrow, sides = out_ref.shape
    size = unknowns_ref.shape[3]
    width = unknowns_ref.shape[2]

    @pl.when(pl.program_id(0) == 0)
    def _():
        for u in range(unknowns_ref.shape[1]):
            for v in range(width):
                keep = live_ref[u, v].astype(jnp.float32).astype(jnp.bfloat16)
                at = (u * width + v) * size
                for c in range(2):
                    leaves_ref[at : at + size, c * sides : (c + 1) * sides] = (
                        unknowns_ref[c, u, v] * keep
                    )

    left = [
        jnp.concatenate(
            [
                aggregate_ref[c, u, v]
                for u in range(unknowns_ref.shape[1])
                for v in range(width)
            ],
            axis=1,
        )
        for c in range(2)
    ]
    real, imag = complex_dot(left[0], left[1], leaves_ref[...])
    for part in range(parts):
        out_ref[part, 0] = real[part * narrow : (part + 1) * narrow].astype(jnp.bfloat16)
        out_ref[part, 1] = imag[part * narrow : (part + 1) * narrow].astype(jnp.bfloat16)


def translate_kernel(groups, own_ref, even_ref, odd_ref, coef_ref, out_ref, beside_ref, wide_ref):
    box_rows = own_ref.shape[0] // PAIR
    depth, sides = own_ref.shape[2], own_ref.shape[3]
    lanes = min(128, sides)
    group = lax.axis_index("dir") // PAIR
    parity = lax.rem(group, 2)
    for ref, slot, missing in (
        (even_ref, 1 - parity, (parity == 0) & (group == groups - 1)),
        (odd_ref, parity, (group == 0) | ((parity == 1) & (group == groups - 1))),
    ):

        @pl.when(missing)
        def _():
            beside_ref[slot] = jnp.zeros_like(ref)

        @pl.when(jnp.logical_not(missing))
        def _():
            beside_ref[slot] = ref[...]

    coefs = coef_ref[...]
    for index in range(coefs.shape[1]):
        wide_ref[index] = jnp.broadcast_to(coefs[:, index : index + 1], (depth, lanes))

    for lane in range(0, sides, lanes):
        span = slice(lane, lane + lanes)
        totals = {}
        for source in range(box_rows):
            held = []
            for col in range(-REACH, PAIR + REACH):
                at = source * PAIR + col % PAIR
                if col < 0:
                    held.append([beside_ref[0, at, c, :, span].astype(jnp.float32) for c in range(2)])
                elif col >= PAIR:
                    held.append([beside_ref[1, at, c, :, span].astype(jnp.float32) for c in range(2)])
                else:
                    held.append([own_ref[at, c, :, span].astype(jnp.float32) for c in range(2)])
            for target in range(max(0, source - REACH), min(box_rows, source + REACH + 1)):
                for col in range(PAIR):
                    real = imag = None
                    for index, (row_step, col_step) in enumerate(far_offsets):
                        if row_step != source - target:
                            continue
                        coef_real, coef_imag = wide_ref[2 * index], wide_ref[2 * index + 1]
                        from_real, from_imag = held[col + col_step + REACH]
                        term_real = coef_real * from_real - coef_imag * from_imag
                        term_imag = coef_real * from_imag + coef_imag * from_real
                        real = term_real if real is None else real + term_real
                        imag = term_imag if imag is None else imag + term_imag
                    real = real.astype(jnp.bfloat16).astype(jnp.float32)
                    imag = imag.astype(jnp.bfloat16).astype(jnp.float32)
                    if (target, col) in totals:
                        old = totals[target, col]
                        totals[target, col] = (old[0] + real, old[1] + imag)
                    else:
                        totals[target, col] = (real, imag)
        for (target, col), (real, imag) in totals.items():
            out_ref[target * PAIR + col, 0, :, span] = real.astype(jnp.bfloat16)
            out_ref[target * PAIR + col, 1, :, span] = imag.astype(jnp.bfloat16)


def row_kernel(near_ref, cross_ref, from_near_ref, from_cross_ref, out_near_ref, out_cross_ref):
    odd = lax.rem(lax.axis_index("sect"), 2)
    for slot, ref in enumerate((near_ref, cross_ref, from_near_ref, from_cross_ref)):
        out_near_ref[:, slot] = ref[:, 1 - odd]
        out_cross_ref[:, slot] = ref[:, odd]


def near_kernel(
    near_ref, cross_ref, from_near_ref, from_cross_ref, row_near_ref, row_cross_ref, blocks_ref,
    out_ref, grid_ref,
):
    size, sides = near_ref.shape[2], near_ref.shape[3]
    deep = near_ref.shape[1]
    wide = 2
    leaf = pl.program_id(0)

    @pl.when(leaf == 0)
    def _():
        col_at, col_count = lax.axis_index("dir"), lax.axis_size("dir")
        row_at, row_count = lax.axis_index("sect"), lax.axis_size("sect")
        col_odd, row_odd = lax.rem(col_at, 2), lax.rem(row_at, 2)
        columns = (2 - col_odd, 1 + col_odd, 3 - 3 * col_odd, 3 * col_odd)
        no_col = ((col_odd == 0) & (col_at == 0)) | ((col_odd == 1) & (col_at == col_count - 1))
        no_row = ((row_odd == 0) & (row_at == 0)) | ((row_odd == 1) & (row_at == row_count - 1))
        for slot, ref in enumerate((near_ref, cross_ref, from_near_ref, from_cross_ref)):
            for u in range(deep):
                for c in range(2):
                    grid_ref[1 + u, columns[slot], :, c * sides : (c + 1) * sides] = ref[c, u]
            for c in range(2):
                half = slice(c * sides, (c + 1) * sides)
                grid_ref[3 - 3 * row_odd, columns[slot], :, half] = row_near_ref[c, slot]
                grid_ref[3 * row_odd, columns[slot], :, half] = row_cross_ref[c, slot]

        @pl.when(no_col)
        def _():
            for i in range(deep + 2):
                grid_ref[i, columns[3]] = jnp.zeros(grid_ref.shape[2:], grid_ref.dtype)

        @pl.when(no_row)
        def _():
            for j in range(wide + 2):
                grid_ref[3 * row_odd, j] = jnp.zeros(grid_ref.shape[2:], grid_ref.dtype)

    u, v = leaf // wide, lax.rem(leaf, wide)
    right = jnp.concatenate(
        [grid_ref[u + a, v + b] for a in range(3) for b in range(3)], axis=0
    )
    left = [jnp.concatenate([blocks_ref[c, 0, 0, k] for k in range(9)], axis=1) for c in range(2)]
    real, imag = complex_dot(left[0], left[1], right)
    out_ref[0, 0, 0] = real
    out_ref[1, 0, 0] = imag


def far_kernel(live_ref, incoming_ref, disaggregate_ref, near_ref, out_ref, right_ref):
    parts, _, narrow, sides = incoming_ref.shape
    leaf = pl.program_id(0)
    wide = live_ref.shape[1]

    @pl.when(leaf == 0)
    def _():
        for part in range(parts):
            for c in range(2):
                right_ref[part * narrow : (part + 1) * narrow, c * sides : (c + 1) * sides] = (
                    incoming_ref[part, c]
                )

    live = live_ref[leaf // wide, lax.rem(leaf, wide)].astype(jnp.float32)
    real, imag = complex_dot(
        disaggregate_ref[0, 0, 0], disaggregate_ref[1, 0, 0], right_ref[...]
    )
    out_ref[0, 0, 0] = (near_ref[0, 0, 0] + real) * live
    out_ref[1, 0, 0] = (near_ref[1, 0, 0] + imag) * live


def direction_coefs(translate, narrow):
    sect_count, dir_count = lax.axis_size("sect"), lax.axis_size("dir")
    groups = dir_count // PAIR
    held = translate.shape[2]
    pieces = narrow // held
    got = []
    for turn in range(pieces):
        sends = []
        for sect in range(sect_count):
            for col in range(dir_count):
                group, block = col // PAIR, sect * PAIR + col % PAIR
                shard = block * pieces + (turn + group // sect_count) % pieces
                sends.append(((group % sect_count) * dir_count + shard, sect * dir_count + col))
        got.append(lax.ppermute(translate, ("sect", "dir"), sends))
    if pieces == 1:
        return got[0]
    first = lax.axis_index("dir") // PAIR // sect_count
    return jnp.concatenate(
        [
            lax.dynamic_index_in_dim(
                jnp.stack(got), lax.rem(piece - first + pieces, pieces), 0, keepdims=False
            )
            for piece in range(pieces)
        ],
        axis=2,
    )


def shards(unknowns, leaf_live, near_blocks, aggregate, disaggregate, translate):
    sect_count, dir_count = lax.axis_size("sect"), lax.axis_size("dir")
    _, deep, wide, size, sides = unknowns.shape
    total_dirs = aggregate.shape[3]
    groups = dir_count // PAIR
    parts = sect_count * PAIR
    narrow = total_dirs // parts
    bf16, f32 = jnp.bfloat16, jnp.float32
    members = [
        [sect * dir_count + group * PAIR + col for sect in range(sect_count) for col in range(PAIR)]
        for group in range(groups)
    ]

    def spread(array):
        return lax.all_to_all(
            array, ("sect", "dir"), split_axis=0, concat_axis=0, tiled=True, axis_index_groups=members
        )

    def swap(array, axis, first, width=1):
        count = lax.axis_size(axis) // width
        return lax.ppermute(
            array,
            axis,
            [(i * width + j, k * width + j) for i, k in swap_pairs(count, first) for j in range(width)],
        )

    column = jax.ShapeDtypeStruct((2, deep, size, sides), bf16)
    col_near, col_cross = pl.pallas_call(
        column_kernel,
        in_specs=[SMEM, VMEM],
        out_specs=[VMEM, VMEM],
        out_shape=[column, column],
        compiler_params=params(8),
        name="columns",
    )(leaf_live, unknowns)
    from_cross = swap(col_cross, "dir", 1)

    steps = 2
    patterns = pl.pallas_call(
        pattern_kernel,
        grid=(steps,),
        in_specs=[
            SMEM,
            pl.BlockSpec(unknowns.shape, lambda i: (0, 0, 0, 0, 0)),
            pl.BlockSpec((2, deep, wide, total_dirs // steps, size), lambda i: (0, 0, 0, i, 0)),
        ],
        out_specs=pl.BlockSpec((parts // steps, 2, narrow, sides), lambda i: (i, 0, 0, 0)),
        out_shape=jax.ShapeDtypeStruct((parts, 2, narrow, sides), bf16),
        scratch_shapes=[pltpu.VMEM((deep * wide * size, 2 * sides), bf16)],
        compiler_params=params(16),
        name="patterns",
    )(leaf_live, unknowns, aggregate)
    own = spread(patterns)
    coefs = direction_coefs(translate, narrow).reshape(2 * len(far_offsets), narrow).T
    from_near = swap(col_near, "dir", 0)
    even = swap(own, "dir", 0, PAIR)
    odd = swap(own, "dir", 1, PAIR)

    row = jax.ShapeDtypeStruct((2, 4, size, sides), bf16)
    row_near, row_cross = pl.pallas_call(
        row_kernel,
        in_specs=[VMEM] * 4,
        out_specs=[VMEM] * 2,
        out_shape=[row, row],
        compiler_params=params(8),
        name="rows",
    )(col_near, col_cross, from_near, from_cross)
    row_near = swap(row_near, "sect", 0)
    row_cross = swap(row_cross, "sect", 1)

    depth = 16
    block = pl.BlockSpec((parts, 2, depth, sides), lambda i: (0, 0, i, 0))
    incoming = pl.pallas_call(
        functools.partial(translate_kernel, groups),
        grid=(narrow // depth,),
        in_specs=[block, block, block, pl.BlockSpec((depth, coefs.shape[1]), lambda i: (i, 0))],
        out_specs=block,
        out_shape=jax.ShapeDtypeStruct(own.shape, bf16),
        scratch_shapes=[
            pltpu.VMEM((2, parts, 2, depth, sides), bf16),
            pltpu.VMEM((coefs.shape[1], depth, min(128, sides)), f32),
        ],
        compiler_params=params(16),
        name="translations",
    )(own, even, odd, coefs)
    returned = spread(incoming)

    leaf_out = pl.BlockSpec((2, 1, 1, size, sides), lambda i: (0, i // wide, i % wide, 0, 0))
    field = jax.ShapeDtypeStruct(unknowns.shape, f32)
    near = pl.pallas_call(
        near_kernel,
        grid=(deep * wide,),
        in_specs=[VMEM] * 6
        + [pl.BlockSpec((2, 1, 1, 9, size, size), lambda i: (0, i // wide, i % wide, 0, 0, 0))],
        out_specs=leaf_out,
        out_shape=field,
        scratch_shapes=[pltpu.VMEM((deep + 2, wide + 2, size, 2 * sides), bf16)],
        compiler_params=params(24),
        name="near",
    )(col_near, col_cross, from_near, from_cross, row_near, row_cross, near_blocks)
    return pl.pallas_call(
        far_kernel,
        grid=(deep * wide,),
        in_specs=[
            SMEM,
            VMEM,
            pl.BlockSpec((2, 1, 1, size, total_dirs), lambda i: (0, i // wide, i % wide, 0, 0)),
            leaf_out,
        ],
        out_specs=leaf_out,
        out_shape=field,
        scratch_shapes=[pltpu.VMEM((total_dirs, 2 * sides), bf16)],
        compiler_params=params(16),
        name="far",
    )(leaf_live, returned, disaggregate, near)


def solution(mesh):
    in_specs = (
        P(None, "sect", "dir", None, None),
        P("sect", "dir"),
        P(None, "sect", "dir", None, None, None),
        P(None, "sect", "dir", None, None),
        P(None, "sect", "dir", None, None),
        P(None, None, "dir"),
    )
    out_specs = P(None, "sect", "dir", None, None)
    return jax.shard_map(shards, mesh=mesh, in_specs=in_specs, out_specs=out_specs, check_vma=False)
```

time: 99.5 us -> 78.4 us (0.79)
  the two profiles are of different devices: /device:TPU:0 before, /device:TPU:16 now
where the time goes in v1:
time: 78.4 us; the launch traced here: 77.5 us
  starting transfers between devices  20.5 us (26%)
  waiting for transfers between devices  20.3 us (26%)
  Pallas kernels  15 us (19%)
  blocking collectives  12.8 us (16%)
  local copies, waits for them, and re-layouts  8.76 us (11%)
    ppermute x6, starting transfers between devices, swap(): lax.ppermute(array, axis, [(i * width + j, k * width + j) for i, k in swa...  14.3 us
    ppermute x6, waiting for transfers between devices, swap(): lax.ppermute(array, axis, [(i * width + j, k * width + j) for i, k in swa...  13.2 us
    all_to_all x1, blocking collectives, spread(): lax.all_to_all(array, ('sect', 'dir'), split_axis=0, concat_axis=0, tiled...  12.8 us
    unnamed x30, local copies, waits for them, and re-layouts  8.68 us
    ppermute x1, waiting for transfers between devices, direction_coefs(): got.append(lax.ppermute(translate, ('sect', 'dir'), sends))  5.5 us
    pallas_call x1, Pallas kernels, shards(): pl.pallas_call(functools.partial(translate_kernel, groups), grid=(narrow...  4.42 us
    all_to_all x1, starting transfers between devices, spread(): lax.all_to_all(array, ('sect', 'dir'), split_axis=0, concat_axis=0, tiled...  4.28 us
    pallas_call x1, Pallas kernels, shards(): pl.pallas_call(near_kernel, grid=(deep * wide,), in_specs=[VMEM] * 6 + [p...  3.76 us
  transfers between devices with their start and end apart: 8, of which 4 were waited for; matrix products, arithmetic and copies ran while one was open for 0% of the time, Pallas kernels for 13%

profile of v1, /device:TPU:16, one launch (start us, length us, event | category | flops | bytes accessed | tf_op | source)
XLA Modules:
  0.0 77.5 jit_solution(12372947727757124375)
XLA Ops:
  0.0 1.0 %copy-done.1 = bf16[2,2,2,128,256]{4,3,2,1,0:T(8,128)(2,1)S(1)} copy-done((bf16[2,2,2,128,256]{4,3,2,1,0:T(8,128)(2,1)S(1)}, bf16[2,2,2,128,256]{4,3,2,1,0:T(8,128)(2,1)}, u32[]{:S(2)}) %copy-start.1) | copy-done | bytes 524312
  1.0 1.2 %copy-done.2 = bf16[2,2,2,512,128]{4,3,2,1,0:T(8,128)(2,1)S(1)} copy-done((bf16[2,2,2,512,128]{4,3,2,1,0:T(8,128)(2,1)S(1)}, bf16[2,2,2,512,128]{4,3,2,1,0:T(8,128)(2,1)}, u32[]{:S(2)}) %copy-start.2) | copy-done | bytes 1048600
  2.3 0.7 copy-done.12
  2.9 1.6 %patterns.1 = bf16[8,2,64,256]{3,2,1,0:T(8,128)(2,1)S(1)} custom-call(s32[2,2]{1,0:T(2,128)S(1)} %copy-done.12, bf16[2,2,2,128,256]{4,3,2,1,0:T(8,128)(2,1)S(1)} %copy-done.1, bf16[2,2,2,512,128]{4,3,2,1,0:T(8,128)(2,1)S(1)} %copy-done.2), custom_call_target="tpu_custom_call" | custom-call | tf_op jit(solution)/shard_map/patterns/pallas_call | solution.py:287
  4.5 12.8 %all_to_all.10.own_ref = bf16[8,2,64,256]{3,2,1,0:T(8,128)(2,1)S(1)} all-to-all(bf16[8,2,64,256]{3,2,1,0:T(8,128)(2,1)S(1)} %patterns.1), channel_id=1, replica_groups={{0,1,8,9,16,17,24,25},{2,3,10,11,18,19,26,27},{4,5,12,13,20,21,28,29},{..., dimensions={0} | all-to-all | bytes 1048576 | tf_op jit(solution)/shard_map/all_to_all | solution.py:263
  17.3 1.6 %collective-permute-start = (bf16[8,2,64,256]{3,2,1,0:T(8,128)(2,1)S(1)}, bf16[8,2,64,256]{3,2,1,0:T(8,128)(2,1)}, u32[]{:S(2)}, u32[]{:S(2)}) collective-permute-start(bf16[8,2,64,256]{3,2,1,0:T(8,128)(2,1)S(1)} %all_to_all.10.own_ref), channel_id=1, source_target_pairs={{0,2},{1,3},{2,0},{3,1},{4,6},{5,7},{6,4},{7,5},{8,10},{9,11},{10,... | collective-permute-start | bytes 1572872 | tf_op jit(solution)/shard_map/ppermute | solution.py:269
  18.9 1.9 %collective-permute-start.1 = (bf16[8,2,64,256]{3,2,1,0:T(8,128)(2,1)S(1)}, bf16[8,2,64,256]{3,2,1,0:T(8,128)(2,1)}, u32[]{:S(2)}, u32[]{:S(2)}) collective-permute-start(bf16[8,2,64,256]{3,2,1,0:T(8,128)(2,1)S(1)} %all_to_all.10.own_ref), channel_id=1, source_target_pairs={{0,0},{1,1},{2,4},{3,5},{4,2},{5,3},{6,6},{7,7},{8,8},{9,9},{10,12... | collective-permute-start | bytes 1572872 | tf_op jit(solution)/shard_map/ppermute | solution.py:269
  20.8 0.6 columns.1
  21.4 1.1 %collective-permute-start.3 = (bf16[2,2,128,256]{3,2,1,0:T(8,128)(2,1)S(1)}, bf16[2,2,128,256]{3,2,1,0:T(8,128)(2,1)S(1)}, u32[]{:S(2)}, u32[]{:S(2)}) collective-permute-start(bf16[2,2,128,256]{3,2,1,0:T(8,128)(2,1)S(1)} %get-tuple-element.9.near_ref), channel_id=1, source_target_pairs={{0,1},{1,0},{2,3},{3,2},{4,5},{5,4},{6,7},{7,6},{8,9},{9,8},{10,11... | collective-permute-start | bytes 786440 | tf_op jit(solution)/shard_map/ppermute | solution.py:269
  22.5 4.3 %collective-permute-start.4 = (bf16[2,2,128,256]{3,2,1,0:T(8,128)(2,1)S(1)}, bf16[2,2,128,256]{3,2,1,0:T(8,128)(2,1)S(1)}, u32[]{:S(2)}, u32[]{:S(2)}) collective-permute-start(bf16[2,2,128,256]{3,2,1,0:T(8,128)(2,1)S(1)} %get-tuple-element.10.cross_ref), channel_id=1, source_target_pairs={{0,0},{1,2},{2,1},{3,4},{4,3},{5,6},{6,5},{7,7},{8,8},{9,10},{10,9... | collective-permute-start | bytes 786440 | tf_op jit(solution)/shard_map/ppermute | solution.py:269
  26.9 2.7 %collective-permute-done.3.from_near_ref = bf16[2,2,128,256]{3,2,1,0:T(8,128)(2,1)S(1)} collective-permute-done((bf16[2,2,128,256]{3,2,1,0:T(8,128)(2,1)S(1)}, bf16[2,2,128,256]{3,2,1,0:T(8,128)(2,1)S(1)}, u32[]{:S(2)}, u32[]{:S(2)}) %collective-permute-start.3) | collective-permute-done | bytes 262176 | tf_op jit(solution)/shard_map/ppermute | solution.py:269
  29.5 10.5 %collective-permute-done.4.from_cross_ref = bf16[2,2,128,256]{3,2,1,0:T(8,128)(2,1)S(1)} collective-permute-done((bf16[2,2,128,256]{3,2,1,0:T(8,128)(2,1)S(1)}, bf16[2,2,128,256]{3,2,1,0:T(8,128)(2,1)S(1)}, u32[]{:S(2)}, u32[]{:S(2)}) %collective-permute-start.4) | collective-permute-done | bytes 262176 | tf_op jit(solution)/shard_map/ppermute | solution.py:269
  40.0 1.1 %rows.1 = (bf16[2,4,128,256]{3,2,1,0:T(8,128)(2,1)}, bf16[2,4,128,256]{3,2,1,0:T(8,128)(2,1)}) custom-call(bf16[2,2,128,256]{3,2,1,0:T(8,128)(2,1)S(1)} %get-tuple-element.9.near_ref, bf16[2,2,128,256]{3,2,1,0:T(8,128)(2,1)S(1)} %get-tuple-element.10.cross_ref, bf16[2,2,128,256]{3,2,1,0:T(8,128)(2,1)S(1)} %collective-permute-done.3.from_near_ref, ...), custom_call_target="tpu_custom_call" | custom-call | tf_op jit(solution)/shard_map/rows/pallas_call | solution.py:308
  41.1 0.7 copy-done.8
  41.8 0.0 collective-permute-start.5
  41.8 5.4 %collective-permute-start.6 = (bf16[2,4,128,256]{3,2,1,0:T(8,128)(2,1)}, bf16[2,4,128,256]{3,2,1,0:T(8,128)(2,1)}, u32[]{:S(2)}, u32[]{:S(2)}) collective-permute-start(bf16[2,4,128,256]{3,2,1,0:T(8,128)(2,1)} %get-tuple-element.12), channel_id=1, source_target_pairs={{0,0},{8,16},{16,8},{24,24},{1,1},{9,17},{17,9},{25,25},{2,2},{10,... | collective-permute-start | bytes 1572872 | tf_op jit(solution)/shard_map/ppermute | solution.py:269
  47.2 1.9 %collective-permute-start.2 = (f32[16,2,64]{2,1,0:T(2,128)S(1)}, f32[16,2,64]{2,1,0:T(2,128)S(1)}, u32[]{:S(2)}, u32[]{:S(2)}) collective-permute-start(f32[16,2,64]{2,1,0:T(2,128)S(1)} %copy-done.14), channel_id=1, source_target_pairs={{0,0},{1,1},{8,2},{9,3},{16,4},{17,5},{24,6},{25,7},{2,8},{3,9},{1... | collective-permute-start | bytes 24584 | tf_op jit(solution)/shard_map/ppermute | solution.py:234
  49.1 5.5 %collective-permute-done.2 = f32[16,2,64]{2,1,0:T(2,128)S(1)} collective-permute-done((f32[16,2,64]{2,1,0:T(2,128)S(1)}, f32[16,2,64]{2,1,0:T(2,128)S(1)}, u32[]{:S(2)}, u32[]{:S(2)}) %collective-permute-start.2) | collective-permute-done | bytes 8224 | tf_op jit(solution)/shard_map/ppermute | solution.py:234
  54.6 0.1 copy.8
  54.7 0.0 collective-permute-done.even_ref
  54.7 0.0 collective-permute-done.1.odd_ref
  54.7 4.4 %translations.1 = bf16[8,2,64,256]{3,2,1,0:T(8,128)(2,1)} custom-call(bf16[8,2,64,256]{3,2,1,0:T(8,128)(2,1)S(1)} %all_to_all.10.own_ref, bf16[8,2,64,256]{3,2,1,0:T(8,128)(2,1)} %collective-permute-done.even_ref, bf16[8,2,64,256]{3,2,1,0:T(8,128)(2,1)} %collective-permute-done.1.odd_ref, f32[64,32]{1,0:T(8,128)S(1)} %bitcast.2), custom_call_target="tpu_custom_call" | custom-call | tf_op jit(solution)/shard_map/translations/pallas_call | solution.py:321
  59.1 4.3 %all-to-all-start.1 = ((bf16[8,2,64,256]{3,2,1,0:T(8,128)(2,1)}), bf16[8,2,64,256]{3,2,1,0:T(8,128)(2,1)}, u32[]{:S(2)}, u32[]{:S(2)}) async-start(bf16[8,2,64,256]{3,2,1,0:T(8,128)(2,1)} %translations.1), calls=%async_computation.1 | async-start | bytes 1048576 | tf_op jit(solution)/shard_map/all_to_all | solution.py:263
  63.4 0.0 collective-permute-done.5.row_near_ref
  63.5 0.9 %copy-done.5 = bf16[2,2,128,256]{3,2,1,0:T(8,128)(2,1)S(1)} copy-done((bf16[2,2,128,256]{3,2,1,0:T(8,128)(2,1)S(1)}, bf16[2,2,128,256]{3,2,1,0:T(8,128)(2,1)}, u32[]{:S(2)}) %copy-start.5) | copy-done | bytes 262168
  64.4 0.9 %copy-done.7 = bf16[2,2,128,256]{3,2,1,0:T(8,128)(2,1)S(1)} copy-done((bf16[2,2,128,256]{3,2,1,0:T(8,128)(2,1)S(1)}, bf16[2,2,128,256]{3,2,1,0:T(8,128)(2,1)}, u32[]{:S(2)}) %copy-start.7) | copy-done | bytes 262168
  65.4 0.9 %copy-done.9 = bf16[2,2,128,256]{3,2,1,0:T(8,128)(2,1)S(1)} copy-done((bf16[2,2,128,256]{3,2,1,0:T(8,128)(2,1)S(1)}, bf16[2,2,128,256]{3,2,1,0:T(8,128)(2,1)}, u32[]{:S(2)}) %copy-start.9) | copy-done | bytes 262168
  66.3 0.9 %copy-done.11 = bf16[2,2,128,256]{3,2,1,0:T(8,128)(2,1)S(1)} copy-done((bf16[2,2,128,256]{3,2,1,0:T(8,128)(2,1)S(1)}, bf16[2,2,128,256]{3,2,1,0:T(8,128)(2,1)}, u32[]{:S(2)}) %copy-start.11) | copy-done | bytes 262168
  67.2 3.8 %near.1.near_ref = f32[2,2,2,128,256]{4,3,2,1,0:T(8,128)S(1)} custom-call(bf16[2,2,128,256]{3,2,1,0:T(8,128)(2,1)S(1)} %copy-done.5, bf16[2,2,128,256]{3,2,1,0:T(8,128)(2,1)S(1)} %copy-done.7, bf16[2,2,128,256]{3,2,1,0:T(8,128)(2,1)S(1)} %copy-done.9, bf16[2,2,128,256]{3,2,1,0:T(8,128)(2,1)S(1)} %copy-done.11, ...), custom_call_target="tpu_custom_call" | custom-call | tf_op jit(solution)/shard_map/near/pallas_call | solution.py:338
  71.0 1.6 %all-to-all-done.1.incoming_ref = bf16[8,2,64,256]{3,2,1,0:T(8,128)(2,1)} async-done(((bf16[8,2,64,256]{3,2,1,0:T(8,128)(2,1)}), bf16[8,2,64,256]{3,2,1,0:T(8,128)(2,1)}, u32[]{:S(2)}, u32[]{:S(2)}) %all-to-all-start.1) | async-done | bytes 524320 | tf_op jit(solution)/shard_map/all_to_all | solution.py:263
  72.7 1.2 %copy-done.3 = bf16[2,2,2,128,512]{4,3,2,1,0:T(8,128)(2,1)S(1)} copy-done((bf16[2,2,2,128,512]{4,3,2,1,0:T(8,128)(2,1)S(1)}, bf16[2,2,2,128,512]{4,3,2,1,0:T(8,128)(2,1)}, u32[]{:S(2)}) %copy-start.3) | copy-done | bytes 1048600
  73.9 3.6 %far.1 = f32[2,2,2,128,256]{4,3,2,1,0:T(8,128)} custom-call(s32[2,2]{1,0:T(2,128)S(1)} %copy-done.13, bf16[8,2,64,256]{3,2,1,0:T(8,128)(2,1)} %all-to-all-done.1.incoming_ref, bf16[2,2,2,128,512]{4,3,2,1,0:T(8,128)(2,1)S(1)} %copy-done.3, f32[2,2,2,128,256]{4,3,2,1,0:T(8,128)S(1)} %near.1.near_ref), custom_call_target="tpu_custom_call" | custom-call | tf_op jit(solution)/shard_map/far/pallas_call | solution.py:349
  (22 shorter events, 0.0 us)
Async XLA Ops:
  0.0 1.0 %copy-start.1 = (bf16[2,2,2,128,256]{4,3,2,1,0:T(8,128)(2,1)S(1)}, bf16[2,2,2,128,256]{4,3,2,1,0:T(8,128)(2,1)}, u32[]{:S(2)}) copy-start(bf16[2,2,2,128,256]{4,3,2,1,0:T(8,128)(2,1)} %unknowns_ref.3) | copy-start | bytes 1572868
  1.0 1.2 %copy-start.2 = (bf16[2,2,2,512,128]{4,3,2,1,0:T(8,128)(2,1)S(1)}, bf16[2,2,2,512,128]{4,3,2,1,0:T(8,128)(2,1)}, u32[]{:S(2)}) copy-start(bf16[2,2,2,512,128]{4,3,2,1,0:T(8,128)(2,1)} %aggregate_ref.1) | copy-start | bytes 3145732
  2.3 0.7 copy-start.12
  2.9 44.2 %copy-start.14 = (f32[16,2,64]{2,1,0:T(2,128)S(1)}, f32[16,2,64]{2,1,0:T(2,128)}, u32[]{:S(2)}) copy-start(f32[16,2,64]{2,1,0:T(2,128)} %param.11) | copy-start | bytes 24580
  17.3 46.1 %copy-start = (bf16[2,2,2,9,128,128]{5,4,3,2,1,0:T(8,128)(2,1)S(1)}, bf16[2,2,2,9,128,128]{5,4,3,2,1,0:T(8,128)(2,1)}, u32[]{:S(2)}) copy-start(bf16[2,2,2,9,128,128]{5,4,3,2,1,0:T(8,128)(2,1)} %blocks_ref.1) | copy-start | bytes 7077892
  17.3 37.4 %collective-permute-start = (bf16[8,2,64,256]{3,2,1,0:T(8,128)(2,1)S(1)}, bf16[8,2,64,256]{3,2,1,0:T(8,128)(2,1)}, u32[]{:S(2)}, u32[]{:S(2)}) collective-permute-start(bf16[8,2,64,256]{3,2,1,0:T(8,128)(2,1)S(1)} %all_to_all.10.own_ref), channel_id=1, source_target_pairs={{0,2},{1,3},{2,0},{3,1},{4,6},{5,7},{6,4},{7,5},{8,10},{9,11},{10,... | collective-permute-start | bytes 1572872 | tf_op jit(solution)/shard_map/ppermute | solution.py:269
  18.9 35.8 %collective-permute-start.1 = (bf16[8,2,64,256]{3,2,1,0:T(8,128)(2,1)S(1)}, bf16[8,2,64,256]{3,2,1,0:T(8,128)(2,1)}, u32[]{:S(2)}, u32[]{:S(2)}) collective-permute-start(bf16[8,2,64,256]{3,2,1,0:T(8,128)(2,1)S(1)} %all_to_all.10.own_ref), channel_id=1, source_target_pairs={{0,0},{1,1},{2,4},{3,5},{4,2},{5,3},{6,6},{7,7},{8,8},{9,9},{10,12... | collective-permute-start | bytes 1572872 | tf_op jit(solution)/shard_map/ppermute | solution.py:269
  21.4 42.0 %copy-start.4 = (bf16[2,2,128,256]{3,2,1,0:T(8,128)(2,1)}, bf16[2,2,128,256]{3,2,1,0:T(8,128)(2,1)S(1)}, u32[]{:S(2)}) copy-start(bf16[2,2,128,256]{3,2,1,0:T(8,128)(2,1)S(1)} %get-tuple-element.9.near_ref) | copy-start | bytes 786436
  21.4 42.0 %copy-start.6 = (bf16[2,2,128,256]{3,2,1,0:T(8,128)(2,1)}, bf16[2,2,128,256]{3,2,1,0:T(8,128)(2,1)S(1)}, u32[]{:S(2)}) copy-start(bf16[2,2,128,256]{3,2,1,0:T(8,128)(2,1)S(1)} %get-tuple-element.10.cross_ref) | copy-start | bytes 786436
  21.4 8.1 %collective-permute-start.3 = (bf16[2,2,128,256]{3,2,1,0:T(8,128)(2,1)S(1)}, bf16[2,2,128,256]{3,2,1,0:T(8,128)(2,1)S(1)}, u32[]{:S(2)}, u32[]{:S(2)}) collective-permute-start(bf16[2,2,128,256]{3,2,1,0:T(8,128)(2,1)S(1)} %get-tuple-element.9.near_ref), channel_id=1, source_target_pairs={{0,1},{1,0},{2,3},{3,2},{4,5},{5,4},{6,7},{7,6},{8,9},{9,8},{10,11... | collective-permute-start | bytes 786440 | tf_op jit(solution)/shard_map/ppermute | solution.py:269
  22.5 17.5 %collective-permute-start.4 = (bf16[2,2,128,256]{3,2,1,0:T(8,128)(2,1)S(1)}, bf16[2,2,128,256]{3,2,1,0:T(8,128)(2,1)S(1)}, u32[]{:S(2)}, u32[]{:S(2)}) collective-permute-start(bf16[2,2,128,256]{3,2,1,0:T(8,128)(2,1)S(1)} %get-tuple-element.10.cross_ref), channel_id=1, source_target_pairs={{0,0},{1,2},{2,1},{3,4},{4,3},{5,6},{6,5},{7,7},{8,8},{9,10},{10,9... | collective-permute-start | bytes 786440 | tf_op jit(solution)/shard_map/ppermute | solution.py:269
  40.0 1.1 %copy-start.10 = (bf16[2,2,128,256]{3,2,1,0:T(8,128)(2,1)}, bf16[2,2,128,256]{3,2,1,0:T(8,128)(2,1)S(1)}, u32[]{:S(2)}) copy-start(bf16[2,2,128,256]{3,2,1,0:T(8,128)(2,1)S(1)} %collective-permute-done.4.from_cross_ref) | copy-start | bytes 786436
  41.1 0.7 copy-start.8
  41.8 21.6 %collective-permute-start.5 = (bf16[2,4,128,256]{3,2,1,0:T(8,128)(2,1)}, bf16[2,4,128,256]{3,2,1,0:T(8,128)(2,1)}, u32[]{:S(2)}, u32[]{:S(2)}) collective-permute-start(bf16[2,4,128,256]{3,2,1,0:T(8,128)(2,1)} %get-tuple-element.11), channel_id=1, source_target_pairs={{0,8},{8,0},{16,24},{24,16},{1,9},{9,1},{17,25},{25,17},{2,10},{10... | collective-permute-start | bytes 1572872 | tf_op jit(solution)/shard_map/ppermute | solution.py:269
  41.8 21.6 %collective-permute-start.6 = (bf16[2,4,128,256]{3,2,1,0:T(8,128)(2,1)}, bf16[2,4,128,256]{3,2,1,0:T(8,128)(2,1)}, u32[]{:S(2)}, u32[]{:S(2)}) collective-permute-start(bf16[2,4,128,256]{3,2,1,0:T(8,128)(2,1)} %get-tuple-element.12), channel_id=1, source_target_pairs={{0,0},{8,16},{16,8},{24,24},{1,1},{9,17},{17,9},{25,25},{2,2},{10,... | collective-permute-start | bytes 1572872 | tf_op jit(solution)/shard_map/ppermute | solution.py:269
  47.2 7.4 %collective-permute-start.2 = (f32[16,2,64]{2,1,0:T(2,128)S(1)}, f32[16,2,64]{2,1,0:T(2,128)S(1)}, u32[]{:S(2)}, u32[]{:S(2)}) collective-permute-start(f32[16,2,64]{2,1,0:T(2,128)S(1)} %copy-done.14), channel_id=1, source_target_pairs={{0,0},{1,1},{8,2},{9,3},{16,4},{17,5},{24,6},{25,7},{2,8},{3,9},{1... | collective-permute-start | bytes 24584 | tf_op jit(solution)/shard_map/ppermute | solution.py:234
  59.1 13.6 %copy-start.13 = (s32[2,2]{1,0:T(2,128)S(1)}, s32[2,2]{1,0:T(2,128)}, u32[]{:S(2)}) copy-start(s32[2,2]{1,0:T(2,128)} %live_ref.5) | copy-start | bytes 52
  59.1 13.6 %all-to-all-start.1 = ((bf16[8,2,64,256]{3,2,1,0:T(8,128)(2,1)}), bf16[8,2,64,256]{3,2,1,0:T(8,128)(2,1)}, u32[]{:S(2)}, u32[]{:S(2)}) async-start(bf16[8,2,64,256]{3,2,1,0:T(8,128)(2,1)} %translations.1), calls=%async_computation.1 | async-start | bytes 1048576 | tf_op jit(solution)/shard_map/all_to_all | solution.py:263
  63.4 1.0 %copy-start.5 = (bf16[2,2,128,256]{3,2,1,0:T(8,128)(2,1)S(1)}, bf16[2,2,128,256]{3,2,1,0:T(8,128)(2,1)}, u32[]{:S(2)}) copy-start(bf16[2,2,128,256]{3,2,1,0:T(8,128)(2,1)} %copy-done.4) | copy-start | bytes 786436
  64.4 0.9 %copy-start.7 = (bf16[2,2,128,256]{3,2,1,0:T(8,128)(2,1)S(1)}, bf16[2,2,128,256]{3,2,1,0:T(8,128)(2,1)}, u32[]{:S(2)}) copy-start(bf16[2,2,128,256]{3,2,1,0:T(8,128)(2,1)} %copy-done.6) | copy-start | bytes 786436
  65.3 0.9 %copy-start.9 = (bf16[2,2,128,256]{3,2,1,0:T(8,128)(2,1)S(1)}, bf16[2,2,128,256]{3,2,1,0:T(8,128)(2,1)}, u32[]{:S(2)}) copy-start(bf16[2,2,128,256]{3,2,1,0:T(8,128)(2,1)} %copy-done.8) | copy-start | bytes 786436
  66.3 0.9 %copy-start.11 = (bf16[2,2,128,256]{3,2,1,0:T(8,128)(2,1)S(1)}, bf16[2,2,128,256]{3,2,1,0:T(8,128)(2,1)}, u32[]{:S(2)}) copy-start(bf16[2,2,128,256]{3,2,1,0:T(8,128)(2,1)} %copy-done.10) | copy-start | bytes 786436
  72.7 1.2 %copy-start.3 = (bf16[2,2,2,128,512]{4,3,2,1,0:T(8,128)(2,1)S(1)}, bf16[2,2,2,128,512]{4,3,2,1,0:T(8,128)(2,1)}, u32[]{:S(2)}) copy-start(bf16[2,2,2,128,512]{4,3,2,1,0:T(8,128)(2,1)} %disaggregate_ref.1) | copy-start | bytes 3145732

commit v2 on v1

v2 whole, which is shorter than its diff:
```python
import functools

import jax
import jax.numpy as jnp
from jax import lax
from jax.experimental import pallas as pl
from jax.experimental.pallas import tpu as pltpu
from jax.sharding import PartitionSpec as P

REACH = 2
PAIR = 2
MIB = 1 << 20
far_offsets = [
    (row_step, col_step)
    for row_step in range(-REACH, REACH + 1)
    for col_step in range(-REACH, REACH + 1)
    if max(abs(row_step), abs(col_step)) == REACH
]
VMEM = pl.BlockSpec(memory_space=pltpu.VMEM)
SMEM = pl.BlockSpec(memory_space=pltpu.SMEM)
ANY = pl.BlockSpec(memory_space=pl.ANY)


def params(mib=56):
    return pltpu.CompilerParams(vmem_limit_bytes=mib * MIB)


def cost(micros):
    return pl.CostEstimate(flops=int(micros * 1.15e9), bytes_accessed=int(micros * 3.69e6), transcendentals=0)


def swap_pairs(count, first):
    pairs = []
    for i in range(count):
        partner = i + 1 if (i - first) % 2 == 0 else i - 1
        pairs.append((i, partner if 0 <= partner < count else None))
    return pairs


def swap_cols(array, first, width=1):
    rows, cols = lax.axis_size("sect"), lax.axis_size("dir")
    sends = []
    for row in range(rows):
        for group, partner in swap_pairs(cols // width, first):
            for col in range(width):
                to = (
                    (row ^ 1) * cols + group * width + col
                    if partner is None
                    else row * cols + partner * width + col
                )
                sends.append((row * cols + group * width + col, to))
    return lax.ppermute(array, ("sect", "dir"), sends)


def swap_rows(array, first):
    rows = lax.axis_size("sect")
    return lax.ppermute(
        array,
        "sect",
        [(row, rows - 1 - row if partner is None else partner) for row, partner in swap_pairs(rows, first)],
    )


def complex_dot(left_real, left_imag, right):
    rows = left_real.shape[0]
    cols = right.shape[1] // 2
    both = jnp.dot(
        jnp.concatenate([left_real, left_imag], axis=0), right, preferred_element_type=jnp.float32
    )
    real = both[:rows, :cols] - both[rows:, cols:]
    imag = both[:rows, cols:] + both[rows:, :cols]
    return real, imag


def pattern_kernel(
    live_ref, unknowns_ref, aggregate_ref, out_ref, near_ref, cross_ref, leaves_ref,
):
    parts, _, narrow, sides = out_ref.shape
    deep, wide, size = unknowns_ref.shape[1:4]

    @pl.when(pl.program_id(0) == 0)
    def _():
        for u in range(deep):
            for v in range(wide):
                keep = live_ref[u, v].astype(jnp.float32).astype(jnp.bfloat16)
                at = (u * wide + v) * size
                for c in range(2):
                    leaves_ref[at : at + size, c * sides : (c + 1) * sides] = (
                        unknowns_ref[c, u, v] * keep
                    )

    left = [
        jnp.concatenate([aggregate_ref[c, u, v] for u in range(deep) for v in range(wide)], axis=1)
        for c in range(2)
    ]
    real, imag = complex_dot(left[0], left[1], leaves_ref[...])
    for part in range(parts):
        out_ref[part, 0] = real[part * narrow : (part + 1) * narrow].astype(jnp.bfloat16)
        out_ref[part, 1] = imag[part * narrow : (part + 1) * narrow].astype(jnp.bfloat16)

    @pl.when(pl.program_id(0) == 0)
    def _():
        odd = lax.rem(lax.axis_index("dir"), 2)

        def leaf(u, v, c):
            at = pl.multiple_of((u * wide + v) * size, size)
            return leaves_ref[pl.ds(at, size), c * sides : (c + 1) * sides]

        for c in range(2):
            for u in range(deep):
                near_ref[c, u] = leaf(u, 1 - odd, c)
                cross_ref[c, u] = leaf(u, odd, c)


def translate_kernel(
    groups, own_ref, even_ref, odd_ref, coef_ref, out_ref, held_ref, made_ref, coefs_ref, wide_ref,
    coef_sem, in_sem, out_sem,
):
    parts, _, narrow, sides = own_ref.shape
    box_rows = parts // PAIR
    depth, lanes = min(16, narrow), min(128, sides)
    group = lax.axis_index("dir") // PAIR
    parity = lax.rem(group, 2)
    no_even = (parity == 0) & (group == groups - 1)
    no_odd = (group == 0) | ((parity == 1) & (group == groups - 1))
    sources = ((own_ref, 2, None), (even_ref, 1 - parity, no_even), (odd_ref, parity, no_odd))

    def span(at):
        return pl.ds(pl.multiple_of(at * depth, depth), depth)

    def arrival(which, at):
        ref, slot, _ = sources[which]
        return pltpu.make_async_copy(
            ref.at[:, :, span(at)], held_ref.at[slot, :, :, span(at)], in_sem.at[which, at]
        )

    def departure(at):
        return pltpu.make_async_copy(
            made_ref.at[:, :, span(at)], out_ref.at[:, :, span(at)], out_sem.at[at]
        )

    coefs_here = pltpu.make_async_copy(coef_ref, coefs_ref, coef_sem)
    coefs_here.start()
    for at in range(narrow // depth):
        for which in range(3):
            arrival(which, at).start()

    coefs_here.wait()
    coefs = coefs_ref[...].T
    for index in range(coefs.shape[1]):
        wide_ref[index] = jnp.broadcast_to(coefs[:, index : index + 1], (narrow, lanes))

    def chunk(at, carry):
        for which in range(3):
            arrival(which, at).wait()
        for _, slot, missing in sources[1:]:

            @pl.when(missing)
            def _():
                held_ref[slot, :, :, span(at)] = jnp.zeros((parts, 2, depth, sides), held_ref.dtype)

        def tile(place, carry):
            across = pl.ds(pl.multiple_of(place * lanes, lanes), lanes)
            for col in range(PAIR):
                totals = {}
                for source in range(box_rows):
                    held = {}
                    for step in range(-REACH, REACH + 1):
                        slot = 0 if col + step < 0 else 1 if col + step >= PAIR else 2
                        box = source * PAIR + (col + step) % PAIR
                        held[step] = [
                            held_ref[slot, box, c, span(at), across].astype(jnp.float32)
                            for c in range(2)
                        ]
                    for target in range(max(0, source - REACH), min(box_rows, source + REACH + 1)):
                        real = imag = None
                        for index, (row_step, step) in enumerate(far_offsets):
                            if row_step != source - target:
                                continue
                            coef_real = wide_ref[2 * index, span(at)]
                            coef_imag = wide_ref[2 * index + 1, span(at)]
                            from_real, from_imag = held[step]
                            term_real = coef_real * from_real - coef_imag * from_imag
                            term_imag = coef_real * from_imag + coef_imag * from_real
                            real = term_real if real is None else real + term_real
                            imag = term_imag if imag is None else imag + term_imag
                        real = real.astype(jnp.bfloat16).astype(jnp.float32)
                        imag = imag.astype(jnp.bfloat16).astype(jnp.float32)
                        if target in totals:
                            old = totals[target]
                            totals[target] = (old[0] + real, old[1] + imag)
                        else:
                            totals[target] = (real, imag)
                for target, total in totals.items():
                    for c in range(2):
                        made_ref[target * PAIR + col, c, span(at), across] = total[c].astype(jnp.bfloat16)
            return carry

        lax.fori_loop(0, sides // lanes, tile, 0, unroll=True)
        departure(at).start()
        return carry

    lax.fori_loop(0, narrow // depth, chunk, 0)
    for at in range(narrow // depth):
        departure(at).wait()


def row_kernel(near_ref, cross_ref, from_cross_ref, out_near_ref, out_cross_ref):
    odd = lax.rem(lax.axis_index("sect"), 2)
    for slot, ref in enumerate((near_ref, cross_ref, from_cross_ref)):
        out_near_ref[:, slot] = ref[:, 1 - odd]
        out_cross_ref[:, slot] = ref[:, odd]


def column_kernel(near_ref, row_near_ref, row_cross_ref, out_ref):
    deep = near_ref.shape[1]
    out_ref[:, :deep] = near_ref[...]
    out_ref[:, deep] = row_near_ref[:, 0]
    out_ref[:, deep + 1] = row_cross_ref[:, 0]


def near_kernel(
    near_ref, cross_ref, from_cross_ref, from_near_ref, row_near_ref, row_cross_ref, blocks_ref,
    out_ref, grid_ref,
):
    sides = near_ref.shape[3]
    deep = near_ref.shape[1]
    wide = 2
    leaf = pl.program_id(0)

    @pl.when(leaf == 0)
    def _():
        col_at, col_count = lax.axis_index("dir"), lax.axis_size("dir")
        row_at, row_count = lax.axis_index("sect"), lax.axis_size("sect")
        col_odd, row_odd = lax.rem(col_at, 2), lax.rem(row_at, 2)
        columns = (2 - col_odd, 1 + col_odd, 3 * col_odd, 3 - 3 * col_odd)
        row_next, row_last = 3 - 3 * row_odd, 3 * row_odd
        no_col = ((col_odd == 0) & (col_at == 0)) | ((col_odd == 1) & (col_at == col_count - 1))
        no_row = ((row_odd == 0) & (row_at == 0)) | ((row_odd == 1) & (row_at == row_count - 1))
        for slot, ref in enumerate((near_ref, cross_ref, from_cross_ref, from_near_ref)):
            for c in range(2):
                half = slice(c * sides, (c + 1) * sides)
                for u in range(deep):
                    grid_ref[1 + u, columns[slot], :, half] = ref[c, u]
                if slot < 3:
                    grid_ref[row_next, columns[slot], :, half] = row_near_ref[c, slot]
                    grid_ref[row_last, columns[slot], :, half] = row_cross_ref[c, slot]
                else:
                    grid_ref[row_next, columns[slot], :, half] = ref[c, deep]
                    grid_ref[row_last, columns[slot], :, half] = ref[c, deep + 1]

        @pl.when(no_col)
        def _():
            for i in range(deep + 2):
                grid_ref[i, columns[2]] = jnp.zeros(grid_ref.shape[2:], grid_ref.dtype)

        @pl.when(no_row)
        def _():
            for j in range(wide + 2):
                grid_ref[row_last, j] = jnp.zeros(grid_ref.shape[2:], grid_ref.dtype)

    u, v = leaf // wide, lax.rem(leaf, wide)
    right = jnp.concatenate(
        [grid_ref[u + a, v + b] for a in range(3) for b in range(3)], axis=0
    )
    left = [jnp.concatenate([blocks_ref[c, 0, 0, k] for k in range(9)], axis=1) for c in range(2)]
    real, imag = complex_dot(left[0], left[1], right)
    out_ref[0, 0, 0] = real
    out_ref[1, 0, 0] = imag


def far_kernel(
    live_ref, incoming_ref, disaggregate_ref, near_ref, out_ref, right_ref, made_ref, in_sem, out_sem
):
    parts, _, narrow, sides = incoming_ref.shape
    deep, wide = live_ref.shape

    def arrival(part, c):
        return pltpu.make_async_copy(
            incoming_ref.at[part, c],
            right_ref.at[part * narrow : (part + 1) * narrow, c * sides : (c + 1) * sides],
            in_sem.at[part, c],
        )

    def departure(u, v):
        return pltpu.make_async_copy(
            made_ref.at[:, u, v], out_ref.at[:, u, v], out_sem.at[u, v]
        )

    for part in range(parts):
        for c in range(2):
            arrival(part, c).start()
    for part in range(parts):
        for c in range(2):
            arrival(part, c).wait()
    for u in range(deep):
        for v in range(wide):
            live = live_ref[u, v].astype(jnp.float32)
            real, imag = complex_dot(
                disaggregate_ref[0, u, v], disaggregate_ref[1, u, v], right_ref[...]
            )
            made_ref[0, u, v] = (near_ref[0, u, v] + real) * live
            made_ref[1, u, v] = (near_ref[1, u, v] + imag) * live
            departure(u, v).start()
    for u in range(deep):
        for v in range(wide):
            departure(u, v).wait()


def direction_coefs(translate, narrow):
    sect_count, dir_count = lax.axis_size("sect"), lax.axis_size("dir")
    groups = dir_count // PAIR
    held = translate.shape[2]
    pieces = narrow // held
    got = []
    for turn in range(pieces):
        sends = []
        for sect in range(sect_count):
            for col in range(dir_count):
                group, block = col // PAIR, sect * PAIR + col % PAIR
                shard = block * pieces + (turn + group // sect_count) % pieces
                sends.append(((group % sect_count) * dir_count + shard, sect * dir_count + col))
        got.append(lax.ppermute(translate, ("sect", "dir"), sends))
    if pieces == 1:
        return got[0]
    first = lax.axis_index("dir") // PAIR // sect_count
    return jnp.concatenate(
        [
            lax.dynamic_index_in_dim(
                jnp.stack(got), lax.rem(piece - first + pieces, pieces), 0, keepdims=False
            )
            for piece in range(pieces)
        ],
        axis=2,
    )


def shards(unknowns, leaf_live, near_blocks, aggregate, disaggregate, translate):
    sect_count, dir_count = lax.axis_size("sect"), lax.axis_size("dir")
    _, deep, wide, size, sides = unknowns.shape
    total_dirs = aggregate.shape[3]
    groups = dir_count // PAIR
    parts = sect_count * PAIR
    narrow = total_dirs // parts
    bf16, f32 = jnp.bfloat16, jnp.float32
    members = [
        [sect * dir_count + group * PAIR + col for sect in range(sect_count) for col in range(PAIR)]
        for group in range(groups)
    ]

    def spread(array):
        return lax.all_to_all(
            array, ("sect", "dir"), split_axis=0, concat_axis=0, tiled=True, axis_index_groups=members
        )

    column = jax.ShapeDtypeStruct((2, deep, size, sides), bf16)
    steps = 2
    whole = [pl.BlockSpec(a.shape, lambda i, n=len(a.shape): (0,) * n) for a in (unknowns, column)]
    patterns, col_near, col_cross = pl.pallas_call(
        pattern_kernel,
        grid=(steps,),
        in_specs=[
            SMEM,
            whole[0],
            pl.BlockSpec((2, deep, wide, total_dirs // steps, size), lambda i: (0, 0, 0, i, 0)),
        ],
        out_specs=[
            pl.BlockSpec((parts // steps, 2, narrow, sides), lambda i: (i, 0, 0, 0)),
            whole[1],
            whole[1],
        ],
        out_shape=[jax.ShapeDtypeStruct((parts, 2, narrow, sides), bf16), column, column],
        scratch_shapes=[pltpu.VMEM((deep * wide * size, 2 * sides), bf16)],
        compiler_params=params(),
        name="patterns",
    )(leaf_live, unknowns, aggregate)
    from_cross = swap_cols(col_cross, 1)
    row = jax.ShapeDtypeStruct((2, 3, size, sides), bf16)
    row_near, row_cross = pl.pallas_call(
        row_kernel,
        in_specs=[VMEM] * 3,
        out_specs=[VMEM] * 2,
        out_shape=[row, row],
        compiler_params=params(16),
        cost_estimate=cost(4000),
        name="rows",
    )(col_near, col_cross, from_cross)
    translate, _ = lax.optimization_barrier((translate, row_cross))
    coefs = direction_coefs(translate, narrow)
    own = spread(patterns)
    own, _, _ = lax.optimization_barrier((own, row_near, row_cross))
    row_near = swap_rows(row_near, 0)
    row_cross = swap_rows(row_cross, 1)
    even = swap_cols(own, 0, PAIR)
    odd = swap_cols(own, 1, PAIR)
    tall = pl.pallas_call(
        column_kernel,
        in_specs=[VMEM] * 3,
        out_specs=VMEM,
        out_shape=jax.ShapeDtypeStruct((2, deep + 2, size, sides), bf16),
        compiler_params=params(16),
        cost_estimate=cost(4000),
        name="columns",
    )(col_near, row_near, row_cross)
    from_near = swap_cols(tall, 0)
    even, odd, coefs, _ = lax.optimization_barrier((even, odd, coefs, tall))
    coefs = coefs.reshape(2 * len(far_offsets), narrow)

    chunks = narrow // min(16, narrow)
    incoming = pl.pallas_call(
        functools.partial(translate_kernel, groups),
        in_specs=[ANY] * 4,
        out_specs=ANY,
        out_shape=jax.ShapeDtypeStruct(own.shape, bf16),
        scratch_shapes=[
            pltpu.VMEM((3, *own.shape), bf16),
            pltpu.VMEM(own.shape, bf16),
            pltpu.VMEM(coefs.shape, f32),
            pltpu.VMEM((2 * len(far_offsets), narrow, min(128, sides)), f32),
            pltpu.SemaphoreType.DMA,
            pltpu.SemaphoreType.DMA((3, chunks)),
            pltpu.SemaphoreType.DMA((chunks,)),
        ],
        compiler_params=params(16),
        cost_estimate=cost(4000),
        name="translations",
    )(own, even, odd, coefs)
    returned = spread(incoming)

    leaf_out = pl.BlockSpec((2, 1, 1, size, sides), lambda i: (0, i // wide, i % wide, 0, 0))
    field = jax.ShapeDtypeStruct(unknowns.shape, f32)
    near = pl.pallas_call(
        near_kernel,
        grid=(deep * wide,),
        in_specs=[VMEM] * 6
        + [pl.BlockSpec((2, 1, 1, 9, size, size), lambda i: (0, i // wide, i % wide, 0, 0, 0))],
        out_specs=leaf_out,
        out_shape=field,
        scratch_shapes=[pltpu.VMEM((deep + 2, wide + 2, size, 2 * sides), bf16)],
        compiler_params=params(16),
        cost_estimate=cost(4000),
        name="near",
    )(
        col_near, col_cross, from_cross, from_near, row_near, row_cross, near_blocks,
    )
    return pl.pallas_call(
        far_kernel,
        in_specs=[SMEM, ANY, VMEM, VMEM],
        out_specs=ANY,
        out_shape=field,
        scratch_shapes=[
            pltpu.VMEM((total_dirs, 2 * sides), bf16),
            pltpu.VMEM(unknowns.shape, f32),
            pltpu.SemaphoreType.DMA((parts, 2)),
            pltpu.SemaphoreType.DMA((deep, wide)),
        ],
        compiler_params=params(16),
        name="far",
    )(leaf_live, returned, disaggregate, near)


def solution(mesh):
    in_specs = (
        P(None, "sect", "dir", None, None),
        P("sect", "dir"),
        P(None, "sect", "dir", None, None, None),
        P(None, "sect", "dir", None, None),
        P(None, "sect", "dir", None, None),
        P(None, None, "dir"),
    )
    out_specs = P(None, "sect", "dir", None, None)
    return jax.shard_map(shards, mesh=mesh, in_specs=in_specs, out_specs=out_specs, check_vma=False)
```

time: 78.4 us -> 57.8 us (0.74)
  the two profiles are of different devices: /device:TPU:16 before, /device:TPU:0 now
where the time goes in v2:
time: 57.8 us; the launch traced here: 57.2 us
  starting transfers between devices  21.7 us (38%)
  waiting for transfers between devices  15.6 us (27%)
  Pallas kernels  15.1 us (26%)
  local copies, waits for them, and re-layouts  4.68 us (8%)
    all_to_all x2, starting transfers between devices, spread(): lax.all_to_all(array, ('sect', 'dir'), split_axis=0, concat_axis=0, tiled...  11.1 us
    ppermute x4, starting transfers between devices, swap_cols(): return lax.ppermute(array, ('sect', 'dir'), sends)  6.43 us
    ppermute x4, waiting for transfers between devices, swap_cols(): return lax.ppermute(array, ('sect', 'dir'), sends)  6.34 us
    all_to_all x2, waiting for transfers between devices, spread(): lax.all_to_all(array, ('sect', 'dir'), split_axis=0, concat_axis=0, tiled...  6.13 us
    unnamed x28, local copies, waits for them, and re-layouts  4.68 us
    pallas_call x1, Pallas kernels, shards(): pl.pallas_call(functools.partial(translate_kernel, groups), in_specs=[ANY...  4.12 us
    pallas_call x1, Pallas kernels, shards(): pl.pallas_call(near_kernel, grid=(deep * wide,), in_specs=[VMEM] * 6 + [p...  3.75 us
    pallas_call x1, Pallas kernels, shards(): pl.pallas_call(far_kernel, in_specs=[SMEM, ANY, VMEM, VMEM], out_specs=AN...  3.23 us
  transfers between devices with their start and end apart: 9, of which 4 were waited for; matrix products, arithmetic and copies ran while one was open for 0% of the time, Pallas kernels for 15%

profile of v2, /device:TPU:0, one launch (start us, length us, event | category | flops | bytes accessed | tf_op | source)
XLA Modules:
  0.0 57.2 jit_solution(9553443692748302620)
XLA Ops:
  0.0 3.1 %patterns.1 = (bf16[8,2,64,256]{3,2,1,0:T(8,128)(2,1)}, bf16[2,2,128,256]{3,2,1,0:T(8,128)(2,1)}, bf16[2,2,128,256]{3,2,1,0:T(8,128)(2,1)}) custom-call(s32[2,2]{1,0:T(2,128)} %live_ref.3, bf16[2,2,2,128,256]{4,3,2,1,0:T(8,128)(2,1)} %unknowns_ref.1, bf16[2,2,2,512,128]{4,3,2,1,0:T(8,128)(2,1)} %aggregate_ref.1), custom_call_target="tpu_custom_call" | custom-call | tf_op jit(solution)/shard_map/patterns/pallas_call | solution.py:359
  3.1 0.5 collective-permute-start
  3.5 6.3 %all-to-all-start = ((bf16[8,2,64,256]{3,2,1,0:T(8,128)(2,1)}), bf16[8,2,64,256]{3,2,1,0:T(8,128)(2,1)}, u32[]{:S(2)}, u32[]{:S(2)}) async-start(bf16[8,2,64,256]{3,2,1,0:T(8,128)(2,1)} %get-tuple-element.15), calls=%async_computation | async-start | bytes 1048576 | tf_op jit(solution)/shard_map/all_to_all | solution.py:352
  9.8 0.0 collective-permute-done.from_cross_ref
  9.8 0.0 copy-start.12
  9.8 1.0 %copy-done.7 = bf16[2,2,128,256]{3,2,1,0:T(8,128)(2,1)S(1)} copy-done((bf16[2,2,128,256]{3,2,1,0:T(8,128)(2,1)S(1)}, bf16[2,2,128,256]{3,2,1,0:T(8,128)(2,1)}, u32[]{:S(2)}) %copy-start.7) | copy-done | bytes 262168
  10.9 0.9 %copy-done.10 = bf16[2,2,128,256]{3,2,1,0:T(8,128)(2,1)S(1)} copy-done((bf16[2,2,128,256]{3,2,1,0:T(8,128)(2,1)S(1)}, bf16[2,2,128,256]{3,2,1,0:T(8,128)(2,1)}, u32[]{:S(2)}) %copy-start.10) | copy-done | bytes 262168
  11.8 0.1 rows.1
  11.9 0.6 collective-permute-start.4
  12.4 1.6 %collective-permute-start.5 = (bf16[2,3,128,256]{3,2,1,0:T(8,128)(2,1)S(1)}, bf16[2,3,128,256]{3,2,1,0:T(8,128)(2,1)S(1)}, u32[]{:S(2)}, u32[]{:S(2)}) collective-permute-start(bf16[2,3,128,256]{3,2,1,0:T(8,128)(2,1)S(1)} %get-tuple-element.19), channel_id=1, source_target_pairs={{0,24},{8,16},{16,8},{24,0},{1,25},{9,17},{17,9},{25,1},{2,26},{10... | collective-permute-start | bytes 1179656 | tf_op jit(solution)/shard_map/ppermute | solution.py:57
  14.1 2.0 %collective-permute-start.3 = (f32[16,2,64]{2,1,0:T(2,128)}, f32[16,2,64]{2,1,0:T(2,128)}, u32[]{:S(2)}, u32[]{:S(2)}) collective-permute-start(f32[16,2,64]{2,1,0:T(2,128)} %param.11), channel_id=1, source_target_pairs={{0,0},{1,1},{8,2},{9,3},{16,4},{17,5},{24,6},{25,7},{2,8},{3,9},{1... | collective-permute-start | bytes 24584 | tf_op jit(solution)/shard_map/ppermute | solution.py:323
  16.0 3.2 %all-to-all-done.own_ref = bf16[8,2,64,256]{3,2,1,0:T(8,128)(2,1)} async-done(((bf16[8,2,64,256]{3,2,1,0:T(8,128)(2,1)}), bf16[8,2,64,256]{3,2,1,0:T(8,128)(2,1)}, u32[]{:S(2)}, u32[]{:S(2)}) %all-to-all-start) | async-done | bytes 524320 | tf_op jit(solution)/shard_map/all_to_all | solution.py:352
  19.2 2.0 %collective-permute-start.2 = (bf16[8,2,64,256]{3,2,1,0:T(8,128)(2,1)}, bf16[8,2,64,256]{3,2,1,0:T(8,128)(2,1)}, u32[]{:S(2)}, u32[]{:S(2)}) collective-permute-start(bf16[8,2,64,256]{3,2,1,0:T(8,128)(2,1)} %all-to-all-done.own_ref), channel_id=1, source_target_pairs={{0,8},{1,9},{2,4},{3,5},{4,2},{5,3},{6,14},{7,15},{8,0},{9,1},{10,... | collective-permute-start | bytes 1572872 | tf_op jit(solution)/shard_map/ppermute | solution.py:52
  21.2 2.3 %collective-permute-start.1 = (bf16[8,2,64,256]{3,2,1,0:T(8,128)(2,1)}, bf16[8,2,64,256]{3,2,1,0:T(8,128)(2,1)}, u32[]{:S(2)}, u32[]{:S(2)}) collective-permute-start(bf16[8,2,64,256]{3,2,1,0:T(8,128)(2,1)} %all-to-all-done.own_ref), channel_id=1, source_target_pairs={{0,2},{1,3},{2,0},{3,1},{4,6},{5,7},{6,4},{7,5},{8,10},{9,11},{10,... | collective-permute-start | bytes 1572872 | tf_op jit(solution)/shard_map/ppermute | solution.py:52
  23.5 0.0 collective-permute-done.4.row_near_ref
  23.5 3.1 %collective-permute-done.5.row_cross_ref = bf16[2,3,128,256]{3,2,1,0:T(8,128)(2,1)S(1)} collective-permute-done((bf16[2,3,128,256]{3,2,1,0:T(8,128)(2,1)S(1)}, bf16[2,3,128,256]{3,2,1,0:T(8,128)(2,1)S(1)}, u32[]{:S(2)}, u32[]{:S(2)}) %collective-permute-start.5) | collective-permute-done | bytes 393248 | tf_op jit(solution)/shard_map/ppermute | solution.py:57
  26.6 0.0 copy-done.8
  26.6 0.9 %columns.1 = bf16[2,4,128,256]{3,2,1,0:T(8,128)(2,1)} custom-call(bf16[2,2,128,256]{3,2,1,0:T(8,128)(2,1)S(1)} %copy-done.8, bf16[2,3,128,256]{3,2,1,0:T(8,128)(2,1)S(1)} %collective-permute-done.4.row_near_ref, bf16[2,3,128,256]{3,2,1,0:T(8,128)(2,1)S(1)} %collective-permute-done.5.row_cross_ref), custom_call_target="tpu_custom_call" | custom-call | flops 4600000151552 | bytes 14759999488 | tf_op jit(solution)/shard_map/columns/pallas_call | solution.py:396
  27.5 0.1 copy-done.5
  27.5 1.7 %collective-permute-start.6 = (bf16[2,4,128,256]{3,2,1,0:T(8,128)(2,1)}, bf16[2,4,128,256]{3,2,1,0:T(8,128)(2,1)}, u32[]{:S(2)}, u32[]{:S(2)}) collective-permute-start(bf16[2,4,128,256]{3,2,1,0:T(8,128)(2,1)} %columns.1), channel_id=1, source_target_pairs={{0,1},{1,0},{2,3},{3,2},{4,5},{5,4},{6,7},{7,6},{8,9},{9,8},{10,11... | collective-permute-start | bytes 1572872 | tf_op jit(solution)/shard_map/ppermute | solution.py:52
  29.3 0.0 collective-permute-done.3
  29.3 0.0 collective-permute-done.2.odd_ref
  29.3 6.3 %collective-permute-done.1.even_ref = bf16[8,2,64,256]{3,2,1,0:T(8,128)(2,1)} collective-permute-done((bf16[8,2,64,256]{3,2,1,0:T(8,128)(2,1)}, bf16[8,2,64,256]{3,2,1,0:T(8,128)(2,1)}, u32[]{:S(2)}, u32[]{:S(2)}) %collective-permute-start.1) | collective-permute-done | bytes 524320 | tf_op jit(solution)/shard_map/ppermute | solution.py:52
  35.6 4.1 %translations.1 = bf16[8,2,64,256]{3,2,1,0:T(8,128)(2,1)} custom-call(bf16[8,2,64,256]{3,2,1,0:T(8,128)(2,1)} %all-to-all-done.own_ref, bf16[8,2,64,256]{3,2,1,0:T(8,128)(2,1)} %collective-permute-done.1.even_ref, bf16[8,2,64,256]{3,2,1,0:T(8,128)(2,1)} %collective-permute-done.2.odd_ref, f32[32,64]{1,0:T(8,128)} %bitcast.coef_ref), custom_call_target="tpu_custom_call" | custom-call | flops 4600000151552 | bytes 14759999488 | tf_op jit(solution)/shard_map/translations/pallas_call | solution.py:410
  39.7 4.9 %all-to-all-start.1 = ((bf16[8,2,64,256]{3,2,1,0:T(8,128)(2,1)}), bf16[8,2,64,256]{3,2,1,0:T(8,128)(2,1)}, u32[]{:S(2)}, u32[]{:S(2)}) async-start(bf16[8,2,64,256]{3,2,1,0:T(8,128)(2,1)} %translations.1), calls=%async_computation.1 | async-start | bytes 1048576 | tf_op jit(solution)/shard_map/all_to_all | solution.py:352
  44.6 0.0 collective-permute-done.6.from_near_ref
  44.7 0.0 copy-start.2
  44.7 1.7 %copy-done.2 = bf16[2,2,2,9,128,128]{5,4,3,2,1,0:T(8,128)(2,1)S(1)} copy-done((bf16[2,2,2,9,128,128]{5,4,3,2,1,0:T(8,128)(2,1)S(1)}, bf16[2,2,2,9,128,128]{5,4,3,2,1,0:T(8,128)(2,1)}, u32[]{:S(2)}) %copy-start.2) | copy-done | bytes 2359320
  46.3 0.9 %copy-done.13 = bf16[2,2,128,256]{3,2,1,0:T(8,128)(2,1)S(1)} copy-done((bf16[2,2,128,256]{3,2,1,0:T(8,128)(2,1)S(1)}, bf16[2,2,128,256]{3,2,1,0:T(8,128)(2,1)}, u32[]{:S(2)}) %copy-start.13) | copy-done | bytes 262168
  47.3 3.7 %near.1.near_ref = f32[2,2,2,128,256]{4,3,2,1,0:T(8,128)S(1)} custom-call(bf16[2,2,128,256]{3,2,1,0:T(8,128)(2,1)S(1)} %copy-done.9, bf16[2,2,128,256]{3,2,1,0:T(8,128)(2,1)S(1)} %copy-done.11, bf16[2,2,128,256]{3,2,1,0:T(8,128)(2,1)S(1)} %copy-done.13, bf16[2,4,128,256]{3,2,1,0:T(8,128)(2,1)} %collective-permute-done.6.from_near_ref, ...), custom_call_target="tpu_custom_call" | custom-call | flops 4600000151552 | bytes 14759999488 | tf_op jit(solution)/shard_map/near/pallas_call | solution.py:432
  51.0 2.9 %all-to-all-done.1.incoming_ref = bf16[8,2,64,256]{3,2,1,0:T(8,128)(2,1)} async-done(((bf16[8,2,64,256]{3,2,1,0:T(8,128)(2,1)}), bf16[8,2,64,256]{3,2,1,0:T(8,128)(2,1)}, u32[]{:S(2)}, u32[]{:S(2)}) %all-to-all-start.1) | async-done | bytes 524320 | tf_op jit(solution)/shard_map/all_to_all | solution.py:352
  54.0 3.2 %far.1 = f32[2,2,2,128,256]{4,3,2,1,0:T(8,128)} custom-call(s32[2,2]{1,0:T(2,128)S(1)} %copy-done.1, bf16[8,2,64,256]{3,2,1,0:T(8,128)(2,1)} %all-to-all-done.1.incoming_ref, bf16[2,2,2,128,512]{4,3,2,1,0:T(8,128)(2,1)S(1)} %copy-done, f32[2,2,2,128,256]{4,3,2,1,0:T(8,128)S(1)} %near.1.near_ref), custom_call_target="tpu_custom_call" | custom-call | tf_op jit(solution)/shard_map/far/pallas_call | solution.py:446
  (20 shorter events, 0.0 us)
Async XLA Ops:
  3.1 6.7 %collective-permute-start = (bf16[2,2,128,256]{3,2,1,0:T(8,128)(2,1)}, bf16[2,2,128,256]{3,2,1,0:T(8,128)(2,1)S(1)}, u32[]{:S(2)}, u32[]{:S(2)}) collective-permute-start(bf16[2,2,128,256]{3,2,1,0:T(8,128)(2,1)} %get-tuple-element.17.cross_ref), channel_id=1, source_target_pairs={{0,8},{1,2},{2,1},{3,4},{4,3},{5,6},{6,5},{7,15},{8,0},{9,10},{10,... | collective-permute-start | bytes 786440 | tf_op jit(solution)/shard_map/ppermute | solution.py:52
  3.5 15.7 %all-to-all-start = ((bf16[8,2,64,256]{3,2,1,0:T(8,128)(2,1)}), bf16[8,2,64,256]{3,2,1,0:T(8,128)(2,1)}, u32[]{:S(2)}, u32[]{:S(2)}) async-start(bf16[8,2,64,256]{3,2,1,0:T(8,128)(2,1)} %get-tuple-element.15), calls=%async_computation | async-start | bytes 1048576 | tf_op jit(solution)/shard_map/all_to_all | solution.py:352
  9.8 2.1 %copy-start.12 = (bf16[2,2,128,256]{3,2,1,0:T(8,128)(2,1)}, bf16[2,2,128,256]{3,2,1,0:T(8,128)(2,1)S(1)}, u32[]{:S(2)}) copy-start(bf16[2,2,128,256]{3,2,1,0:T(8,128)(2,1)S(1)} %collective-permute-done.from_cross_ref) | copy-start | bytes 786436
  9.8 1.0 %copy-start.7 = (bf16[2,2,128,256]{3,2,1,0:T(8,128)(2,1)S(1)}, bf16[2,2,128,256]{3,2,1,0:T(8,128)(2,1)}, u32[]{:S(2)}) copy-start(bf16[2,2,128,256]{3,2,1,0:T(8,128)(2,1)} %get-tuple-element.16.near_ref) | copy-start | bytes 786436
  10.9 0.9 %copy-start.10 = (bf16[2,2,128,256]{3,2,1,0:T(8,128)(2,1)S(1)}, bf16[2,2,128,256]{3,2,1,0:T(8,128)(2,1)}, u32[]{:S(2)}) copy-start(bf16[2,2,128,256]{3,2,1,0:T(8,128)(2,1)} %get-tuple-element.17.cross_ref) | copy-start | bytes 786436
  11.8 14.8 %copy-start.8 = (bf16[2,2,128,256]{3,2,1,0:T(8,128)(2,1)S(1)}, bf16[2,2,128,256]{3,2,1,0:T(8,128)(2,1)}, u32[]{:S(2)}) copy-start(bf16[2,2,128,256]{3,2,1,0:T(8,128)(2,1)} %get-tuple-element.16.near_ref) | copy-start | bytes 786436
  11.9 11.6 %collective-permute-start.4 = (bf16[2,3,128,256]{3,2,1,0:T(8,128)(2,1)S(1)}, bf16[2,3,128,256]{3,2,1,0:T(8,128)(2,1)S(1)}, u32[]{:S(2)}, u32[]{:S(2)}) collective-permute-start(bf16[2,3,128,256]{3,2,1,0:T(8,128)(2,1)S(1)} %get-tuple-element.18), channel_id=1, source_target_pairs={{0,8},{8,0},{16,24},{24,16},{1,9},{9,1},{17,25},{25,17},{2,10},{10... | collective-permute-start | bytes 1179656 | tf_op jit(solution)/shard_map/ppermute | solution.py:57
  12.4 14.2 %collective-permute-start.5 = (bf16[2,3,128,256]{3,2,1,0:T(8,128)(2,1)S(1)}, bf16[2,3,128,256]{3,2,1,0:T(8,128)(2,1)S(1)}, u32[]{:S(2)}, u32[]{:S(2)}) collective-permute-start(bf16[2,3,128,256]{3,2,1,0:T(8,128)(2,1)S(1)} %get-tuple-element.19), channel_id=1, source_target_pairs={{0,24},{8,16},{16,8},{24,0},{1,25},{9,17},{17,9},{25,1},{2,26},{10... | collective-permute-start | bytes 1179656 | tf_op jit(solution)/shard_map/ppermute | solution.py:57
  14.1 15.2 %collective-permute-start.3 = (f32[16,2,64]{2,1,0:T(2,128)}, f32[16,2,64]{2,1,0:T(2,128)}, u32[]{:S(2)}, u32[]{:S(2)}) collective-permute-start(f32[16,2,64]{2,1,0:T(2,128)} %param.11), channel_id=1, source_target_pairs={{0,0},{1,1},{8,2},{9,3},{16,4},{17,5},{24,6},{25,7},{2,8},{3,9},{1... | collective-permute-start | bytes 24584 | tf_op jit(solution)/shard_map/ppermute | solution.py:323
  19.2 10.1 %collective-permute-start.2 = (bf16[8,2,64,256]{3,2,1,0:T(8,128)(2,1)}, bf16[8,2,64,256]{3,2,1,0:T(8,128)(2,1)}, u32[]{:S(2)}, u32[]{:S(2)}) collective-permute-start(bf16[8,2,64,256]{3,2,1,0:T(8,128)(2,1)} %all-to-all-done.own_ref), channel_id=1, source_target_pairs={{0,8},{1,9},{2,4},{3,5},{4,2},{5,3},{6,14},{7,15},{8,0},{9,1},{10,... | collective-permute-start | bytes 1572872 | tf_op jit(solution)/shard_map/ppermute | solution.py:52
  21.2 14.4 %collective-permute-start.1 = (bf16[8,2,64,256]{3,2,1,0:T(8,128)(2,1)}, bf16[8,2,64,256]{3,2,1,0:T(8,128)(2,1)}, u32[]{:S(2)}, u32[]{:S(2)}) collective-permute-start(bf16[8,2,64,256]{3,2,1,0:T(8,128)(2,1)} %all-to-all-done.own_ref), channel_id=1, source_target_pairs={{0,2},{1,3},{2,0},{3,1},{4,6},{5,7},{6,4},{7,5},{8,10},{9,11},{10,... | collective-permute-start | bytes 1572872 | tf_op jit(solution)/shard_map/ppermute | solution.py:52
  23.5 4.0 %copy-start.3 = (bf16[2,3,128,256]{3,2,1,0:T(8,128)(2,1)}, bf16[2,3,128,256]{3,2,1,0:T(8,128)(2,1)S(1)}, u32[]{:S(2)}) copy-start(bf16[2,3,128,256]{3,2,1,0:T(8,128)(2,1)S(1)} %collective-permute-done.4.row_near_ref) | copy-start | bytes 1179652
  26.6 0.9 %copy-start.5 = (bf16[2,3,128,256]{3,2,1,0:T(8,128)(2,1)}, bf16[2,3,128,256]{3,2,1,0:T(8,128)(2,1)S(1)}, u32[]{:S(2)}) copy-start(bf16[2,3,128,256]{3,2,1,0:T(8,128)(2,1)S(1)} %collective-permute-done.5.row_cross_ref) | copy-start | bytes 1179652
  27.5 17.1 %collective-permute-start.6 = (bf16[2,4,128,256]{3,2,1,0:T(8,128)(2,1)}, bf16[2,4,128,256]{3,2,1,0:T(8,128)(2,1)}, u32[]{:S(2)}, u32[]{:S(2)}) collective-permute-start(bf16[2,4,128,256]{3,2,1,0:T(8,128)(2,1)} %columns.1), channel_id=1, source_target_pairs={{0,1},{1,0},{2,3},{3,2},{4,5},{5,4},{6,7},{7,6},{8,9},{9,8},{10,11... | collective-permute-start | bytes 1572872 | tf_op jit(solution)/shard_map/ppermute | solution.py:52
  35.6 9.0 %copy-start.4 = (bf16[2,3,128,256]{3,2,1,0:T(8,128)(2,1)S(1)}, bf16[2,3,128,256]{3,2,1,0:T(8,128)(2,1)}, u32[]{:S(2)}) copy-start(bf16[2,3,128,256]{3,2,1,0:T(8,128)(2,1)} %copy-done.3) | copy-start | bytes 1179652
  35.6 9.0 %copy-start.6 = (bf16[2,3,128,256]{3,2,1,0:T(8,128)(2,1)S(1)}, bf16[2,3,128,256]{3,2,1,0:T(8,128)(2,1)}, u32[]{:S(2)}) copy-start(bf16[2,3,128,256]{3,2,1,0:T(8,128)(2,1)} %copy-done.5) | copy-start | bytes 1179652
  35.6 9.0 %copy-start.9 = (bf16[2,2,128,256]{3,2,1,0:T(8,128)(2,1)S(1)}, bf16[2,2,128,256]{3,2,1,0:T(8,128)(2,1)}, u32[]{:S(2)}) copy-start(bf16[2,2,128,256]{3,2,1,0:T(8,128)(2,1)} %get-tuple-element.16.near_ref) | copy-start | bytes 786436
  35.6 9.1 %copy-start.11 = (bf16[2,2,128,256]{3,2,1,0:T(8,128)(2,1)S(1)}, bf16[2,2,128,256]{3,2,1,0:T(8,128)(2,1)}, u32[]{:S(2)}) copy-start(bf16[2,2,128,256]{3,2,1,0:T(8,128)(2,1)} %get-tuple-element.17.cross_ref) | copy-start | bytes 786436
  39.7 14.2 %all-to-all-start.1 = ((bf16[8,2,64,256]{3,2,1,0:T(8,128)(2,1)}), bf16[8,2,64,256]{3,2,1,0:T(8,128)(2,1)}, u32[]{:S(2)}, u32[]{:S(2)}) async-start(bf16[8,2,64,256]{3,2,1,0:T(8,128)(2,1)} %translations.1), calls=%async_computation.1 | async-start | bytes 1048576 | tf_op jit(solution)/shard_map/all_to_all | solution.py:352
  44.7 1.7 %copy-start.2 = (bf16[2,2,2,9,128,128]{5,4,3,2,1,0:T(8,128)(2,1)S(1)}, bf16[2,2,2,9,128,128]{5,4,3,2,1,0:T(8,128)(2,1)}, u32[]{:S(2)}) copy-start(bf16[2,2,2,9,128,128]{5,4,3,2,1,0:T(8,128)(2,1)} %blocks_ref.1) | copy-start | bytes 7077892
  46.3 0.9 %copy-start.13 = (bf16[2,2,128,256]{3,2,1,0:T(8,128)(2,1)S(1)}, bf16[2,2,128,256]{3,2,1,0:T(8,128)(2,1)}, u32[]{:S(2)}) copy-start(bf16[2,2,128,256]{3,2,1,0:T(8,128)(2,1)} %copy-done.12) | copy-start | bytes 786436
  47.3 6.7 %copy-start = (bf16[2,2,2,128,512]{4,3,2,1,0:T(8,128)(2,1)S(1)}, bf16[2,2,2,128,512]{4,3,2,1,0:T(8,128)(2,1)}, u32[]{:S(2)}) copy-start(bf16[2,2,2,128,512]{4,3,2,1,0:T(8,128)(2,1)} %disaggregate_ref.1) | copy-start | bytes 3145732
  47.3 6.7 %copy-start.1 = (s32[2,2]{1,0:T(2,128)S(1)}, s32[2,2]{1,0:T(2,128)}, u32[]{:S(2)}) copy-start(s32[2,2]{1,0:T(2,128)} %live_ref.3) | copy-start | bytes 52

commit v3 on v2

v3 whole, which is shorter than its diff:
```python
import jax
import jax.numpy as jnp
from jax import lax
from jax.experimental import pallas as pl
from jax.experimental.pallas import tpu as pltpu
from jax.sharding import PartitionSpec as P

REACH = 2
MIB = 1 << 20
far_offsets = [
    (row_step, col_step)
    for row_step in range(-REACH, REACH + 1)
    for col_step in range(-REACH, REACH + 1)
    if max(abs(row_step), abs(col_step)) == REACH
]
VMEM = pl.BlockSpec(memory_space=pltpu.VMEM)
SMEM = pl.BlockSpec(memory_space=pltpu.SMEM)
ANY = pl.BlockSpec(memory_space=pl.ANY)


def params(mib=56):
    return pltpu.CompilerParams(vmem_limit_bytes=mib * MIB)


def cost(micros):
    return pl.CostEstimate(flops=int(micros * 1.15e9), bytes_accessed=int(micros * 3.69e6), transcendentals=0)


def swap_pairs(count, first):
    pairs = []
    for i in range(count):
        partner = i + 1 if (i - first) % 2 == 0 else i - 1
        pairs.append((i, partner if 0 <= partner < count else None))
    return pairs


def swap_cols(array, first):
    rows, cols = lax.axis_size("sect"), lax.axis_size("dir")
    sends = []
    for row in range(rows):
        for col, partner in swap_pairs(cols, first):
            to = (row ^ 1) * cols + col if partner is None else row * cols + partner
            sends.append((row * cols + col, to))
    return lax.ppermute(array, ("sect", "dir"), sends)


def swap_rows(array, first):
    rows, cols = lax.axis_size("sect"), lax.axis_size("dir")
    sends = []
    for row, partner in swap_pairs(rows, first):
        for col in range(cols):
            to = row * cols + (col ^ 1) if partner is None else partner * cols + col
            sends.append((row * cols + col, to))
    return lax.ppermute(array, ("sect", "dir"), sends)


def complex_dot(left_real, left_imag, right):
    rows = left_real.shape[0]
    cols = right.shape[1] // 2
    both = jnp.dot(
        jnp.concatenate([left_real, left_imag], axis=0), right, preferred_element_type=jnp.float32
    )
    real = both[:rows, :cols] - both[rows:, cols:]
    imag = both[:rows, cols:] + both[rows:, :cols]
    return real, imag


def pattern_kernel(
    live_ref, unknowns_ref, aggregate_ref, out_ref, near_ref, cross_ref, leaves_ref,
):
    rows, cols, _, narrow, sides = out_ref.shape
    deep, wide, size = unknowns_ref.shape[1:4]

    @pl.when(pl.program_id(0) == 0)
    def _():
        for u in range(deep):
            for v in range(wide):
                keep = live_ref[u, v].astype(jnp.float32).astype(jnp.bfloat16)
                at = (u * wide + v) * size
                for c in range(2):
                    leaves_ref[at : at + size, c * sides : (c + 1) * sides] = (
                        unknowns_ref[c, u, v] * keep
                    )

    left = [
        jnp.concatenate([aggregate_ref[c, u, v] for u in range(deep) for v in range(wide)], axis=1)
        for c in range(2)
    ]
    real, imag = complex_dot(left[0], left[1], leaves_ref[...])
    for row in range(rows):
        for col in range(cols):
            at = (col * rows + row) * narrow
            out_ref[row, col, 0] = real[at : at + narrow].astype(jnp.bfloat16)
            out_ref[row, col, 1] = imag[at : at + narrow].astype(jnp.bfloat16)

    @pl.when(pl.program_id(0) == 0)
    def _():
        odd = lax.rem(lax.axis_index("dir"), 2)

        def leaf(u, v, c):
            at = pl.multiple_of((u * wide + v) * size, size)
            return leaves_ref[pl.ds(at, size), c * sides : (c + 1) * sides]

        for c in range(2):
            for u in range(deep):
                near_ref[c, u] = leaf(u, 1 - odd, c)
                cross_ref[c, u] = leaf(u, odd, c)


def translate_kernel(
    from_ref, coef_ref, out_ref, held_ref, made_ref, coefs_ref, turned_ref, wide_ref, coef_sem, in_sem,
    out_sem,
):
    box_rows, box_cols, _, narrow, sides = from_ref.shape
    lanes = min(128, sides)

    def across(place):
        return pl.ds(pl.multiple_of(place * lanes, lanes), lanes)

    def arrival(place):
        return pltpu.make_async_copy(
            from_ref.at[..., across(place)], held_ref.at[..., across(place)], in_sem.at[place]
        )

    def departure(place):
        return pltpu.make_async_copy(
            made_ref.at[..., across(place)], out_ref.at[..., across(place)], out_sem.at[place]
        )

    coefs_here = pltpu.make_async_copy(coef_ref, coefs_ref, coef_sem)
    coefs_here.start()
    for place in range(sides // lanes):
        arrival(place).start()
    coefs_here.wait()
    turned_ref[...] = coefs_ref[...].T
    first = pl.multiple_of(lax.axis_index("sect") * narrow, narrow)
    coefs = turned_ref[pl.ds(first, narrow)]
    for index in range(coefs.shape[1]):
        wide_ref[index] = jnp.broadcast_to(coefs[:, index : index + 1], (narrow, lanes))

    def tile(place, carry):
        arrival(place).wait()
        for col in range(box_cols):
            totals = {}
            for source in range(box_rows):
                held = {
                    step: [
                        held_ref[source, col + step, c, :, across(place)].astype(jnp.float32)
                        for c in range(2)
                    ]
                    for step in range(-REACH, REACH + 1)
                    if 0 <= col + step < box_cols
                }
                for target in range(max(0, source - REACH), min(box_rows, source + REACH + 1)):
                    real = imag = None
                    for index, (row_step, step) in enumerate(far_offsets):
                        if row_step != source - target or step not in held:
                            continue
                        coef_real, coef_imag = wide_ref[2 * index], wide_ref[2 * index + 1]
                        from_real, from_imag = held[step]
                        term_real = coef_real * from_real - coef_imag * from_imag
                        term_imag = coef_real * from_imag + coef_imag * from_real
                        real = term_real if real is None else real + term_real
                        imag = term_imag if imag is None else imag + term_imag
                    if real is None:
                        continue
                    real = real.astype(jnp.bfloat16).astype(jnp.float32)
                    imag = imag.astype(jnp.bfloat16).astype(jnp.float32)
                    if target in totals:
                        old = totals[target]
                        real, imag = old[0] + real, old[1] + imag
                    totals[target] = (real, imag)
            for target in range(box_rows):
                for c in range(2):
                    made_ref[target, col, c, :, across(place)] = (
                        totals[target][c].astype(jnp.bfloat16)
                        if target in totals
                        else jnp.zeros((narrow, lanes), jnp.bfloat16)
                    )
        departure(place).start()
        return carry

    lax.fori_loop(0, sides // lanes, tile, 0)
    for place in range(sides // lanes):
        departure(place).wait()


def translate_grid(sources, coefs):
    box_rows, box_cols = sources.shape[:2]
    widened = jnp.pad(sources.astype(jnp.float32), ((REACH, REACH), (REACH, REACH), (0, 0), (0, 0), (0, 0)))
    accum = jnp.zeros(sources.shape, jnp.float32)
    for row_step in range(-REACH, REACH + 1):
        total = jnp.zeros(sources.shape, jnp.float32)
        for index, (step_row, step_col) in enumerate(far_offsets):
            if step_row == row_step:
                shifted = widened[
                    REACH + step_row : REACH + step_row + box_rows,
                    REACH + step_col : REACH + step_col + box_cols,
                ]
                coef_real = coefs[index, 0][None, None, :, None]
                coef_imag = coefs[index, 1][None, None, :, None]
                real = coef_real * shifted[:, :, 0] - coef_imag * shifted[:, :, 1]
                imag = coef_real * shifted[:, :, 1] + coef_imag * shifted[:, :, 0]
                total = total + jnp.stack([real, imag], axis=2)
        accum = accum + total.astype(jnp.bfloat16).astype(jnp.float32)
    return accum.astype(jnp.bfloat16)


def move(copies, sem):
    arrivals = [
        pltpu.make_async_copy(source, held, sem.at[0, i]) for i, (source, held, _) in enumerate(copies)
    ]
    departures = [
        pltpu.make_async_copy(held, target, sem.at[1, i]) for i, (_, held, target) in enumerate(copies)
    ]
    for copy in arrivals:
        copy.start()
    for arrival, departure in zip(arrivals, departures):
        arrival.wait()
        departure.start()
    for copy in departures:
        copy.wait()


def row_kernel(
    near_ref, cross_ref, from_cross_ref, from_near_ref, out_near_ref, out_cross_ref, held_ref, sem
):
    odd = lax.rem(lax.axis_index("sect"), 2)
    copies = []
    for slot, ref in enumerate((near_ref, cross_ref, from_cross_ref, from_near_ref)):
        copies.append((ref.at[:, 1 - odd], held_ref.at[0, slot], out_near_ref.at[:, slot]))
        copies.append((ref.at[:, odd], held_ref.at[1, slot], out_cross_ref.at[:, slot]))
    move(copies, sem)


def near_kernel(
    near_ref, cross_ref, from_cross_ref, from_near_ref, row_near_ref, row_cross_ref, blocks_ref,
    out_ref, grid_ref,
):
    sides = near_ref.shape[3]
    deep = near_ref.shape[1]
    wide = 2
    leaf = pl.program_id(0)

    @pl.when(leaf == 0)
    def _():
        col_at, col_count = lax.axis_index("dir"), lax.axis_size("dir")
        row_at, row_count = lax.axis_index("sect"), lax.axis_size("sect")
        col_odd, row_odd = lax.rem(col_at, 2), lax.rem(row_at, 2)
        columns = (2 - col_odd, 1 + col_odd, 3 * col_odd, 3 - 3 * col_odd)
        row_next, row_last = 3 - 3 * row_odd, 3 * row_odd
        no_col = ((col_odd == 0) & (col_at == 0)) | ((col_odd == 1) & (col_at == col_count - 1))
        no_row = ((row_odd == 0) & (row_at == 0)) | ((row_odd == 1) & (row_at == row_count - 1))
        for slot, ref in enumerate((near_ref, cross_ref, from_cross_ref, from_near_ref)):
            for c in range(2):
                half = slice(c * sides, (c + 1) * sides)
                for u in range(deep):
                    grid_ref[1 + u, columns[slot], :, half] = ref[c, u]
                grid_ref[row_next, columns[slot], :, half] = row_near_ref[c, slot]
                grid_ref[row_last, columns[slot], :, half] = row_cross_ref[c, slot]

        @pl.when(no_col)
        def _():
            for i in range(deep + 2):
                grid_ref[i, columns[2]] = jnp.zeros(grid_ref.shape[2:], grid_ref.dtype)

        @pl.when(no_row)
        def _():
            for j in range(wide + 2):
                grid_ref[row_last, j] = jnp.zeros(grid_ref.shape[2:], grid_ref.dtype)

    u, v = leaf // wide, lax.rem(leaf, wide)
    right = jnp.concatenate(
        [grid_ref[u + a, v + b] for a in range(3) for b in range(3)], axis=0
    )
    left = [jnp.concatenate([blocks_ref[c, 0, 0, k] for k in range(9)], axis=1) for c in range(2)]
    real, imag = complex_dot(left[0], left[1], right)
    out_ref[0, 0, 0] = real
    out_ref[1, 0, 0] = imag


def far_kernel(
    live_ref, incoming_ref, disaggregate_ref, near_ref, out_ref, right_ref, made_ref, in_sem, out_sem
):
    rows, cols, _, narrow, sides = incoming_ref.shape
    deep, wide = live_ref.shape

    def arrival(row, c):
        return pltpu.make_async_copy(
            incoming_ref.at[row, :, c],
            right_ref.at[:, row, :, c * sides : (c + 1) * sides],
            in_sem.at[row, c],
        )

    def departure(u, v):
        return pltpu.make_async_copy(
            made_ref.at[:, u, v], out_ref.at[:, u, v], out_sem.at[u, v]
        )

    places = [(row, c) for row in range(rows) for c in range(2)]
    for place in places:
        arrival(*place).start()
    for place in places:
        arrival(*place).wait()
    right = right_ref[...].reshape(cols * rows * narrow, 2 * sides)
    for u in range(deep):
        for v in range(wide):
            live = live_ref[u, v].astype(jnp.float32)
            real, imag = complex_dot(disaggregate_ref[0, u, v], disaggregate_ref[1, u, v], right)
            made_ref[0, u, v] = (near_ref[0, u, v] + real) * live
            made_ref[1, u, v] = (near_ref[1, u, v] + imag) * live
            departure(u, v).start()
    for u in range(deep):
        for v in range(wide):
            departure(u, v).wait()


def shards(unknowns, leaf_live, near_blocks, aggregate, disaggregate, translate):
    sect_count, dir_count = lax.axis_size("sect"), lax.axis_size("dir")
    _, deep, wide, size, sides = unknowns.shape
    total_dirs = aggregate.shape[3]
    narrow = total_dirs // (sect_count * dir_count)
    held = translate.shape[2]
    bf16, f32 = jnp.bfloat16, jnp.float32
    tiled = narrow % 16 == 0
    steps = 2
    rows, cols = (sect_count, dir_count) if tiled else (1, steps)
    block = total_dirs // (rows * cols)

    column = jax.ShapeDtypeStruct((2, deep, size, sides), bf16)
    whole = [pl.BlockSpec(a.shape, lambda i, n=len(a.shape): (0,) * n) for a in (unknowns, column)]
    patterns, col_near, col_cross = pl.pallas_call(
        pattern_kernel,
        grid=(steps,),
        in_specs=[
            SMEM,
            whole[0],
            pl.BlockSpec((2, deep, wide, total_dirs // steps, size), lambda i: (0, 0, 0, i, 0)),
        ],
        out_specs=[
            pl.BlockSpec((rows, cols // steps, 2, block, sides), lambda i: (0, i, 0, 0, 0)),
            whole[1],
            whole[1],
        ],
        out_shape=[jax.ShapeDtypeStruct((rows, cols, 2, block, sides), bf16), column, column],
        scratch_shapes=[pltpu.VMEM((deep * wide * size, 2 * sides), bf16)],
        compiler_params=params(),
        name="patterns",
    )(leaf_live, unknowns, aggregate)
    from_cross = swap_cols(col_cross, 1)
    from_near = swap_cols(col_near, 0)

    row = jax.ShapeDtypeStruct((2, 4, size, sides), bf16)
    row_near, row_cross = pl.pallas_call(
        row_kernel,
        in_specs=[ANY] * 4,
        out_specs=[ANY] * 2,
        out_shape=[row, row],
        scratch_shapes=[
            pltpu.VMEM((2, 4, 2, size, sides), bf16),
            pltpu.SemaphoreType.DMA((2, 8)),
        ],
        compiler_params=params(),
        cost_estimate=cost(4000),
        name="rows",
    )(col_near, col_cross, from_cross, from_near)

    def spread(array):
        flat = array.reshape(rows * cols, 2, block, sides)
        return lax.all_to_all(flat, ("sect", "dir"), split_axis=0, concat_axis=0, tiled=True).reshape(array.shape)

    if tiled:
        own = spread(patterns)
        own, _, _ = lax.optimization_barrier((own, row_near, row_cross))
        lanes = min(128, sides)
        incoming = pl.pallas_call(
            translate_kernel,
            in_specs=[ANY] * 2,
            out_specs=ANY,
            out_shape=jax.ShapeDtypeStruct(own.shape, bf16),
            scratch_shapes=[
                pltpu.VMEM(own.shape, bf16),
                pltpu.VMEM(own.shape, bf16),
                pltpu.VMEM((2 * len(far_offsets), held), f32),
                pltpu.VMEM((held, 2 * len(far_offsets)), f32),
                pltpu.VMEM((2 * len(far_offsets), narrow, lanes), f32),
                pltpu.SemaphoreType.DMA,
                pltpu.SemaphoreType.DMA((sides // lanes,)),
                pltpu.SemaphoreType.DMA((sides // lanes,)),
            ],
            compiler_params=params(16),
            cost_estimate=cost(4000),
            name="translations",
        )(own, translate.reshape(2 * len(far_offsets), held))
        returned = spread(incoming)
    else:
        split = (2, dir_count, sect_count, narrow, sides)
        base = patterns[0].transpose(1, 0, 2, 3).reshape(split).transpose(0, 2, 1, 3, 4)
        base = base.reshape(2, total_dirs, sides)[None, None]
        own = lax.all_to_all(base, "sect", split_axis=3, concat_axis=0, tiled=True)
        own = lax.all_to_all(own, "dir", split_axis=3, concat_axis=1, tiled=True)
        coefs = lax.dynamic_slice_in_dim(translate, lax.axis_index("sect") * narrow, narrow, 2)
        incoming = translate_grid(own, coefs)
        returned = lax.all_to_all(incoming, "sect", split_axis=0, concat_axis=3, tiled=True)
        returned = lax.all_to_all(returned, "dir", split_axis=1, concat_axis=3, tiled=True)[0, 0]
        returned = returned.reshape(2, cols, block, sides).transpose(1, 0, 2, 3)[None]

    row_near = swap_rows(row_near, 0)
    row_cross = swap_rows(row_cross, 1)
    field = jax.ShapeDtypeStruct(unknowns.shape, f32)
    near = pl.pallas_call(
        near_kernel,
        grid=(deep * wide,),
        in_specs=[VMEM] * 6
        + [pl.BlockSpec((2, 1, 1, 9, size, size), lambda i: (0, i // wide, i % wide, 0, 0, 0))],
        out_specs=pl.BlockSpec((2, 1, 1, size, sides), lambda i: (0, i // wide, i % wide, 0, 0)),
        out_shape=field,
        scratch_shapes=[pltpu.VMEM((deep + 2, wide + 2, size, 2 * sides), bf16)],
        compiler_params=params(16),
        cost_estimate=cost(4000),
        name="near",
    )(col_near, col_cross, from_cross, from_near, row_near, row_cross, near_blocks)
    return pl.pallas_call(
        far_kernel,
        in_specs=[SMEM, ANY, VMEM, VMEM],
        out_specs=ANY,
        out_shape=field,
        scratch_shapes=[
            pltpu.VMEM((cols, rows, block, 2 * sides), bf16),
            pltpu.VMEM(unknowns.shape, f32),
            pltpu.SemaphoreType.DMA((rows, 2)),
            pltpu.SemaphoreType.DMA((deep, wide)),
        ],
        compiler_params=params(16),
        name="far",
    )(leaf_live, returned, disaggregate, near)


def solution(mesh):
    in_specs = (
        P(None, "sect", "dir", None, None),
        P("sect", "dir"),
        P(None, "sect", "dir", None, None, None),
        P(None, "sect", "dir", None, None),
        P(None, "sect", "dir", None, None),
        P(None, None, "dir"),
    )
    out_specs = P(None, "sect", "dir", None, None)
    return jax.shard_map(shards, mesh=mesh, in_specs=in_specs, out_specs=out_specs, check_vma=False)
```

time: 57.8 us -> 56 us (0.969)
  starting transfers between devices: 21.7 us -> 15.8 us
  waiting for transfers between devices: 15.6 us -> 21 us
  local copies, waits for them, and re-layouts: 4.68 us -> 3.08 us
    all_to_all x2, waiting for transfers between devices: 6.13 us -> 12.5 us  [spread(): lax.all_to_all(flat, ('sect', 'dir'), split_axis=0, concat_axis=0, tiled=...]
    ppermute x4 -> x2, starting transfers between devices: 6.43 us -> 2.94 us  [swap_cols(): return lax.ppermute(array, ('sect', 'dir'), sends)]
    ppermute x3 -> x2, waiting for transfers between devices: 3.13 us -> 0.01 us  [swap_rows(): return lax.ppermute(array, ('sect', 'dir'), sends)]
    ppermute x4 -> x2, waiting for transfers between devices: 6.34 us -> 8.49 us  [swap_cols(): return lax.ppermute(array, ('sect', 'dir'), sends)]
    ppermute x3 -> x2, starting transfers between devices: 4.16 us -> 2.51 us  [swap_rows(): return lax.ppermute(array, ('sect', 'dir'), sends)]
    unnamed x28 -> x20, local copies, waits for them, and re-layouts: 4.68 us -> 3.08 us
    all_to_all x2, starting transfers between devices: 11.1 us -> 10.4 us  [spread(): lax.all_to_all(flat, ('sect', 'dir'), split_axis=0, concat_axis=0, tiled=...]
    pallas_call x3 -> x2, Pallas kernels: 5.06 us -> 5.29 us  [the longest x1 3.21 us: shards(): pl.pallas_call(translate_kernel, in_specs=[ANY] * 2, out_specs=ANY, out_s...]
  transfers between devices with their start and end apart: 9 -> 6, of which waited for: 4 -> 3; matrix products, arithmetic and copies ran while one was open for 0% -> 0% of each run, Pallas kernels for 15% -> 17%
where the time goes in v3:
time: 56 us; the launch traced here: 55.6 us
  waiting for transfers between devices  21 us (38%)
  starting transfers between devices  15.8 us (28%)
  Pallas kernels  15.5 us (28%)
  local copies, waits for them, and re-layouts  3.08 us (6%)
    all_to_all x2, waiting for transfers between devices, spread(): lax.all_to_all(flat, ('sect', 'dir'), split_axis=0, concat_axis=0, tiled=...  12.5 us
    all_to_all x2, starting transfers between devices, spread(): lax.all_to_all(flat, ('sect', 'dir'), split_axis=0, concat_axis=0, tiled=...  10.4 us
    ppermute x2, waiting for transfers between devices, swap_cols(): return lax.ppermute(array, ('sect', 'dir'), sends)  8.49 us
    pallas_call x1, Pallas kernels, shards(): pl.pallas_call(near_kernel, grid=(deep * wide,), in_specs=[VMEM] * 6 + [p...  3.9 us
    pallas_call x1, Pallas kernels, shards(): pl.pallas_call(far_kernel, in_specs=[SMEM, ANY, VMEM, VMEM], out_specs=AN...  3.26 us
    pallas_call x1, Pallas kernels, shards(): pl.pallas_call(translate_kernel, in_specs=[ANY] * 2, out_specs=ANY, out_s...  3.21 us
    unnamed x20, local copies, waits for them, and re-layouts  3.08 us
    pallas_call x1, Pallas kernels, shards(): pl.pallas_call(pattern_kernel, grid=(steps,), in_specs=[SMEM, whole[0], p...  3.08 us
  transfers between devices with their start and end apart: 6, of which 3 were waited for; matrix products, arithmetic and copies ran while one was open for 0% of the time, Pallas kernels for 17%

profile of v3, /device:TPU:0, one launch (start us, length us, event | category | flops | bytes accessed | tf_op | source)
XLA Modules:
  0.0 55.6 jit_solution(9442840865252201983)
XLA Ops:
  0.0 3.1 %patterns.1 = (bf16[4,8,2,16,256]{4,3,2,1,0:T(8,128)(2,1)}, bf16[2,2,128,256]{3,2,1,0:T(8,128)(2,1)}, bf16[2,2,128,256]{3,2,1,0:T(8,128)(2,1)}) custom-call(s32[2,2]{1,0:T(2,128)} %live_ref.3, bf16[2,2,2,128,256]{4,3,2,1,0:T(8,128)(2,1)} %unknowns_ref.1, bf16[2,2,2,512,128]{4,3,2,1,0:T(8,128)(2,1)} %aggregate_ref.1), custom_call_target="tpu_custom_call" | custom-call | tf_op jit(solution)/shard_map/patterns/pallas_call | solution.py:332
  3.1 2.9 %collective-permute-start.1 = (bf16[2,2,128,256]{3,2,1,0:T(8,128)(2,1)}, bf16[2,2,128,256]{3,2,1,0:T(8,128)(2,1)S(1)}, u32[]{:S(2)}, u32[]{:S(2)}) collective-permute-start(bf16[2,2,128,256]{3,2,1,0:T(8,128)(2,1)} %get-tuple-element.12.near_ref), channel_id=1, source_target_pairs={{0,1},{1,0},{2,3},{3,2},{4,5},{5,4},{6,7},{7,6},{8,9},{9,8},{10,11... | collective-permute-start | bytes 786440 | tf_op jit(solution)/shard_map/ppermute | solution.py:44
  6.0 0.0 collective-permute-start
  6.0 6.5 %all-to-all-start = ((bf16[32,2,16,256]{3,2,1,0:T(8,128)(2,1)}), bf16[32,2,16,256]{3,2,1,0:T(8,128)(2,1)}, u32[]{:S(2)}, u32[]{:S(2)}) async-start(bf16[32,2,16,256]{3,2,1,0:T(8,128)(2,1)} %bitcast.6), calls=%async_computation | async-start | bytes 1048576 | tf_op jit(solution)/shard_map/all_to_all | solution.py:370
  12.5 8.5 %collective-permute-done.1.from_near_ref = bf16[2,2,128,256]{3,2,1,0:T(8,128)(2,1)S(1)} collective-permute-done((bf16[2,2,128,256]{3,2,1,0:T(8,128)(2,1)}, bf16[2,2,128,256]{3,2,1,0:T(8,128)(2,1)S(1)}, u32[]{:S(2)}, u32[]{:S(2)}) %collective-permute-start.1) | collective-permute-done | bytes 262176 | tf_op jit(solution)/shard_map/ppermute | solution.py:44
  21.0 0.0 copy-start.5
  21.0 0.0 collective-permute-done.from_cross_ref
  21.0 0.7 %copy-done.5 = bf16[2,2,128,256]{3,2,1,0:T(8,128)(2,1)} copy-done((bf16[2,2,128,256]{3,2,1,0:T(8,128)(2,1)}, bf16[2,2,128,256]{3,2,1,0:T(8,128)(2,1)S(1)}, u32[]{:S(2)}) %copy-start.5) | copy-done | bytes 262168
  21.7 0.0 copy-start.7
  21.7 0.7 %copy-done.7 = bf16[2,2,128,256]{3,2,1,0:T(8,128)(2,1)} copy-done((bf16[2,2,128,256]{3,2,1,0:T(8,128)(2,1)}, bf16[2,2,128,256]{3,2,1,0:T(8,128)(2,1)S(1)}, u32[]{:S(2)}) %copy-start.7) | copy-done | bytes 262168
  22.4 0.0 copy-start.9
  22.4 2.1 %rows.1 = (bf16[2,4,128,256]{3,2,1,0:T(8,128)(2,1)}, bf16[2,4,128,256]{3,2,1,0:T(8,128)(2,1)}) custom-call(bf16[2,2,128,256]{3,2,1,0:T(8,128)(2,1)} %get-tuple-element.12.near_ref, bf16[2,2,128,256]{3,2,1,0:T(8,128)(2,1)} %get-tuple-element.13.cross_ref, bf16[2,2,128,256]{3,2,1,0:T(8,128)(2,1)} %copy-done.7, bf16[2,2,128,256]{3,2,1,0:T(8,128)(2,1)} %copy-done.5), custom_call_target="tpu_custom_call" | custom-call | flops 4600000151552 | bytes 14759999488 | tf_op jit(solution)/shard_map/rows/pallas_call | solution.py:354
  24.5 0.1 collective-permute-start.2
  24.6 2.4 %collective-permute-start.3 = (bf16[2,4,128,256]{3,2,1,0:T(8,128)(2,1)}, bf16[2,4,128,256]{3,2,1,0:T(8,128)(2,1)}, u32[]{:S(2)}, u32[]{:S(2)}) collective-permute-start(bf16[2,4,128,256]{3,2,1,0:T(8,128)(2,1)} %get-tuple-element.15), channel_id=1, source_target_pairs={{0,1},{1,0},{2,3},{3,2},{4,5},{5,4},{6,7},{7,6},{8,16},{9,17},{10,... | collective-permute-start | bytes 1572872 | tf_op jit(solution)/shard_map/ppermute | solution.py:54
  27.0 1.8 %all-to-all-done = bf16[32,2,16,256]{3,2,1,0:T(8,128)(2,1)} async-done(((bf16[32,2,16,256]{3,2,1,0:T(8,128)(2,1)}), bf16[32,2,16,256]{3,2,1,0:T(8,128)(2,1)}, u32[]{:S(2)}, u32[]{:S(2)}) %all-to-all-start) | async-done | bytes 524320 | tf_op jit(solution)/shard_map/all_to_all | solution.py:370
  28.9 0.0 copy-done.9
  28.9 0.0 copy-start.8
  28.9 3.2 %translations.1 = bf16[4,8,2,16,256]{4,3,2,1,0:T(8,128)(2,1)} custom-call(bf16[4,8,2,16,256]{4,3,2,1,0:T(8,128)(2,1)} %bitcast.1.from_ref, f32[32,64]{1,0:T(8,128)S(1)} %bitcast.5), custom_call_target="tpu_custom_call" | custom-call | flops 4600000151552 | bytes 14759999488 | tf_op jit(solution)/shard_map/translations/pallas_call | solution.py:376
  32.1 3.8 %all-to-all-start.1 = ((bf16[32,2,16,256]{3,2,1,0:T(8,128)(2,1)}), bf16[32,2,16,256]{3,2,1,0:T(8,128)(2,1)}, u32[]{:S(2)}, u32[]{:S(2)}) async-start(bf16[32,2,16,256]{3,2,1,0:T(8,128)(2,1)} %bitcast.3), calls=%async_computation.1 | async-start | bytes 1048576 | tf_op jit(solution)/shard_map/all_to_all | solution.py:370
  36.0 0.0 collective-permute-done.2.row_near_ref
  36.0 0.0 collective-permute-done.3.row_cross_ref
  36.0 0.0 copy-done.3
  36.0 0.0 copy-done.4
  36.0 0.0 copy-done.6
  36.0 0.0 copy-done.8
  36.0 0.0 copy-start.2
  36.0 1.7 %copy-done.2 = bf16[2,2,2,9,128,128]{5,4,3,2,1,0:T(8,128)(2,1)S(1)} copy-done((bf16[2,2,2,9,128,128]{5,4,3,2,1,0:T(8,128)(2,1)S(1)}, bf16[2,2,2,9,128,128]{5,4,3,2,1,0:T(8,128)(2,1)}, u32[]{:S(2)}) %copy-start.2) | copy-done | bytes 2359320
  37.7 3.9 %near.1.near_ref = f32[2,2,2,128,256]{4,3,2,1,0:T(8,128)S(1)} custom-call(bf16[2,2,128,256]{3,2,1,0:T(8,128)(2,1)S(1)} %copy-done.3, bf16[2,2,128,256]{3,2,1,0:T(8,128)(2,1)S(1)} %copy-done.4, bf16[2,2,128,256]{3,2,1,0:T(8,128)(2,1)S(1)} %copy-done.8, bf16[2,2,128,256]{3,2,1,0:T(8,128)(2,1)S(1)} %copy-done.6, ...), custom_call_target="tpu_custom_call" | custom-call | flops 4600000151552 | bytes 14759999488 | tf_op jit(solution)/shard_map/near/pallas_call | solution.py:411
  41.6 10.7 %all-to-all-done.1 = bf16[32,2,16,256]{3,2,1,0:T(8,128)(2,1)} async-done(((bf16[32,2,16,256]{3,2,1,0:T(8,128)(2,1)}), bf16[32,2,16,256]{3,2,1,0:T(8,128)(2,1)}, u32[]{:S(2)}, u32[]{:S(2)}) %all-to-all-start.1) | async-done | bytes 524320 | tf_op jit(solution)/shard_map/all_to_all | solution.py:370
  52.3 0.0 copy-done
  52.3 0.0 copy-done.1
  52.3 3.3 %far.1 = f32[2,2,2,128,256]{4,3,2,1,0:T(8,128)} custom-call(s32[2,2]{1,0:T(2,128)S(1)} %copy-done.1, bf16[4,8,2,16,256]{4,3,2,1,0:T(8,128)(2,1)} %bitcast.4.incoming_ref, bf16[2,2,2,128,512]{4,3,2,1,0:T(8,128)(2,1)S(1)} %copy-done, f32[2,2,2,128,256]{4,3,2,1,0:T(8,128)S(1)} %near.1.near_ref), custom_call_target="tpu_custom_call" | custom-call | tf_op jit(solution)/shard_map/far/pallas_call | solution.py:423
  (5 shorter events, 0.0 us)
Async XLA Ops:
  3.1 17.9 %collective-permute-start.1 = (bf16[2,2,128,256]{3,2,1,0:T(8,128)(2,1)}, bf16[2,2,128,256]{3,2,1,0:T(8,128)(2,1)S(1)}, u32[]{:S(2)}, u32[]{:S(2)}) collective-permute-start(bf16[2,2,128,256]{3,2,1,0:T(8,128)(2,1)} %get-tuple-element.12.near_ref), channel_id=1, source_target_pairs={{0,1},{1,0},{2,3},{3,2},{4,5},{5,4},{6,7},{7,6},{8,9},{9,8},{10,11... | collective-permute-start | bytes 786440 | tf_op jit(solution)/shard_map/ppermute | solution.py:44
  6.0 15.0 %collective-permute-start = (bf16[2,2,128,256]{3,2,1,0:T(8,128)(2,1)}, bf16[2,2,128,256]{3,2,1,0:T(8,128)(2,1)S(1)}, u32[]{:S(2)}, u32[]{:S(2)}) collective-permute-start(bf16[2,2,128,256]{3,2,1,0:T(8,128)(2,1)} %get-tuple-element.13.cross_ref), channel_id=1, source_target_pairs={{0,8},{1,2},{2,1},{3,4},{4,3},{5,6},{6,5},{7,15},{8,0},{9,10},{10,... | collective-permute-start | bytes 786440 | tf_op jit(solution)/shard_map/ppermute | solution.py:44
  6.0 22.8 %all-to-all-start = ((bf16[32,2,16,256]{3,2,1,0:T(8,128)(2,1)}), bf16[32,2,16,256]{3,2,1,0:T(8,128)(2,1)}, u32[]{:S(2)}, u32[]{:S(2)}) async-start(bf16[32,2,16,256]{3,2,1,0:T(8,128)(2,1)} %bitcast.6), calls=%async_computation | async-start | bytes 1048576 | tf_op jit(solution)/shard_map/all_to_all | solution.py:370
  21.0 0.7 %copy-start.5 = (bf16[2,2,128,256]{3,2,1,0:T(8,128)(2,1)}, bf16[2,2,128,256]{3,2,1,0:T(8,128)(2,1)S(1)}, u32[]{:S(2)}) copy-start(bf16[2,2,128,256]{3,2,1,0:T(8,128)(2,1)S(1)} %collective-permute-done.1.from_near_ref) | copy-start | bytes 786436
  21.7 0.7 %copy-start.7 = (bf16[2,2,128,256]{3,2,1,0:T(8,128)(2,1)}, bf16[2,2,128,256]{3,2,1,0:T(8,128)(2,1)S(1)}, u32[]{:S(2)}) copy-start(bf16[2,2,128,256]{3,2,1,0:T(8,128)(2,1)S(1)} %collective-permute-done.from_cross_ref) | copy-start | bytes 786436
  22.4 6.4 %copy-start.9 = (f32[16,2,64]{2,1,0:T(2,128)S(1)}, f32[16,2,64]{2,1,0:T(2,128)}, u32[]{:S(2)}) copy-start(f32[16,2,64]{2,1,0:T(2,128)} %param.11) | copy-start | bytes 24580
  24.5 11.4 %collective-permute-start.2 = (bf16[2,4,128,256]{3,2,1,0:T(8,128)(2,1)}, bf16[2,4,128,256]{3,2,1,0:T(8,128)(2,1)}, u32[]{:S(2)}, u32[]{:S(2)}) collective-permute-start(bf16[2,4,128,256]{3,2,1,0:T(8,128)(2,1)} %get-tuple-element.14), channel_id=1, source_target_pairs={{0,8},{1,9},{2,10},{3,11},{4,12},{5,13},{6,14},{7,15},{8,0},{9,1},... | collective-permute-start | bytes 1572872 | tf_op jit(solution)/shard_map/ppermute | solution.py:54
  24.6 11.4 %collective-permute-start.3 = (bf16[2,4,128,256]{3,2,1,0:T(8,128)(2,1)}, bf16[2,4,128,256]{3,2,1,0:T(8,128)(2,1)}, u32[]{:S(2)}, u32[]{:S(2)}) collective-permute-start(bf16[2,4,128,256]{3,2,1,0:T(8,128)(2,1)} %get-tuple-element.15), channel_id=1, source_target_pairs={{0,1},{1,0},{2,3},{3,2},{4,5},{5,4},{6,7},{7,6},{8,16},{9,17},{10,... | collective-permute-start | bytes 1572872 | tf_op jit(solution)/shard_map/ppermute | solution.py:54
  28.9 7.1 %copy-start.3 = (bf16[2,2,128,256]{3,2,1,0:T(8,128)(2,1)S(1)}, bf16[2,2,128,256]{3,2,1,0:T(8,128)(2,1)}, u32[]{:S(2)}) copy-start(bf16[2,2,128,256]{3,2,1,0:T(8,128)(2,1)} %get-tuple-element.12.near_ref) | copy-start | bytes 786436
  28.9 7.1 %copy-start.4 = (bf16[2,2,128,256]{3,2,1,0:T(8,128)(2,1)S(1)}, bf16[2,2,128,256]{3,2,1,0:T(8,128)(2,1)}, u32[]{:S(2)}) copy-start(bf16[2,2,128,256]{3,2,1,0:T(8,128)(2,1)} %get-tuple-element.13.cross_ref) | copy-start | bytes 786436
  28.9 7.1 %copy-start.6 = (bf16[2,2,128,256]{3,2,1,0:T(8,128)(2,1)S(1)}, bf16[2,2,128,256]{3,2,1,0:T(8,128)(2,1)}, u32[]{:S(2)}) copy-start(bf16[2,2,128,256]{3,2,1,0:T(8,128)(2,1)} %copy-done.5) | copy-start | bytes 786436
  28.9 7.1 %copy-start.8 = (bf16[2,2,128,256]{3,2,1,0:T(8,128)(2,1)S(1)}, bf16[2,2,128,256]{3,2,1,0:T(8,128)(2,1)}, u32[]{:S(2)}) copy-start(bf16[2,2,128,256]{3,2,1,0:T(8,128)(2,1)} %copy-done.7) | copy-start | bytes 786436
  32.1 20.2 %all-to-all-start.1 = ((bf16[32,2,16,256]{3,2,1,0:T(8,128)(2,1)}), bf16[32,2,16,256]{3,2,1,0:T(8,128)(2,1)}, u32[]{:S(2)}, u32[]{:S(2)}) async-start(bf16[32,2,16,256]{3,2,1,0:T(8,128)(2,1)} %bitcast.3), calls=%async_computation.1 | async-start | bytes 1048576 | tf_op jit(solution)/shard_map/all_to_all | solution.py:370
  36.0 1.7 %copy-start.2 = (bf16[2,2,2,9,128,128]{5,4,3,2,1,0:T(8,128)(2,1)S(1)}, bf16[2,2,2,9,128,128]{5,4,3,2,1,0:T(8,128)(2,1)}, u32[]{:S(2)}) copy-start(bf16[2,2,2,9,128,128]{5,4,3,2,1,0:T(8,128)(2,1)} %blocks_ref.1) | copy-start | bytes 7077892
  37.7 14.6 %copy-start = (bf16[2,2,2,128,512]{4,3,2,1,0:T(8,128)(2,1)S(1)}, bf16[2,2,2,128,512]{4,3,2,1,0:T(8,128)(2,1)}, u32[]{:S(2)}) copy-start(bf16[2,2,2,128,512]{4,3,2,1,0:T(8,128)(2,1)} %disaggregate_ref.1) | copy-start | bytes 3145732
  37.7 14.6 %copy-start.1 = (s32[2,2]{1,0:T(2,128)S(1)}, s32[2,2]{1,0:T(2,128)}, u32[]{:S(2)}) copy-start(s32[2,2]{1,0:T(2,128)} %live_ref.3) | copy-start | bytes 52

commit v4 on v3

--- a/solution.py
+++ b/solution.py
@@ -14,7 +14,6 @@
     if max(abs(row_step), abs(col_step)) == REACH
 ]
 VMEM = pl.BlockSpec(memory_space=pltpu.VMEM)
-SMEM = pl.BlockSpec(memory_space=pltpu.SMEM)
 ANY = pl.BlockSpec(memory_space=pl.ANY)
 
 
@@ -44,12 +43,12 @@
     return lax.ppermute(array, ("sect", "dir"), sends)
 
 
-def swap_rows(array, first):
+def swap_rows(array, first, turn=0):
     rows, cols = lax.axis_size("sect"), lax.axis_size("dir")
     sends = []
     for row, partner in swap_pairs(rows, first):
         for col in range(cols):
-            to = row * cols + (col ^ 1) if partner is None else partner * cols + col
+            to = row * cols + (col ^ 1) if partner is None else partner * cols + (col ^ turn)
             sends.append((row * cols + col, to))
     return lax.ppermute(array, ("sect", "dir"), sends)
 
@@ -66,7 +65,8 @@
 
 
 def pattern_kernel(
-    live_ref, unknowns_ref, aggregate_ref, out_ref, near_ref, cross_ref, leaves_ref,
+    live_ref, unknowns_ref, aggregate_ref, out_ref, near_ref, cross_ref, corner_near_ref,
+    corner_cross_ref, leaves_ref,
 ):
     rows, cols, _, narrow, sides = out_ref.shape
     deep, wide, size = unknowns_ref.shape[1:4]
@@ -96,6 +96,7 @@
     @pl.when(pl.program_id(0) == 0)
     def _():
         odd = lax.rem(lax.axis_index("dir"), 2)
+        row_odd = lax.rem(lax.axis_index("sect"), 2)
 
         def leaf(u, v, c):
             at = pl.multiple_of((u * wide + v) * size, size)
@@ -105,6 +106,8 @@
             for u in range(deep):
                 near_ref[c, u] = leaf(u, 1 - odd, c)
                 cross_ref[c, u] = leaf(u, odd, c)
+            corner_near_ref[c] = leaf(1 - row_odd, 1 - odd, c)
+            corner_cross_ref[c] = leaf(row_odd, 1 - odd, c)
 
 
 def translate_kernel(
@@ -222,20 +225,18 @@
         copy.wait()
 
 
-def row_kernel(
-    near_ref, cross_ref, from_cross_ref, from_near_ref, out_near_ref, out_cross_ref, held_ref, sem
-):
+def row_kernel(near_ref, cross_ref, from_cross_ref, out_near_ref, out_cross_ref, held_ref, sem):
     odd = lax.rem(lax.axis_index("sect"), 2)
     copies = []
-    for slot, ref in enumerate((near_ref, cross_ref, from_cross_ref, from_near_ref)):
+    for slot, ref in enumerate((near_ref, cross_ref, from_cross_ref)):
         copies.append((ref.at[:, 1 - odd], held_ref.at[0, slot], out_near_ref.at[:, slot]))
         copies.append((ref.at[:, odd], held_ref.at[1, slot], out_cross_ref.at[:, slot]))
     move(copies, sem)
 
 
 def near_kernel(
-    near_ref, cross_ref, from_cross_ref, from_near_ref, row_near_ref, row_cross_ref, blocks_ref,
-    out_ref, grid_ref,
+    near_ref, cross_ref, from_cross_ref, from_near_ref, row_near_ref, row_cross_ref, corner_near_ref,
+    corner_cross_ref, blocks_ref, out_ref, grid_ref,
 ):
     sides = near_ref.shape[3]
     deep = near_ref.shape[1]
@@ -256,8 +257,12 @@
                 half = slice(c * sides, (c + 1) * sides)
                 for u in range(deep):
                     grid_ref[1 + u, columns[slot], :, half] = ref[c, u]
-                grid_ref[row_next, columns[slot], :, half] = row_near_ref[c, slot]
-                grid_ref[row_last, columns[slot], :, half] = row_cross_ref[c, slot]
+                if slot < 3:
+                    grid_ref[row_next, columns[slot], :, half] = row_near_ref[c, slot]
+                    grid_ref[row_last, columns[slot], :, half] = row_cross_ref[c, slot]
+                else:
+                    grid_ref[row_next, columns[slot], :, half] = corner_near_ref[c]
+                    grid_ref[row_last, columns[slot], :, half] = corner_cross_ref[c]
 
         @pl.when(no_col)
         def _():
@@ -280,7 +285,8 @@
 
 
 def far_kernel(
-    live_ref, incoming_ref, disaggregate_ref, near_ref, out_ref, right_ref, made_ref, in_sem, out_sem
+    live_ref, incoming_ref, disaggregate_ref, near_ref, out_ref, live_here, right_ref, made_ref, live_sem,
+    in_sem, out_sem,
 ):
     rows, cols, _, narrow, sides = incoming_ref.shape
     deep, wide = live_ref.shape
@@ -298,14 +304,17 @@
         )
 
     places = [(row, c) for row in range(rows) for c in range(2)]
+    live_copy = pltpu.make_async_copy(live_ref, live_here, live_sem)
+    live_copy.start()
     for place in places:
         arrival(*place).start()
+    live_copy.wait()
     for place in places:
         arrival(*place).wait()
     right = right_ref[...].reshape(cols * rows * narrow, 2 * sides)
     for u in range(deep):
         for v in range(wide):
-            live = live_ref[u, v].astype(jnp.float32)
+            live = live_here[u : u + 1, v : v + 1].astype(jnp.float32)
             real, imag = complex_dot(disaggregate_ref[0, u, v], disaggregate_ref[1, u, v], right)
             made_ref[0, u, v] = (near_ref[0, u, v] + real) * live
             made_ref[1, u, v] = (near_ref[1, u, v] + imag) * live
@@ -323,17 +332,21 @@
     held = translate.shape[2]
     bf16, f32 = jnp.bfloat16, jnp.float32
     tiled = narrow % 16 == 0
-    steps = 2
+    steps = 1
     rows, cols = (sect_count, dir_count) if tiled else (1, steps)
     block = total_dirs // (rows * cols)
 
     column = jax.ShapeDtypeStruct((2, deep, size, sides), bf16)
-    whole = [pl.BlockSpec(a.shape, lambda i, n=len(a.shape): (0,) * n) for a in (unknowns, column)]
-    patterns, col_near, col_cross = pl.pallas_call(
+    corner = jax.ShapeDtypeStruct((2, size, sides), bf16)
+    blocks = jax.ShapeDtypeStruct((rows, cols, 2, block, sides), bf16)
+    whole = [
+        pl.BlockSpec(a.shape, lambda i, n=len(a.shape): (0,) * n) for a in (unknowns, column, corner)
+    ]
+    patterns, col_near, col_cross, corner_near, corner_cross = pl.pallas_call(
         pattern_kernel,
         grid=(steps,),
         in_specs=[
-            SMEM,
+            pl.BlockSpec(memory_space=pltpu.SMEM),
             whole[0],
             pl.BlockSpec((2, deep, wide, total_dirs // steps, size), lambda i: (0, 0, 0, i, 0)),
         ],
@@ -341,29 +354,33 @@
             pl.BlockSpec((rows, cols // steps, 2, block, sides), lambda i: (0, i, 0, 0, 0)),
             whole[1],
             whole[1],
+            whole[2],
+            whole[2],
         ],
-        out_shape=[jax.ShapeDtypeStruct((rows, cols, 2, block, sides), bf16), column, column],
+        out_shape=[blocks, column, column, corner, corner],
         scratch_shapes=[pltpu.VMEM((deep * wide * size, 2 * sides), bf16)],
         compiler_params=params(),
         name="patterns",
     )(leaf_live, unknowns, aggregate)
     from_cross = swap_cols(col_cross, 1)
     from_near = swap_cols(col_near, 0)
-
-    row = jax.ShapeDtypeStruct((2, 4, size, sides), bf16)
+    corner_near = swap_rows(corner_near, 0, 1)
+    corner_cross = swap_rows(corner_cross, 1, 1)
+
+    row = jax.ShapeDtypeStruct((2, 3, size, sides), bf16)
     row_near, row_cross = pl.pallas_call(
         row_kernel,
-        in_specs=[ANY] * 4,
+        in_specs=[ANY] * 3,
         out_specs=[ANY] * 2,
         out_shape=[row, row],
         scratch_shapes=[
-            pltpu.VMEM((2, 4, 2, size, sides), bf16),
-            pltpu.SemaphoreType.DMA((2, 8)),
+            pltpu.VMEM((2, 3, 2, size, sides), bf16),
+            pltpu.SemaphoreType.DMA((2, 6)),
         ],
         compiler_params=params(),
         cost_estimate=cost(4000),
         name="rows",
-    )(col_near, col_cross, from_cross, from_near)
+    )(col_near, col_cross, from_cross)
 
     def spread(array):
         flat = array.reshape(rows * cols, 2, block, sides)
@@ -389,7 +406,7 @@
                 pltpu.SemaphoreType.DMA((sides // lanes,)),
             ],
             compiler_params=params(16),
-            cost_estimate=cost(4000),
+            cost_estimate=cost(8),
             name="translations",
         )(own, translate.reshape(2 * len(far_offsets), held))
         returned = spread(incoming)
@@ -411,7 +428,7 @@
     near = pl.pallas_call(
         near_kernel,
         grid=(deep * wide,),
-        in_specs=[VMEM] * 6
+        in_specs=[VMEM] * 8
         + [pl.BlockSpec((2, 1, 1, 9, size, size), lambda i: (0, i // wide, i % wide, 0, 0, 0))],
         out_specs=pl.BlockSpec((2, 1, 1, size, sides), lambda i: (0, i // wide, i % wide, 0, 0)),
         out_shape=field,
@@ -419,15 +436,20 @@
         compiler_params=params(16),
         cost_estimate=cost(4000),
         name="near",
-    )(col_near, col_cross, from_cross, from_near, row_near, row_cross, near_blocks)
+    )(
+        col_near, col_cross, from_cross, from_near, row_near, row_cross, corner_near, corner_cross,
+        near_blocks,
+    )
     return pl.pallas_call(
         far_kernel,
-        in_specs=[SMEM, ANY, VMEM, VMEM],
+        in_specs=[ANY, ANY, VMEM, VMEM],
         out_specs=ANY,
         out_shape=field,
         scratch_shapes=[
+            pltpu.VMEM(leaf_live.shape, jnp.int32),
             pltpu.VMEM((cols, rows, block, 2 * sides), bf16),
             pltpu.VMEM(unknowns.shape, f32),
+            pltpu.SemaphoreType.DMA,
             pltpu.SemaphoreType.DMA((rows, 2)),
             pltpu.SemaphoreType.DMA((deep, wide)),
         ],

time: 56 us -> 53.3 us (0.952)
  waiting for transfers between devices: 21 us -> 18.6 us
  Pallas kernels: 15.5 us -> 14.6 us
    ppermute x2, waiting for transfers between devices: 8.49 us -> 0.01 us  [swap_cols(): return lax.ppermute(array, ('sect', 'dir'), sends)]
    all_to_all x2, waiting for transfers between devices: 12.5 us -> 17.7 us  [spread(): lax.all_to_all(flat, ('sect', 'dir'), split_axis=0, concat_axis=0, tiled=...]
    ppermute x2 -> x4, waiting for transfers between devices: 0.01 us -> 0.89 us  [swap_rows(): return lax.ppermute(array, ('sect', 'dir'), sends)]
    pallas_call x4, Pallas kernels: 12.3 us -> 11.5 us  [the longest x1 3.77 us: shards(): pl.pallas_call(near_kernel, grid=(deep * wide,), in_specs=[VMEM] * 8 + [p...]
    ppermute x2, starting transfers between devices: 2.94 us -> 2.12 us  [swap_cols(): return lax.ppermute(array, ('sect', 'dir'), sends)]
    ppermute x2 -> x4, starting transfers between devices: 2.51 us -> 3.24 us  [swap_rows(): return lax.ppermute(array, ('sect', 'dir'), sends)]
    unnamed x20 -> x16, local copies, waits for them, and re-layouts: 3.08 us -> 3.33 us
  transfers between devices with their start and end apart: 6 -> 8, of which waited for: 3 -> 3; matrix products, arithmetic and copies ran while one was open for 0% -> 0% of each run, Pallas kernels for 17% -> 17%
where the time goes in v4:
time: 53.3 us; the launch traced here: 52.9 us
  waiting for transfers between devices  18.6 us (35%)
  starting transfers between devices  16.2 us (30%)
  Pallas kernels  14.6 us (27%)
  local copies, waits for them, and re-layouts  3.33 us (6%)
    all_to_all x2, waiting for transfers between devices, spread(): lax.all_to_all(flat, ('sect', 'dir'), split_axis=0, concat_axis=0, tiled=...  17.7 us
    all_to_all x2, starting transfers between devices, spread(): lax.all_to_all(flat, ('sect', 'dir'), split_axis=0, concat_axis=0, tiled=...  10.9 us
    pallas_call x1, Pallas kernels, shards(): pl.pallas_call(near_kernel, grid=(deep * wide,), in_specs=[VMEM] * 8 + [p...  3.77 us
    unnamed x16, local copies, waits for them, and re-layouts  3.33 us
    ppermute x4, starting transfers between devices, swap_rows(): return lax.ppermute(array, ('sect', 'dir'), sends)  3.24 us
    pallas_call x1, Pallas kernels, shards(): pl.pallas_call(translate_kernel, in_specs=[ANY] * 2, out_specs=ANY, out_s...  3.17 us
    pallas_call x1, Pallas kernels, shards(): pl.pallas_call(pattern_kernel, grid=(steps,), in_specs=[pl.BlockSpec(memo...  2.94 us
    pallas_call x1, Pallas kernels, shards(): pl.pallas_call(far_kernel, in_specs=[ANY, ANY, VMEM, VMEM], out_specs=ANY...  2.75 us
  transfers between devices with their start and end apart: 8, of which 3 were waited for; matrix products, arithmetic and copies ran while one was open for 0% of the time, Pallas kernels for 17%

profile of v4, /device:TPU:0, one launch (start us, length us, event | category | flops | bytes accessed | tf_op | source)
XLA Modules:
  0.0 52.9 jit_solution(13040111776366690919)
XLA Ops:
  0.0 2.9 %patterns.1 = (bf16[4,8,2,16,256]{4,3,2,1,0:T(8,128)(2,1)}, bf16[2,2,128,256]{3,2,1,0:T(8,128)(2,1)}, bf16[2,2,128,256]{3,2,1,0:T(8,128)(2,1)}, bf16[2,128,256]{2,1,0:T(8,128)(2,1)}, bf16[2,128,256]{2,1,0:T(8,128)(2,1)}) custom-call(s32[2,2]{1,0:T(2,128)} %live_ref.3, bf16[2,2,2,128,256]{4,3,2,1,0:T(8,128)(2,1)} %unknowns_ref.1, ...), custom_call_target="tpu_custom_call" | custom-call | tf_op jit(solution)/shard_map/patterns/pallas_call | solution.py:345
  2.9 0.5 collective-permute-start
  3.4 7.5 %all-to-all-start = ((bf16[32,2,16,256]{3,2,1,0:T(8,128)(2,1)}), bf16[32,2,16,256]{3,2,1,0:T(8,128)(2,1)}, u32[]{:S(2)}, u32[]{:S(2)}) async-start(bf16[32,2,16,256]{3,2,1,0:T(8,128)(2,1)} %bitcast.6), calls=%async_computation | async-start | bytes 1048576 | tf_op jit(solution)/shard_map/all_to_all | solution.py:387
  10.9 1.5 %collective-permute-start.4 = (bf16[2,128,256]{2,1,0:T(8,128)(2,1)}, bf16[2,128,256]{2,1,0:T(8,128)(2,1)}, u32[]{:S(2)}, u32[]{:S(2)}) collective-permute-start(bf16[2,128,256]{2,1,0:T(8,128)(2,1)} %get-tuple-element.19), channel_id=1, source_target_pairs={{0,9},{1,8},{2,11},{3,10},{4,13},{5,12},{6,15},{7,14},{8,1},{9,0},... | collective-permute-start | bytes 393224 | tf_op jit(solution)/shard_map/ppermute | solution.py:53
  12.4 0.4 collective-permute-start.5
  12.8 1.7 %collective-permute-start.1 = (bf16[2,2,128,256]{3,2,1,0:T(8,128)(2,1)}, bf16[2,2,128,256]{3,2,1,0:T(8,128)(2,1)}, u32[]{:S(2)}, u32[]{:S(2)}) collective-permute-start(bf16[2,2,128,256]{3,2,1,0:T(8,128)(2,1)} %get-tuple-element.14.near_ref), channel_id=1, source_target_pairs={{0,1},{1,0},{2,3},{3,2},{4,5},{5,4},{6,7},{7,6},{8,9},{9,8},{10,11... | collective-permute-start | bytes 786440 | tf_op jit(solution)/shard_map/ppermute | solution.py:43
  14.5 0.0 collective-permute-done.from_cross_ref
  14.5 0.0 copy-start.5
  14.5 0.7 %copy-done.5 = bf16[2,2,128,256]{3,2,1,0:T(8,128)(2,1)} copy-done((bf16[2,2,128,256]{3,2,1,0:T(8,128)(2,1)}, bf16[2,2,128,256]{3,2,1,0:T(8,128)(2,1)S(1)}, u32[]{:S(2)}) %copy-start.5) | copy-done | bytes 262168
  15.2 0.0 copy-start.7
  15.2 2.0 %rows.1 = (bf16[2,3,128,256]{3,2,1,0:T(8,128)(2,1)}, bf16[2,3,128,256]{3,2,1,0:T(8,128)(2,1)}) custom-call(bf16[2,2,128,256]{3,2,1,0:T(8,128)(2,1)} %get-tuple-element.14.near_ref, bf16[2,2,128,256]{3,2,1,0:T(8,128)(2,1)} %get-tuple-element.15.cross_ref, bf16[2,2,128,256]{3,2,1,0:T(8,128)(2,1)} %copy-done.5), custom_call_target="tpu_custom_call" | custom-call | flops 4600000151552 | bytes 14759999488 | tf_op jit(solution)/shard_map/rows/pallas_call | solution.py:371
  17.2 0.8 %collective-permute-start.2 = (bf16[2,3,128,256]{3,2,1,0:T(8,128)(2,1)}, bf16[2,3,128,256]{3,2,1,0:T(8,128)(2,1)S(1)}, u32[]{:S(2)}, u32[]{:S(2)}) collective-permute-start(bf16[2,3,128,256]{3,2,1,0:T(8,128)(2,1)} %get-tuple-element.16), channel_id=1, source_target_pairs={{0,8},{1,9},{2,10},{3,11},{4,12},{5,13},{6,14},{7,15},{8,0},{9,1},... | collective-permute-start | bytes 1179656 | tf_op jit(solution)/shard_map/ppermute | solution.py:53
  18.0 0.6 %collective-permute-start.3 = (bf16[2,3,128,256]{3,2,1,0:T(8,128)(2,1)}, bf16[2,3,128,256]{3,2,1,0:T(8,128)(2,1)S(1)}, u32[]{:S(2)}, u32[]{:S(2)}) collective-permute-start(bf16[2,3,128,256]{3,2,1,0:T(8,128)(2,1)} %get-tuple-element.17), channel_id=1, source_target_pairs={{0,1},{1,0},{2,3},{3,2},{4,5},{5,4},{6,7},{7,6},{8,16},{9,17},{10,... | collective-permute-start | bytes 1179656 | tf_op jit(solution)/shard_map/ppermute | solution.py:53
  18.5 8.7 %all-to-all-done = bf16[32,2,16,256]{3,2,1,0:T(8,128)(2,1)} async-done(((bf16[32,2,16,256]{3,2,1,0:T(8,128)(2,1)}), bf16[32,2,16,256]{3,2,1,0:T(8,128)(2,1)}, u32[]{:S(2)}, u32[]{:S(2)}) %all-to-all-start) | async-done | bytes 524320 | tf_op jit(solution)/shard_map/all_to_all | solution.py:387
  27.2 0.0 copy-done.7
  27.2 0.0 copy-start.3
  27.3 3.2 %translations.1 = bf16[4,8,2,16,256]{4,3,2,1,0:T(8,128)(2,1)} custom-call(bf16[4,8,2,16,256]{4,3,2,1,0:T(8,128)(2,1)} %bitcast.1.from_ref, f32[32,64]{1,0:T(8,128)S(1)} %bitcast.5), custom_call_target="tpu_custom_call" | custom-call | flops 9200000000 | bytes 29520000 | tf_op jit(solution)/shard_map/translations/pallas_call | solution.py:393
  30.4 3.4 %all-to-all-start.1 = ((bf16[32,2,16,256]{3,2,1,0:T(8,128)(2,1)}), bf16[32,2,16,256]{3,2,1,0:T(8,128)(2,1)}, u32[]{:S(2)}, u32[]{:S(2)}) async-start(bf16[32,2,16,256]{3,2,1,0:T(8,128)(2,1)} %bitcast.3), calls=%async_computation.1 | async-start | bytes 1048576 | tf_op jit(solution)/shard_map/all_to_all | solution.py:387
  33.8 0.0 collective-permute-done.4.corner_near_ref
  33.8 0.0 collective-permute-done.5.corner_cross_ref
  33.8 0.0 collective-permute-done.1.from_near_ref
  33.8 0.0 collective-permute-done.2.row_near_ref
  33.8 0.9 %collective-permute-done.3.row_cross_ref = bf16[2,3,128,256]{3,2,1,0:T(8,128)(2,1)S(1)} collective-permute-done((bf16[2,3,128,256]{3,2,1,0:T(8,128)(2,1)}, bf16[2,3,128,256]{3,2,1,0:T(8,128)(2,1)S(1)}, u32[]{:S(2)}, u32[]{:S(2)}) %collective-permute-start.3) | collective-permute-done | bytes 393248 | tf_op jit(solution)/shard_map/ppermute | solution.py:53
  34.7 0.0 copy-done.3
  34.7 0.0 copy-done.4
  34.7 1.7 %copy-done.2 = bf16[2,2,2,9,128,128]{5,4,3,2,1,0:T(8,128)(2,1)S(1)} copy-done((bf16[2,2,2,9,128,128]{5,4,3,2,1,0:T(8,128)(2,1)S(1)}, bf16[2,2,2,9,128,128]{5,4,3,2,1,0:T(8,128)(2,1)}, u32[]{:S(2)}) %copy-start.2) | copy-done | bytes 2359320
  36.4 0.9 %copy-done.6 = bf16[2,2,128,256]{3,2,1,0:T(8,128)(2,1)S(1)} copy-done((bf16[2,2,128,256]{3,2,1,0:T(8,128)(2,1)S(1)}, bf16[2,2,128,256]{3,2,1,0:T(8,128)(2,1)}, u32[]{:S(2)}) %copy-start.6) | copy-done | bytes 262168
  37.3 3.8 %near.1.near_ref = f32[2,2,2,128,256]{4,3,2,1,0:T(8,128)S(1)} custom-call(bf16[2,2,128,256]{3,2,1,0:T(8,128)(2,1)S(1)} %copy-done.3, bf16[2,2,128,256]{3,2,1,0:T(8,128)(2,1)S(1)} %copy-done.4, bf16[2,2,128,256]{3,2,1,0:T(8,128)(2,1)S(1)} %copy-done.6, bf16[2,2,128,256]{3,2,1,0:T(8,128)(2,1)} %collective-permute-done.1.from_near_ref, ...), custom_call_target="tpu_custom_call" | custom-call | flops 4600000151552 | bytes 14759999488 | tf_op jit(solution)/shard_map/near/pallas_call | solution.py:428
  41.1 9.0 %all-to-all-done.1 = bf16[32,2,16,256]{3,2,1,0:T(8,128)(2,1)} async-done(((bf16[32,2,16,256]{3,2,1,0:T(8,128)(2,1)}), bf16[32,2,16,256]{3,2,1,0:T(8,128)(2,1)}, u32[]{:S(2)}, u32[]{:S(2)}) %all-to-all-start.1) | async-done | bytes 524320 | tf_op jit(solution)/shard_map/all_to_all | solution.py:387
  50.1 0.0 copy-done
  50.1 0.0 copy-done.1
  50.1 2.7 %far.1 = f32[2,2,2,128,256]{4,3,2,1,0:T(8,128)} custom-call(s32[2,2]{1,0:T(2,128)S(1)} %copy-done.1, bf16[4,8,2,16,256]{4,3,2,1,0:T(8,128)(2,1)} %bitcast.4.incoming_ref, bf16[2,2,2,128,512]{4,3,2,1,0:T(8,128)(2,1)S(1)} %copy-done, f32[2,2,2,128,256]{4,3,2,1,0:T(8,128)S(1)} %near.1.near_ref), custom_call_target="tpu_custom_call" | custom-call | tf_op jit(solution)/shard_map/far/pallas_call | solution.py:443
  (5 shorter events, 0.0 us)
Async XLA Ops:
  2.9 11.5 %collective-permute-start = (bf16[2,2,128,256]{3,2,1,0:T(8,128)(2,1)}, bf16[2,2,128,256]{3,2,1,0:T(8,128)(2,1)S(1)}, u32[]{:S(2)}, u32[]{:S(2)}) collective-permute-start(bf16[2,2,128,256]{3,2,1,0:T(8,128)(2,1)} %get-tuple-element.15.cross_ref), channel_id=1, source_target_pairs={{0,8},{1,2},{2,1},{3,4},{4,3},{5,6},{6,5},{7,15},{8,0},{9,10},{10,... | collective-permute-start | bytes 786440 | tf_op jit(solution)/shard_map/ppermute | solution.py:43
  3.4 23.8 %all-to-all-start = ((bf16[32,2,16,256]{3,2,1,0:T(8,128)(2,1)}), bf16[32,2,16,256]{3,2,1,0:T(8,128)(2,1)}, u32[]{:S(2)}, u32[]{:S(2)}) async-start(bf16[32,2,16,256]{3,2,1,0:T(8,128)(2,1)} %bitcast.6), calls=%async_computation | async-start | bytes 1048576 | tf_op jit(solution)/shard_map/all_to_all | solution.py:387
  10.9 22.9 %collective-permute-start.4 = (bf16[2,128,256]{2,1,0:T(8,128)(2,1)}, bf16[2,128,256]{2,1,0:T(8,128)(2,1)}, u32[]{:S(2)}, u32[]{:S(2)}) collective-permute-start(bf16[2,128,256]{2,1,0:T(8,128)(2,1)} %get-tuple-element.19), channel_id=1, source_target_pairs={{0,9},{1,8},{2,11},{3,10},{4,13},{5,12},{6,15},{7,14},{8,1},{9,0},... | collective-permute-start | bytes 393224 | tf_op jit(solution)/shard_map/ppermute | solution.py:53
  12.4 21.4 %collective-permute-start.5 = (bf16[2,128,256]{2,1,0:T(8,128)(2,1)}, bf16[2,128,256]{2,1,0:T(8,128)(2,1)}, u32[]{:S(2)}, u32[]{:S(2)}) collective-permute-start(bf16[2,128,256]{2,1,0:T(8,128)(2,1)} %get-tuple-element.20), channel_id=1, source_target_pairs={{0,1},{1,0},{2,3},{3,2},{4,5},{5,4},{6,7},{7,6},{8,17},{9,16},{10,... | collective-permute-start | bytes 393224 | tf_op jit(solution)/shard_map/ppermute | solution.py:53
  12.8 21.0 %collective-permute-start.1 = (bf16[2,2,128,256]{3,2,1,0:T(8,128)(2,1)}, bf16[2,2,128,256]{3,2,1,0:T(8,128)(2,1)}, u32[]{:S(2)}, u32[]{:S(2)}) collective-permute-start(bf16[2,2,128,256]{3,2,1,0:T(8,128)(2,1)} %get-tuple-element.14.near_ref), channel_id=1, source_target_pairs={{0,1},{1,0},{2,3},{3,2},{4,5},{5,4},{6,7},{7,6},{8,9},{9,8},{10,11... | collective-permute-start | bytes 786440 | tf_op jit(solution)/shard_map/ppermute | solution.py:43
  14.5 0.7 %copy-start.5 = (bf16[2,2,128,256]{3,2,1,0:T(8,128)(2,1)}, bf16[2,2,128,256]{3,2,1,0:T(8,128)(2,1)S(1)}, u32[]{:S(2)}) copy-start(bf16[2,2,128,256]{3,2,1,0:T(8,128)(2,1)S(1)} %collective-permute-done.from_cross_ref) | copy-start | bytes 786436
  15.2 12.1 %copy-start.7 = (f32[16,2,64]{2,1,0:T(2,128)S(1)}, f32[16,2,64]{2,1,0:T(2,128)}, u32[]{:S(2)}) copy-start(f32[16,2,64]{2,1,0:T(2,128)} %param.11) | copy-start | bytes 24580
  17.2 16.7 %collective-permute-start.2 = (bf16[2,3,128,256]{3,2,1,0:T(8,128)(2,1)}, bf16[2,3,128,256]{3,2,1,0:T(8,128)(2,1)S(1)}, u32[]{:S(2)}, u32[]{:S(2)}) collective-permute-start(bf16[2,3,128,256]{3,2,1,0:T(8,128)(2,1)} %get-tuple-element.16), channel_id=1, source_target_pairs={{0,8},{1,9},{2,10},{3,11},{4,12},{5,13},{6,14},{7,15},{8,0},{9,1},... | collective-permute-start | bytes 1179656 | tf_op jit(solution)/shard_map/ppermute | solution.py:53
  18.0 16.8 %collective-permute-start.3 = (bf16[2,3,128,256]{3,2,1,0:T(8,128)(2,1)}, bf16[2,3,128,256]{3,2,1,0:T(8,128)(2,1)S(1)}, u32[]{:S(2)}, u32[]{:S(2)}) collective-permute-start(bf16[2,3,128,256]{3,2,1,0:T(8,128)(2,1)} %get-tuple-element.17), channel_id=1, source_target_pairs={{0,1},{1,0},{2,3},{3,2},{4,5},{5,4},{6,7},{7,6},{8,16},{9,17},{10,... | collective-permute-start | bytes 1179656 | tf_op jit(solution)/shard_map/ppermute | solution.py:53
  27.2 7.5 %copy-start.3 = (bf16[2,2,128,256]{3,2,1,0:T(8,128)(2,1)S(1)}, bf16[2,2,128,256]{3,2,1,0:T(8,128)(2,1)}, u32[]{:S(2)}) copy-start(bf16[2,2,128,256]{3,2,1,0:T(8,128)(2,1)} %get-tuple-element.14.near_ref) | copy-start | bytes 786436
  27.3 7.5 %copy-start.4 = (bf16[2,2,128,256]{3,2,1,0:T(8,128)(2,1)S(1)}, bf16[2,2,128,256]{3,2,1,0:T(8,128)(2,1)}, u32[]{:S(2)}) copy-start(bf16[2,2,128,256]{3,2,1,0:T(8,128)(2,1)} %get-tuple-element.15.cross_ref) | copy-start | bytes 786436
  30.4 19.7 %all-to-all-start.1 = ((bf16[32,2,16,256]{3,2,1,0:T(8,128)(2,1)}), bf16[32,2,16,256]{3,2,1,0:T(8,128)(2,1)}, u32[]{:S(2)}, u32[]{:S(2)}) async-start(bf16[32,2,16,256]{3,2,1,0:T(8,128)(2,1)} %bitcast.3), calls=%async_computation.1 | async-start | bytes 1048576 | tf_op jit(solution)/shard_map/all_to_all | solution.py:387
  34.7 1.7 %copy-start.2 = (bf16[2,2,2,9,128,128]{5,4,3,2,1,0:T(8,128)(2,1)S(1)}, bf16[2,2,2,9,128,128]{5,4,3,2,1,0:T(8,128)(2,1)}, u32[]{:S(2)}) copy-start(bf16[2,2,2,9,128,128]{5,4,3,2,1,0:T(8,128)(2,1)} %blocks_ref.1) | copy-start | bytes 7077892
  36.4 0.9 %copy-start.6 = (bf16[2,2,128,256]{3,2,1,0:T(8,128)(2,1)S(1)}, bf16[2,2,128,256]{3,2,1,0:T(8,128)(2,1)}, u32[]{:S(2)}) copy-start(bf16[2,2,128,256]{3,2,1,0:T(8,128)(2,1)} %copy-done.5) | copy-start | bytes 786436
  37.3 12.8 %copy-start = (bf16[2,2,2,128,512]{4,3,2,1,0:T(8,128)(2,1)S(1)}, bf16[2,2,2,128,512]{4,3,2,1,0:T(8,128)(2,1)}, u32[]{:S(2)}) copy-start(bf16[2,2,2,128,512]{4,3,2,1,0:T(8,128)(2,1)} %disaggregate_ref.1) | copy-start | bytes 3145732
  37.3 12.8 %copy-start.1 = (s32[2,2]{1,0:T(2,128)S(1)}, s32[2,2]{1,0:T(2,128)}, u32[]{:S(2)}) copy-start(s32[2,2]{1,0:T(2,128)} %live_ref.3) | copy-start | bytes 52

commit v5 on v4

--- a/solution.py
+++ b/solution.py
@@ -110,45 +110,26 @@
             corner_cross_ref[c] = leaf(row_odd, 1 - odd, c)
 
 
-def translate_kernel(
-    from_ref, coef_ref, out_ref, held_ref, made_ref, coefs_ref, turned_ref, wide_ref, coef_sem, in_sem,
-    out_sem,
-):
+def translate_kernel(from_ref, coef_ref, out_ref, turned_ref, wide_ref):
     box_rows, box_cols, _, narrow, sides = from_ref.shape
     lanes = min(128, sides)
 
     def across(place):
         return pl.ds(pl.multiple_of(place * lanes, lanes), lanes)
 
-    def arrival(place):
-        return pltpu.make_async_copy(
-            from_ref.at[..., across(place)], held_ref.at[..., across(place)], in_sem.at[place]
-        )
-
-    def departure(place):
-        return pltpu.make_async_copy(
-            made_ref.at[..., across(place)], out_ref.at[..., across(place)], out_sem.at[place]
-        )
-
-    coefs_here = pltpu.make_async_copy(coef_ref, coefs_ref, coef_sem)
-    coefs_here.start()
-    for place in range(sides // lanes):
-        arrival(place).start()
-    coefs_here.wait()
-    turned_ref[...] = coefs_ref[...].T
+    turned_ref[...] = coef_ref[...].T
     first = pl.multiple_of(lax.axis_index("sect") * narrow, narrow)
     coefs = turned_ref[pl.ds(first, narrow)]
     for index in range(coefs.shape[1]):
         wide_ref[index] = jnp.broadcast_to(coefs[:, index : index + 1], (narrow, lanes))
 
     def tile(place, carry):
-        arrival(place).wait()
         for col in range(box_cols):
             totals = {}
             for source in range(box_rows):
                 held = {
                     step: [
-                        held_ref[source, col + step, c, :, across(place)].astype(jnp.float32)
+                        from_ref[source, col + step, c, :, across(place)].astype(jnp.float32)
                         for c in range(2)
                     ]
                     for step in range(-REACH, REACH + 1)
@@ -175,17 +156,14 @@
                     totals[target] = (real, imag)
             for target in range(box_rows):
                 for c in range(2):
-                    made_ref[target, col, c, :, across(place)] = (
+                    out_ref[target, col, c, :, across(place)] = (
                         totals[target][c].astype(jnp.bfloat16)
                         if target in totals
                         else jnp.zeros((narrow, lanes), jnp.bfloat16)
                     )
-        departure(place).start()
         return carry
 
     lax.fori_loop(0, sides // lanes, tile, 0)
-    for place in range(sides // lanes):
-        departure(place).wait()
 
 
 def translate_grid(sources, coefs):
@@ -378,7 +356,7 @@
             pltpu.SemaphoreType.DMA((2, 6)),
         ],
         compiler_params=params(),
-        cost_estimate=cost(4000),
+        cost_estimate=cost(8),
         name="rows",
     )(col_near, col_cross, from_cross)
 
@@ -392,18 +370,12 @@
         lanes = min(128, sides)
         incoming = pl.pallas_call(
             translate_kernel,
-            in_specs=[ANY] * 2,
-            out_specs=ANY,
+            in_specs=[VMEM] * 2,
+            out_specs=VMEM,
             out_shape=jax.ShapeDtypeStruct(own.shape, bf16),
             scratch_shapes=[
-                pltpu.VMEM(own.shape, bf16),
-                pltpu.VMEM(own.shape, bf16),
-                pltpu.VMEM((2 * len(far_offsets), held), f32),
                 pltpu.VMEM((held, 2 * len(far_offsets)), f32),
                 pltpu.VMEM((2 * len(far_offsets), narrow, lanes), f32),
-                pltpu.SemaphoreType.DMA,
-                pltpu.SemaphoreType.DMA((sides // lanes,)),
-                pltpu.SemaphoreType.DMA((sides // lanes,)),
             ],
             compiler_params=params(16),
             cost_estimate=cost(8),
@@ -434,7 +406,7 @@
         out_shape=field,
         scratch_shapes=[pltpu.VMEM((deep + 2, wide + 2, size, 2 * sides), bf16)],
         compiler_params=params(16),
-        cost_estimate=cost(4000),
+        cost_estimate=cost(12),
         name="near",
     )(
         col_near, col_cross, from_cross, from_near, row_near, row_cross, corner_near, corner_cross,

time: 53.3 us -> 50.9 us (0.955)
  local copies, waits for them, and re-layouts: 3.33 us -> 8.41 us
  waiting for transfers between devices: 18.6 us -> 14.6 us
  Pallas kernels: 14.6 us -> 11.8 us
  starting transfers between devices: 16.2 us -> 15.4 us
    unnamed x16 -> x24, local copies, waits for them, and re-layouts: 3.33 us -> 8.41 us
    all_to_all x2, waiting for transfers between devices: 17.7 us -> 13.6 us  [spread(): lax.all_to_all(flat, ('sect', 'dir'), split_axis=0, concat_axis=0, tiled=...]
    pallas_call x1, Pallas kernels: 3.77 us -> 2.66 us  [shards(): pl.pallas_call(near_kernel, grid=(deep * wide,), in_specs=[VMEM] * 8 + [p...]
    pallas_call x1, Pallas kernels: 2.75 us -> 1.74 us  [shards(): pl.pallas_call(far_kernel, in_specs=[ANY, ANY, VMEM, VMEM], out_specs=ANY...]
    all_to_all x2, starting transfers between devices: 10.9 us -> 9.98 us  [spread(): lax.all_to_all(flat, ('sect', 'dir'), split_axis=0, concat_axis=0, tiled=...]
    pallas_call x1, Pallas kernels: 3.17 us -> 2.53 us  [shards(): pl.pallas_call(translate_kernel, in_specs=[VMEM] * 2, out_specs=VMEM, out...]
  transfers between devices with their start and end apart: 8 -> 8, of which waited for: 3 -> 3; matrix products, arithmetic and copies ran while one was open for 0% -> 0% of each run, Pallas kernels for 17% -> 14%
where the time goes in v5:
time: 50.9 us; the launch traced here: 50.4 us
  starting transfers between devices  15.4 us (30%)
  waiting for transfers between devices  14.6 us (29%)
  Pallas kernels  11.8 us (23%)
  local copies, waits for them, and re-layouts  8.41 us (17%)
    all_to_all x2, waiting for transfers between devices, spread(): lax.all_to_all(flat, ('sect', 'dir'), split_axis=0, concat_axis=0, tiled=...  13.6 us
    all_to_all x2, starting transfers between devices, spread(): lax.all_to_all(flat, ('sect', 'dir'), split_axis=0, concat_axis=0, tiled=...  9.98 us
    unnamed x24, local copies, waits for them, and re-layouts  8.41 us
    ppermute x4, starting transfers between devices, swap_rows(): return lax.ppermute(array, ('sect', 'dir'), sends)  3.31 us
    pallas_call x1, Pallas kernels, shards(): pl.pallas_call(pattern_kernel, grid=(steps,), in_specs=[pl.BlockSpec(memo...  2.94 us
    pallas_call x1, Pallas kernels, shards(): pl.pallas_call(near_kernel, grid=(deep * wide,), in_specs=[VMEM] * 8 + [p...  2.66 us
    pallas_call x1, Pallas kernels, shards(): pl.pallas_call(translate_kernel, in_specs=[VMEM] * 2, out_specs=VMEM, out...  2.53 us
    ppermute x2, starting transfers between devices, swap_cols(): return lax.ppermute(array, ('sect', 'dir'), sends)  2.12 us
  transfers between devices with their start and end apart: 8, of which 3 were waited for; matrix products, arithmetic and copies ran while one was open for 0% of the time, Pallas kernels for 14%

profile of v5, /device:TPU:0, one launch (start us, length us, event | category | flops | bytes accessed | tf_op | source)
XLA Modules:
  0.0 50.4 jit_solution(13487176913796316148)
XLA Ops:
  0.0 2.9 %patterns.1 = (bf16[4,8,2,16,256]{4,3,2,1,0:T(8,128)(2,1)}, bf16[2,2,128,256]{3,2,1,0:T(8,128)(2,1)}, bf16[2,2,128,256]{3,2,1,0:T(8,128)(2,1)}, bf16[2,128,256]{2,1,0:T(8,128)(2,1)}, bf16[2,128,256]{2,1,0:T(8,128)(2,1)}) custom-call(s32[2,2]{1,0:T(2,128)} %live_ref.3, bf16[2,2,2,128,256]{4,3,2,1,0:T(8,128)(2,1)} %unknowns_ref.1, ...), custom_call_target="tpu_custom_call" | custom-call | tf_op jit(solution)/shard_map/patterns/pallas_call | solution.py:323
  2.9 0.5 collective-permute-start
  3.4 7.4 %all-to-all-start = ((bf16[32,2,16,256]{3,2,1,0:T(8,128)(2,1)}), bf16[32,2,16,256]{3,2,1,0:T(8,128)(2,1)S(1)}, u32[]{:S(2)}, u32[]{:S(2)}) async-start(bf16[32,2,16,256]{3,2,1,0:T(8,128)(2,1)} %bitcast.8), calls=%async_computation | async-start | bytes 1048576 | tf_op jit(solution)/shard_map/all_to_all | solution.py:365
  10.8 1.6 %collective-permute-start.4 = (bf16[2,128,256]{2,1,0:T(8,128)(2,1)}, bf16[2,128,256]{2,1,0:T(8,128)(2,1)S(1)}, u32[]{:S(2)}, u32[]{:S(2)}) collective-permute-start(bf16[2,128,256]{2,1,0:T(8,128)(2,1)} %get-tuple-element.19), channel_id=1, source_target_pairs={{0,9},{1,8},{2,11},{3,10},{4,13},{5,12},{6,15},{7,14},{8,1},{9,0},... | collective-permute-start | bytes 393224 | tf_op jit(solution)/shard_map/ppermute | solution.py:53
  12.4 0.4 collective-permute-start.5
  12.7 1.7 %collective-permute-start.1 = (bf16[2,2,128,256]{3,2,1,0:T(8,128)(2,1)}, bf16[2,2,128,256]{3,2,1,0:T(8,128)(2,1)S(1)}, u32[]{:S(2)}, u32[]{:S(2)}) collective-permute-start(bf16[2,2,128,256]{3,2,1,0:T(8,128)(2,1)} %get-tuple-element.14.near_ref), channel_id=1, source_target_pairs={{0,1},{1,0},{2,3},{3,2},{4,5},{5,4},{6,7},{7,6},{8,9},{9,8},{10,11... | collective-permute-start | bytes 786440 | tf_op jit(solution)/shard_map/ppermute | solution.py:43
  14.4 0.0 collective-permute-done.from_cross_ref
  14.4 0.7 %copy-done.5 = bf16[2,2,128,256]{3,2,1,0:T(8,128)(2,1)} copy-done((bf16[2,2,128,256]{3,2,1,0:T(8,128)(2,1)}, bf16[2,2,128,256]{3,2,1,0:T(8,128)(2,1)S(1)}, u32[]{:S(2)}) %copy-start.5) | copy-done | bytes 262168
  15.1 2.0 %rows.1 = (bf16[2,3,128,256]{3,2,1,0:T(8,128)(2,1)}, bf16[2,3,128,256]{3,2,1,0:T(8,128)(2,1)}) custom-call(bf16[2,2,128,256]{3,2,1,0:T(8,128)(2,1)} %get-tuple-element.14.near_ref, bf16[2,2,128,256]{3,2,1,0:T(8,128)(2,1)} %get-tuple-element.15.cross_ref, bf16[2,2,128,256]{3,2,1,0:T(8,128)(2,1)} %copy-done.5), custom_call_target="tpu_custom_call" | custom-call | flops 9200000000 | bytes 29520000 | tf_op jit(solution)/shard_map/rows/pallas_call | solution.py:349
  17.1 0.8 %collective-permute-start.2 = (bf16[2,3,128,256]{3,2,1,0:T(8,128)(2,1)}, bf16[2,3,128,256]{3,2,1,0:T(8,128)(2,1)S(1)}, u32[]{:S(2)}, u32[]{:S(2)}) collective-permute-start(bf16[2,3,128,256]{3,2,1,0:T(8,128)(2,1)} %get-tuple-element.16), channel_id=1, source_target_pairs={{0,8},{1,9},{2,10},{3,11},{4,12},{5,13},{6,14},{7,15},{8,0},{9,1},... | collective-permute-start | bytes 1179656 | tf_op jit(solution)/shard_map/ppermute | solution.py:53
  17.9 0.6 %collective-permute-start.3 = (bf16[2,3,128,256]{3,2,1,0:T(8,128)(2,1)}, bf16[2,3,128,256]{3,2,1,0:T(8,128)(2,1)S(1)}, u32[]{:S(2)}, u32[]{:S(2)}) collective-permute-start(bf16[2,3,128,256]{3,2,1,0:T(8,128)(2,1)} %get-tuple-element.17), channel_id=1, source_target_pairs={{0,1},{1,0},{2,3},{3,2},{4,5},{5,4},{6,7},{7,6},{8,16},{9,17},{10,... | collective-permute-start | bytes 1179656 | tf_op jit(solution)/shard_map/ppermute | solution.py:53
  18.4 8.7 %all-to-all-done = bf16[32,2,16,256]{3,2,1,0:T(8,128)(2,1)S(1)} async-done(((bf16[32,2,16,256]{3,2,1,0:T(8,128)(2,1)}), bf16[32,2,16,256]{3,2,1,0:T(8,128)(2,1)S(1)}, u32[]{:S(2)}, u32[]{:S(2)}) %all-to-all-start) | async-done | bytes 524320 | tf_op jit(solution)/shard_map/all_to_all | solution.py:365
  27.1 2.5 %translations.1 = bf16[4,8,2,16,256]{4,3,2,1,0:T(8,128)(2,1)} custom-call(bf16[4,8,2,16,256]{4,3,2,1,0:T(8,128)(2,1)S(1)} %bitcast.6, f32[32,64]{1,0:T(8,128)S(1)} %bitcast.7), custom_call_target="tpu_custom_call" | custom-call | flops 9200000000 | bytes 29520000 | tf_op jit(solution)/shard_map/translations/pallas_call | solution.py:371
  29.7 2.6 %all-to-all-start.1 = ((bf16[32,2,16,256]{3,2,1,0:T(8,128)(2,1)}), bf16[32,2,16,256]{3,2,1,0:T(8,128)(2,1)S(1)}, u32[]{:S(2)}, u32[]{:S(2)}) async-start(bf16[32,2,16,256]{3,2,1,0:T(8,128)(2,1)} %bitcast.3), calls=%async_computation.1 | async-start | bytes 1048576 | tf_op jit(solution)/shard_map/all_to_all | solution.py:365
  32.3 0.0 copy-start
  32.3 0.0 copy-start.1
  32.3 0.0 collective-permute-done.4.corner_near_ref
  32.3 0.0 collective-permute-done.5.corner_cross_ref
  32.3 0.6 %copy-done.9 = bf16[2,128,256]{2,1,0:T(8,128)(2,1)} copy-done((bf16[2,128,256]{2,1,0:T(8,128)(2,1)}, bf16[2,128,256]{2,1,0:T(8,128)(2,1)S(1)}, u32[]{:S(2)}) %copy-start.9) | copy-done | bytes 131096
  33.0 0.0 collective-permute-done.1.from_near_ref
  33.0 0.7 %copy-done.7 = bf16[2,2,128,256]{3,2,1,0:T(8,128)(2,1)} copy-done((bf16[2,2,128,256]{3,2,1,0:T(8,128)(2,1)}, bf16[2,2,128,256]{3,2,1,0:T(8,128)(2,1)S(1)}, u32[]{:S(2)}) %copy-start.7) | copy-done | bytes 262168
  33.7 0.0 collective-permute-done.2.row_near_ref
  33.7 1.0 %collective-permute-done.3.row_cross_ref = bf16[2,3,128,256]{3,2,1,0:T(8,128)(2,1)S(1)} collective-permute-done((bf16[2,3,128,256]{3,2,1,0:T(8,128)(2,1)}, bf16[2,3,128,256]{3,2,1,0:T(8,128)(2,1)S(1)}, u32[]{:S(2)}, u32[]{:S(2)}) %collective-permute-start.3) | collective-permute-done | bytes 393248 | tf_op jit(solution)/shard_map/ppermute | solution.py:53
  34.7 1.7 %copy-done.2 = bf16[2,2,2,9,128,128]{5,4,3,2,1,0:T(8,128)(2,1)S(1)} copy-done((bf16[2,2,2,9,128,128]{5,4,3,2,1,0:T(8,128)(2,1)S(1)}, bf16[2,2,2,9,128,128]{5,4,3,2,1,0:T(8,128)(2,1)}, u32[]{:S(2)}) %copy-start.2) | copy-done | bytes 2359320
  36.4 0.9 %copy-done.3 = bf16[2,2,128,256]{3,2,1,0:T(8,128)(2,1)S(1)} copy-done((bf16[2,2,128,256]{3,2,1,0:T(8,128)(2,1)S(1)}, bf16[2,2,128,256]{3,2,1,0:T(8,128)(2,1)}, u32[]{:S(2)}) %copy-start.3) | copy-done | bytes 262168
  37.3 0.9 %copy-done.4 = bf16[2,2,128,256]{3,2,1,0:T(8,128)(2,1)S(1)} copy-done((bf16[2,2,128,256]{3,2,1,0:T(8,128)(2,1)S(1)}, bf16[2,2,128,256]{3,2,1,0:T(8,128)(2,1)}, u32[]{:S(2)}) %copy-start.4) | copy-done | bytes 262168
  38.3 0.9 %copy-done.6 = bf16[2,2,128,256]{3,2,1,0:T(8,128)(2,1)S(1)} copy-done((bf16[2,2,128,256]{3,2,1,0:T(8,128)(2,1)S(1)}, bf16[2,2,128,256]{3,2,1,0:T(8,128)(2,1)}, u32[]{:S(2)}) %copy-start.6) | copy-done | bytes 262168
  39.2 0.9 %copy-done.8 = bf16[2,2,128,256]{3,2,1,0:T(8,128)(2,1)S(1)} copy-done((bf16[2,2,128,256]{3,2,1,0:T(8,128)(2,1)S(1)}, bf16[2,2,128,256]{3,2,1,0:T(8,128)(2,1)}, u32[]{:S(2)}) %copy-start.8) | copy-done | bytes 262168
  40.2 0.9 %copy-done.10 = bf16[2,128,256]{2,1,0:T(8,128)(2,1)S(1)} copy-done((bf16[2,128,256]{2,1,0:T(8,128)(2,1)S(1)}, bf16[2,128,256]{2,1,0:T(8,128)(2,1)}, u32[]{:S(2)}) %copy-start.10) | copy-done | bytes 131096
  41.1 2.7 %near.1.near_ref = f32[2,2,2,128,256]{4,3,2,1,0:T(8,128)S(1)} custom-call(bf16[2,2,128,256]{3,2,1,0:T(8,128)(2,1)S(1)} %copy-done.3, bf16[2,2,128,256]{3,2,1,0:T(8,128)(2,1)S(1)} %copy-done.4, bf16[2,2,128,256]{3,2,1,0:T(8,128)(2,1)S(1)} %copy-done.6, bf16[2,2,128,256]{3,2,1,0:T(8,128)(2,1)S(1)} %copy-done.8, ...), custom_call_target="tpu_custom_call" | custom-call | flops 13799999488 | bytes 44280000 | tf_op jit(solution)/shard_map/near/pallas_call | solution.py:400
  43.8 4.9 %all-to-all-done.1 = bf16[32,2,16,256]{3,2,1,0:T(8,128)(2,1)S(1)} async-done(((bf16[32,2,16,256]{3,2,1,0:T(8,128)(2,1)}), bf16[32,2,16,256]{3,2,1,0:T(8,128)(2,1)S(1)}, u32[]{:S(2)}, u32[]{:S(2)}) %all-to-all-start.1) | async-done | bytes 524320 | tf_op jit(solution)/shard_map/all_to_all | solution.py:365
  48.6 1.7 %far.1 = f32[2,2,2,128,256]{4,3,2,1,0:T(8,128)} custom-call(s32[2,2]{1,0:T(2,128)S(1)} %copy-done.1, bf16[4,8,2,16,256]{4,3,2,1,0:T(8,128)(2,1)S(1)} %bitcast.5, bf16[2,2,2,128,512]{4,3,2,1,0:T(8,128)(2,1)S(1)} %copy-done, f32[2,2,2,128,256]{4,3,2,1,0:T(8,128)S(1)} %near.1.near_ref), custom_call_target="tpu_custom_call" | custom-call | tf_op jit(solution)/shard_map/far/pallas_call | solution.py:415
  (13 shorter events, 0.0 us)
Async XLA Ops:
  2.9 11.5 %collective-permute-start = (bf16[2,2,128,256]{3,2,1,0:T(8,128)(2,1)}, bf16[2,2,128,256]{3,2,1,0:T(8,128)(2,1)S(1)}, u32[]{:S(2)}, u32[]{:S(2)}) collective-permute-start(bf16[2,2,128,256]{3,2,1,0:T(8,128)(2,1)} %get-tuple-element.15.cross_ref), channel_id=1, source_target_pairs={{0,8},{1,2},{2,1},{3,4},{4,3},{5,6},{6,5},{7,15},{8,0},{9,10},{10,... | collective-permute-start | bytes 786440 | tf_op jit(solution)/shard_map/ppermute | solution.py:43
  3.4 23.7 %all-to-all-start = ((bf16[32,2,16,256]{3,2,1,0:T(8,128)(2,1)}), bf16[32,2,16,256]{3,2,1,0:T(8,128)(2,1)S(1)}, u32[]{:S(2)}, u32[]{:S(2)}) async-start(bf16[32,2,16,256]{3,2,1,0:T(8,128)(2,1)} %bitcast.8), calls=%async_computation | async-start | bytes 1048576 | tf_op jit(solution)/shard_map/all_to_all | solution.py:365
  10.8 21.5 %collective-permute-start.4 = (bf16[2,128,256]{2,1,0:T(8,128)(2,1)}, bf16[2,128,256]{2,1,0:T(8,128)(2,1)S(1)}, u32[]{:S(2)}, u32[]{:S(2)}) collective-permute-start(bf16[2,128,256]{2,1,0:T(8,128)(2,1)} %get-tuple-element.19), channel_id=1, source_target_pairs={{0,9},{1,8},{2,11},{3,10},{4,13},{5,12},{6,15},{7,14},{8,1},{9,0},... | collective-permute-start | bytes 393224 | tf_op jit(solution)/shard_map/ppermute | solution.py:53
  12.4 20.0 %collective-permute-start.5 = (bf16[2,128,256]{2,1,0:T(8,128)(2,1)}, bf16[2,128,256]{2,1,0:T(8,128)(2,1)S(1)}, u32[]{:S(2)}, u32[]{:S(2)}) collective-permute-start(bf16[2,128,256]{2,1,0:T(8,128)(2,1)} %get-tuple-element.20), channel_id=1, source_target_pairs={{0,1},{1,0},{2,3},{3,2},{4,5},{5,4},{6,7},{7,6},{8,17},{9,16},{10,... | collective-permute-start | bytes 393224 | tf_op jit(solution)/shard_map/ppermute | solution.py:53
  12.7 14.4 %copy-start.11 = (f32[16,2,64]{2,1,0:T(2,128)S(1)}, f32[16,2,64]{2,1,0:T(2,128)}, u32[]{:S(2)}) copy-start(f32[16,2,64]{2,1,0:T(2,128)} %param.11) | copy-start | bytes 24580
  12.7 20.2 %collective-permute-start.1 = (bf16[2,2,128,256]{3,2,1,0:T(8,128)(2,1)}, bf16[2,2,128,256]{3,2,1,0:T(8,128)(2,1)S(1)}, u32[]{:S(2)}, u32[]{:S(2)}) collective-permute-start(bf16[2,2,128,256]{3,2,1,0:T(8,128)(2,1)} %get-tuple-element.14.near_ref), channel_id=1, source_target_pairs={{0,1},{1,0},{2,3},{3,2},{4,5},{5,4},{6,7},{7,6},{8,9},{9,8},{10,11... | collective-permute-start | bytes 786440 | tf_op jit(solution)/shard_map/ppermute | solution.py:43
  14.4 0.7 %copy-start.5 = (bf16[2,2,128,256]{3,2,1,0:T(8,128)(2,1)}, bf16[2,2,128,256]{3,2,1,0:T(8,128)(2,1)S(1)}, u32[]{:S(2)}) copy-start(bf16[2,2,128,256]{3,2,1,0:T(8,128)(2,1)S(1)} %collective-permute-done.from_cross_ref) | copy-start | bytes 786436
  17.1 16.6 %collective-permute-start.2 = (bf16[2,3,128,256]{3,2,1,0:T(8,128)(2,1)}, bf16[2,3,128,256]{3,2,1,0:T(8,128)(2,1)S(1)}, u32[]{:S(2)}, u32[]{:S(2)}) collective-permute-start(bf16[2,3,128,256]{3,2,1,0:T(8,128)(2,1)} %get-tuple-element.16), channel_id=1, source_target_pairs={{0,8},{1,9},{2,10},{3,11},{4,12},{5,13},{6,14},{7,15},{8,0},{9,1},... | collective-permute-start | bytes 1179656 | tf_op jit(solution)/shard_map/ppermute | solution.py:53
  17.9 16.9 %collective-permute-start.3 = (bf16[2,3,128,256]{3,2,1,0:T(8,128)(2,1)}, bf16[2,3,128,256]{3,2,1,0:T(8,128)(2,1)S(1)}, u32[]{:S(2)}, u32[]{:S(2)}) collective-permute-start(bf16[2,3,128,256]{3,2,1,0:T(8,128)(2,1)} %get-tuple-element.17), channel_id=1, source_target_pairs={{0,1},{1,0},{2,3},{3,2},{4,5},{5,4},{6,7},{7,6},{8,16},{9,17},{10,... | collective-permute-start | bytes 1179656 | tf_op jit(solution)/shard_map/ppermute | solution.py:53
  29.7 19.0 %all-to-all-start.1 = ((bf16[32,2,16,256]{3,2,1,0:T(8,128)(2,1)}), bf16[32,2,16,256]{3,2,1,0:T(8,128)(2,1)S(1)}, u32[]{:S(2)}, u32[]{:S(2)}) async-start(bf16[32,2,16,256]{3,2,1,0:T(8,128)(2,1)} %bitcast.3), calls=%async_computation.1 | async-start | bytes 1048576 | tf_op jit(solution)/shard_map/all_to_all | solution.py:365
  32.3 16.4 %copy-start = (bf16[2,2,2,128,512]{4,3,2,1,0:T(8,128)(2,1)S(1)}, bf16[2,2,2,128,512]{4,3,2,1,0:T(8,128)(2,1)}, u32[]{:S(2)}) copy-start(bf16[2,2,2,128,512]{4,3,2,1,0:T(8,128)(2,1)} %disaggregate_ref.1) | copy-start | bytes 3145732
  32.3 16.3 %copy-start.1 = (s32[2,2]{1,0:T(2,128)S(1)}, s32[2,2]{1,0:T(2,128)}, u32[]{:S(2)}) copy-start(s32[2,2]{1,0:T(2,128)} %live_ref.3) | copy-start | bytes 52
  32.3 0.6 %copy-start.9 = (bf16[2,128,256]{2,1,0:T(8,128)(2,1)}, bf16[2,128,256]{2,1,0:T(8,128)(2,1)S(1)}, u32[]{:S(2)}) copy-start(bf16[2,128,256]{2,1,0:T(8,128)(2,1)S(1)} %collective-permute-done.5.corner_cross_ref) | copy-start | bytes 393220
  33.0 0.7 %copy-start.7 = (bf16[2,2,128,256]{3,2,1,0:T(8,128)(2,1)}, bf16[2,2,128,256]{3,2,1,0:T(8,128)(2,1)S(1)}, u32[]{:S(2)}) copy-start(bf16[2,2,128,256]{3,2,1,0:T(8,128)(2,1)S(1)} %collective-permute-done.1.from_near_ref) | copy-start | bytes 786436
  34.7 1.7 %copy-start.2 = (bf16[2,2,2,9,128,128]{5,4,3,2,1,0:T(8,128)(2,1)S(1)}, bf16[2,2,2,9,128,128]{5,4,3,2,1,0:T(8,128)(2,1)}, u32[]{:S(2)}) copy-start(bf16[2,2,2,9,128,128]{5,4,3,2,1,0:T(8,128)(2,1)} %blocks_ref.1) | copy-start | bytes 7077892
  36.4 0.9 %copy-start.3 = (bf16[2,2,128,256]{3,2,1,0:T(8,128)(2,1)S(1)}, bf16[2,2,128,256]{3,2,1,0:T(8,128)(2,1)}, u32[]{:S(2)}) copy-start(bf16[2,2,128,256]{3,2,1,0:T(8,128)(2,1)} %get-tuple-element.14.near_ref) | copy-start | bytes 786436
  37.3 0.9 %copy-start.4 = (bf16[2,2,128,256]{3,2,1,0:T(8,128)(2,1)S(1)}, bf16[2,2,128,256]{3,2,1,0:T(8,128)(2,1)}, u32[]{:S(2)}) copy-start(bf16[2,2,128,256]{3,2,1,0:T(8,128)(2,1)} %get-tuple-element.15.cross_ref) | copy-start | bytes 786436
  38.3 0.9 %copy-start.6 = (bf16[2,2,128,256]{3,2,1,0:T(8,128)(2,1)S(1)}, bf16[2,2,128,256]{3,2,1,0:T(8,128)(2,1)}, u32[]{:S(2)}) copy-start(bf16[2,2,128,256]{3,2,1,0:T(8,128)(2,1)} %copy-done.5) | copy-start | bytes 786436
  39.2 0.9 %copy-start.8 = (bf16[2,2,128,256]{3,2,1,0:T(8,128)(2,1)S(1)}, bf16[2,2,128,256]{3,2,1,0:T(8,128)(2,1)}, u32[]{:S(2)}) copy-start(bf16[2,2,128,256]{3,2,1,0:T(8,128)(2,1)} %copy-done.7) | copy-start | bytes 786436
  40.2 0.9 %copy-start.10 = (bf16[2,128,256]{2,1,0:T(8,128)(2,1)S(1)}, bf16[2,128,256]{2,1,0:T(8,128)(2,1)}, u32[]{:S(2)}) copy-start(bf16[2,128,256]{2,1,0:T(8,128)(2,1)} %copy-done.9) | copy-start | bytes 393220

commit v6 on v5

--- a/solution.py
+++ b/solution.py
@@ -110,60 +110,52 @@
             corner_cross_ref[c] = leaf(row_odd, 1 - odd, c)
 
 
-def translate_kernel(from_ref, coef_ref, out_ref, turned_ref, wide_ref):
+def translate_kernel(from_ref, coef_ref, out_ref, turned_ref, wide_ref, held_ref):
     box_rows, box_cols, _, narrow, sides = from_ref.shape
     lanes = min(128, sides)
-
-    def across(place):
-        return pl.ds(pl.multiple_of(place * lanes, lanes), lanes)
 
     turned_ref[...] = coef_ref[...].T
     first = pl.multiple_of(lax.axis_index("sect") * narrow, narrow)
     coefs = turned_ref[pl.ds(first, narrow)]
-    for index in range(coefs.shape[1]):
-        wide_ref[index] = jnp.broadcast_to(coefs[:, index : index + 1], (narrow, lanes))
+    for index in range(len(far_offsets)):
+        real, imag = [
+            jnp.broadcast_to(coefs[:, 2 * index + c : 2 * index + c + 1], (narrow, lanes)) for c in range(2)
+        ]
+        wide_ref[index, 0] = real
+        wide_ref[index, 1] = imag
+        wide_ref[index, 2] = real + imag
 
     def tile(place, carry):
+        across = pl.ds(pl.multiple_of(place * lanes, lanes), lanes)
+        real = from_ref[:, :, 0, :, across].astype(jnp.float32)
+        imag = from_ref[:, :, 1, :, across].astype(jnp.float32)
+        held_ref[:, :, 0] = real
+        held_ref[:, :, 1] = imag
+        held_ref[:, :, 2] = real + imag
         for col in range(box_cols):
-            totals = {}
+            totals = [None] * box_rows
             for source in range(box_rows):
                 held = {
-                    step: [
-                        from_ref[source, col + step, c, :, across(place)].astype(jnp.float32)
-                        for c in range(2)
-                    ]
+                    step: [held_ref[source, col + step, k] for k in range(3)]
                     for step in range(-REACH, REACH + 1)
                     if 0 <= col + step < box_cols
                 }
-                for target in range(max(0, source - REACH), min(box_rows, source + REACH + 1)):
-                    real = imag = None
-                    for index, (row_step, step) in enumerate(far_offsets):
-                        if row_step != source - target or step not in held:
-                            continue
-                        coef_real, coef_imag = wide_ref[2 * index], wide_ref[2 * index + 1]
-                        from_real, from_imag = held[step]
-                        term_real = coef_real * from_real - coef_imag * from_imag
-                        term_imag = coef_real * from_imag + coef_imag * from_real
-                        real = term_real if real is None else real + term_real
-                        imag = term_imag if imag is None else imag + term_imag
-                    if real is None:
-                        continue
-                    real = real.astype(jnp.bfloat16).astype(jnp.float32)
-                    imag = imag.astype(jnp.bfloat16).astype(jnp.float32)
-                    if target in totals:
+                for index, (row_step, step) in enumerate(far_offsets):
+                    target = source - row_step
+                    if 0 <= target < box_rows and step in held:
+                        terms = [wide_ref[index, k] * held[step][k] for k in range(3)]
                         old = totals[target]
-                        real, imag = old[0] + real, old[1] + imag
-                    totals[target] = (real, imag)
-            for target in range(box_rows):
-                for c in range(2):
-                    out_ref[target, col, c, :, across(place)] = (
-                        totals[target][c].astype(jnp.bfloat16)
-                        if target in totals
-                        else jnp.zeros((narrow, lanes), jnp.bfloat16)
-                    )
+                        totals[target] = terms if old is None else [a + b for a, b in zip(old, terms)]
+            for target, total in enumerate(totals):
+                if total is None:
+                    out_ref[target, col, :, :, across] = jnp.zeros((2, narrow, lanes), jnp.bfloat16)
+                else:
+                    a, b, c = total
+                    out_ref[target, col, 0, :, across] = (a - b).astype(jnp.bfloat16)
+                    out_ref[target, col, 1, :, across] = (c - a - b).astype(jnp.bfloat16)
         return carry
 
-    lax.fori_loop(0, sides // lanes, tile, 0)
+    lax.fori_loop(0, sides // lanes, tile, 0, unroll=True)
 
 
 def translate_grid(sources, coefs):
@@ -375,7 +367,8 @@
             out_shape=jax.ShapeDtypeStruct(own.shape, bf16),
             scratch_shapes=[
                 pltpu.VMEM((held, 2 * len(far_offsets)), f32),
-                pltpu.VMEM((2 * len(far_offsets), narrow, lanes), f32),
+                pltpu.VMEM((len(far_offsets), 3, narrow, lanes), f32),
+                pltpu.VMEM((rows, cols, 3, narrow, lanes), f32),
             ],
             compiler_params=params(16),
             cost_estimate=cost(8),

time: 50.9 us -> 50.4 us (level)
    ppermute x4, waiting for transfers between devices: 1.04 us -> 1.62 us  [swap_rows(): return lax.ppermute(array, ('sect', 'dir'), sends)]
    all_to_all x2, waiting for transfers between devices: 13.6 us -> 13 us  [spread(): lax.all_to_all(flat, ('sect', 'dir'), split_axis=0, concat_axis=0, tiled=...]
    pallas_call x1, Pallas kernels: 2.53 us -> 2.02 us  [shards(): pl.pallas_call(translate_kernel, in_specs=[VMEM] * 2, out_specs=VMEM, out...]
  transfers between devices with their start and end apart: 8 -> 8, of which waited for: 3 -> 3; matrix products, arithmetic and copies ran while one was open for 0% -> 0% of each run, Pallas kernels for 14% -> 13%
where the time goes in v6:
time: 50.4 us; the launch traced here: 49.9 us
  starting transfers between devices  15.4 us (31%)
  waiting for transfers between devices  14.6 us (29%)
  Pallas kernels  11.3 us (22%)
  local copies, waits for them, and re-layouts  8.41 us (17%)
    all_to_all x2, waiting for transfers between devices, spread(): lax.all_to_all(flat, ('sect', 'dir'), split_axis=0, concat_axis=0, tiled=...  13 us
    all_to_all x2, starting transfers between devices, spread(): lax.all_to_all(flat, ('sect', 'dir'), split_axis=0, concat_axis=0, tiled=...  9.98 us
    unnamed x24, local copies, waits for them, and re-layouts  8.41 us
    ppermute x4, starting transfers between devices, swap_rows(): return lax.ppermute(array, ('sect', 'dir'), sends)  3.31 us
    pallas_call x1, Pallas kernels, shards(): pl.pallas_call(pattern_kernel, grid=(steps,), in_specs=[pl.BlockSpec(memo...  2.94 us
    pallas_call x1, Pallas kernels, shards(): pl.pallas_call(near_kernel, grid=(deep * wide,), in_specs=[VMEM] * 8 + [p...  2.66 us
    ppermute x2, starting transfers between devices, swap_cols(): return lax.ppermute(array, ('sect', 'dir'), sends)  2.12 us
    pallas_call x1, Pallas kernels, shards(): pl.pallas_call(translate_kernel, in_specs=[VMEM] * 2, out_specs=VMEM, out...  2.02 us
  transfers between devices with their start and end apart: 8, of which 3 were waited for; matrix products, arithmetic and copies ran while one was open for 0% of the time, Pallas kernels for 13%

profile of v6, /device:TPU:0, one launch (start us, length us, event | category | flops | bytes accessed | tf_op | source)
XLA Modules:
  0.0 49.9 jit_solution(1972367843167700267)
XLA Ops:
  0.0 2.9 %patterns.1 = (bf16[4,8,2,16,256]{4,3,2,1,0:T(8,128)(2,1)}, bf16[2,2,128,256]{3,2,1,0:T(8,128)(2,1)}, bf16[2,2,128,256]{3,2,1,0:T(8,128)(2,1)}, bf16[2,128,256]{2,1,0:T(8,128)(2,1)}, bf16[2,128,256]{2,1,0:T(8,128)(2,1)}) custom-call(s32[2,2]{1,0:T(2,128)} %live_ref.3, bf16[2,2,2,128,256]{4,3,2,1,0:T(8,128)(2,1)} %unknowns_ref.1, ...), custom_call_target="tpu_custom_call" | custom-call | tf_op jit(solution)/shard_map/patterns/pallas_call | solution.py:315
  2.9 0.5 collective-permute-start
  3.4 7.4 %all-to-all-start = ((bf16[32,2,16,256]{3,2,1,0:T(8,128)(2,1)}), bf16[32,2,16,256]{3,2,1,0:T(8,128)(2,1)S(1)}, u32[]{:S(2)}, u32[]{:S(2)}) async-start(bf16[32,2,16,256]{3,2,1,0:T(8,128)(2,1)} %bitcast.8), calls=%async_computation | async-start | bytes 1048576 | tf_op jit(solution)/shard_map/all_to_all | solution.py:357
  10.8 1.6 %collective-permute-start.4 = (bf16[2,128,256]{2,1,0:T(8,128)(2,1)}, bf16[2,128,256]{2,1,0:T(8,128)(2,1)S(1)}, u32[]{:S(2)}, u32[]{:S(2)}) collective-permute-start(bf16[2,128,256]{2,1,0:T(8,128)(2,1)} %get-tuple-element.19), channel_id=1, source_target_pairs={{0,9},{1,8},{2,11},{3,10},{4,13},{5,12},{6,15},{7,14},{8,1},{9,0},... | collective-permute-start | bytes 393224 | tf_op jit(solution)/shard_map/ppermute | solution.py:53
  12.4 0.4 collective-permute-start.5
  12.7 1.7 %collective-permute-start.1 = (bf16[2,2,128,256]{3,2,1,0:T(8,128)(2,1)}, bf16[2,2,128,256]{3,2,1,0:T(8,128)(2,1)S(1)}, u32[]{:S(2)}, u32[]{:S(2)}) collective-permute-start(bf16[2,2,128,256]{3,2,1,0:T(8,128)(2,1)} %get-tuple-element.14.near_ref), channel_id=1, source_target_pairs={{0,1},{1,0},{2,3},{3,2},{4,5},{5,4},{6,7},{7,6},{8,9},{9,8},{10,11... | collective-permute-start | bytes 786440 | tf_op jit(solution)/shard_map/ppermute | solution.py:43
  14.4 0.0 collective-permute-done.from_cross_ref
  14.4 0.7 %copy-done.5 = bf16[2,2,128,256]{3,2,1,0:T(8,128)(2,1)} copy-done((bf16[2,2,128,256]{3,2,1,0:T(8,128)(2,1)}, bf16[2,2,128,256]{3,2,1,0:T(8,128)(2,1)S(1)}, u32[]{:S(2)}) %copy-start.5) | copy-done | bytes 262168
  15.1 2.0 %rows.1 = (bf16[2,3,128,256]{3,2,1,0:T(8,128)(2,1)}, bf16[2,3,128,256]{3,2,1,0:T(8,128)(2,1)}) custom-call(bf16[2,2,128,256]{3,2,1,0:T(8,128)(2,1)} %get-tuple-element.14.near_ref, bf16[2,2,128,256]{3,2,1,0:T(8,128)(2,1)} %get-tuple-element.15.cross_ref, bf16[2,2,128,256]{3,2,1,0:T(8,128)(2,1)} %copy-done.5), custom_call_target="tpu_custom_call" | custom-call | flops 9200000000 | bytes 29520000 | tf_op jit(solution)/shard_map/rows/pallas_call | solution.py:341
  17.1 0.8 %collective-permute-start.2 = (bf16[2,3,128,256]{3,2,1,0:T(8,128)(2,1)}, bf16[2,3,128,256]{3,2,1,0:T(8,128)(2,1)S(1)}, u32[]{:S(2)}, u32[]{:S(2)}) collective-permute-start(bf16[2,3,128,256]{3,2,1,0:T(8,128)(2,1)} %get-tuple-element.16), channel_id=1, source_target_pairs={{0,8},{1,9},{2,10},{3,11},{4,12},{5,13},{6,14},{7,15},{8,0},{9,1},... | collective-permute-start | bytes 1179656 | tf_op jit(solution)/shard_map/ppermute | solution.py:53
  17.9 0.6 %collective-permute-start.3 = (bf16[2,3,128,256]{3,2,1,0:T(8,128)(2,1)}, bf16[2,3,128,256]{3,2,1,0:T(8,128)(2,1)S(1)}, u32[]{:S(2)}, u32[]{:S(2)}) collective-permute-start(bf16[2,3,128,256]{3,2,1,0:T(8,128)(2,1)} %get-tuple-element.17), channel_id=1, source_target_pairs={{0,1},{1,0},{2,3},{3,2},{4,5},{5,4},{6,7},{7,6},{8,16},{9,17},{10,... | collective-permute-start | bytes 1179656 | tf_op jit(solution)/shard_map/ppermute | solution.py:53
  18.4 8.7 %all-to-all-done = bf16[32,2,16,256]{3,2,1,0:T(8,128)(2,1)S(1)} async-done(((bf16[32,2,16,256]{3,2,1,0:T(8,128)(2,1)}), bf16[32,2,16,256]{3,2,1,0:T(8,128)(2,1)S(1)}, u32[]{:S(2)}, u32[]{:S(2)}) %all-to-all-start) | async-done | bytes 524320 | tf_op jit(solution)/shard_map/all_to_all | solution.py:357
  27.1 2.0 %translations.1 = bf16[4,8,2,16,256]{4,3,2,1,0:T(8,128)(2,1)} custom-call(bf16[4,8,2,16,256]{4,3,2,1,0:T(8,128)(2,1)S(1)} %bitcast.6, f32[32,64]{1,0:T(8,128)S(1)} %bitcast.7), custom_call_target="tpu_custom_call" | custom-call | flops 9200000000 | bytes 29520000 | tf_op jit(solution)/shard_map/translations/pallas_call | solution.py:363
  29.2 2.6 %all-to-all-start.1 = ((bf16[32,2,16,256]{3,2,1,0:T(8,128)(2,1)}), bf16[32,2,16,256]{3,2,1,0:T(8,128)(2,1)S(1)}, u32[]{:S(2)}, u32[]{:S(2)}) async-start(bf16[32,2,16,256]{3,2,1,0:T(8,128)(2,1)} %bitcast.3), calls=%async_computation.1 | async-start | bytes 1048576 | tf_op jit(solution)/shard_map/all_to_all | solution.py:357
  31.8 0.0 copy-start
  31.8 0.0 copy-start.1
  31.8 0.0 collective-permute-done.4.corner_near_ref
  31.8 0.0 collective-permute-done.5.corner_cross_ref
  31.8 0.6 %copy-done.9 = bf16[2,128,256]{2,1,0:T(8,128)(2,1)} copy-done((bf16[2,128,256]{2,1,0:T(8,128)(2,1)}, bf16[2,128,256]{2,1,0:T(8,128)(2,1)S(1)}, u32[]{:S(2)}) %copy-start.9) | copy-done | bytes 131096
  32.5 0.0 collective-permute-done.1.from_near_ref
  32.5 0.7 %copy-done.7 = bf16[2,2,128,256]{3,2,1,0:T(8,128)(2,1)} copy-done((bf16[2,2,128,256]{3,2,1,0:T(8,128)(2,1)}, bf16[2,2,128,256]{3,2,1,0:T(8,128)(2,1)S(1)}, u32[]{:S(2)}) %copy-start.7) | copy-done | bytes 262168
  33.2 0.0 collective-permute-done.2.row_near_ref
  33.2 1.6 %collective-permute-done.3.row_cross_ref = bf16[2,3,128,256]{3,2,1,0:T(8,128)(2,1)S(1)} collective-permute-done((bf16[2,3,128,256]{3,2,1,0:T(8,128)(2,1)}, bf16[2,3,128,256]{3,2,1,0:T(8,128)(2,1)S(1)}, u32[]{:S(2)}, u32[]{:S(2)}) %collective-permute-start.3) | collective-permute-done | bytes 393248 | tf_op jit(solution)/shard_map/ppermute | solution.py:53
  34.8 1.7 %copy-done.2 = bf16[2,2,2,9,128,128]{5,4,3,2,1,0:T(8,128)(2,1)S(1)} copy-done((bf16[2,2,2,9,128,128]{5,4,3,2,1,0:T(8,128)(2,1)S(1)}, bf16[2,2,2,9,128,128]{5,4,3,2,1,0:T(8,128)(2,1)}, u32[]{:S(2)}) %copy-start.2) | copy-done | bytes 2359320
  36.4 0.9 %copy-done.3 = bf16[2,2,128,256]{3,2,1,0:T(8,128)(2,1)S(1)} copy-done((bf16[2,2,128,256]{3,2,1,0:T(8,128)(2,1)S(1)}, bf16[2,2,128,256]{3,2,1,0:T(8,128)(2,1)}, u32[]{:S(2)}) %copy-start.3) | copy-done | bytes 262168
  37.4 0.9 %copy-done.4 = bf16[2,2,128,256]{3,2,1,0:T(8,128)(2,1)S(1)} copy-done((bf16[2,2,128,256]{3,2,1,0:T(8,128)(2,1)S(1)}, bf16[2,2,128,256]{3,2,1,0:T(8,128)(2,1)}, u32[]{:S(2)}) %copy-start.4) | copy-done | bytes 262168
  38.4 0.9 %copy-done.6 = bf16[2,2,128,256]{3,2,1,0:T(8,128)(2,1)S(1)} copy-done((bf16[2,2,128,256]{3,2,1,0:T(8,128)(2,1)S(1)}, bf16[2,2,128,256]{3,2,1,0:T(8,128)(2,1)}, u32[]{:S(2)}) %copy-start.6) | copy-done | bytes 262168
  39.3 0.9 %copy-done.8 = bf16[2,2,128,256]{3,2,1,0:T(8,128)(2,1)S(1)} copy-done((bf16[2,2,128,256]{3,2,1,0:T(8,128)(2,1)S(1)}, bf16[2,2,128,256]{3,2,1,0:T(8,128)(2,1)}, u32[]{:S(2)}) %copy-start.8) | copy-done | bytes 262168
  40.3 0.9 %copy-done.10 = bf16[2,128,256]{2,1,0:T(8,128)(2,1)S(1)} copy-done((bf16[2,128,256]{2,1,0:T(8,128)(2,1)S(1)}, bf16[2,128,256]{2,1,0:T(8,128)(2,1)}, u32[]{:S(2)}) %copy-start.10) | copy-done | bytes 131096
  41.2 2.7 %near.1.near_ref = f32[2,2,2,128,256]{4,3,2,1,0:T(8,128)S(1)} custom-call(bf16[2,2,128,256]{3,2,1,0:T(8,128)(2,1)S(1)} %copy-done.3, bf16[2,2,128,256]{3,2,1,0:T(8,128)(2,1)S(1)} %copy-done.4, bf16[2,2,128,256]{3,2,1,0:T(8,128)(2,1)S(1)} %copy-done.6, bf16[2,2,128,256]{3,2,1,0:T(8,128)(2,1)S(1)} %copy-done.8, ...), custom_call_target="tpu_custom_call" | custom-call | flops 13799999488 | bytes 44280000 | tf_op jit(solution)/shard_map/near/pallas_call | solution.py:393
  43.8 4.3 %all-to-all-done.1 = bf16[32,2,16,256]{3,2,1,0:T(8,128)(2,1)S(1)} async-done(((bf16[32,2,16,256]{3,2,1,0:T(8,128)(2,1)}), bf16[32,2,16,256]{3,2,1,0:T(8,128)(2,1)S(1)}, u32[]{:S(2)}, u32[]{:S(2)}) %all-to-all-start.1) | async-done | bytes 524320 | tf_op jit(solution)/shard_map/all_to_all | solution.py:357
  48.1 1.7 %far.1 = f32[2,2,2,128,256]{4,3,2,1,0:T(8,128)} custom-call(s32[2,2]{1,0:T(2,128)S(1)} %copy-done.1, bf16[4,8,2,16,256]{4,3,2,1,0:T(8,128)(2,1)S(1)} %bitcast.5, bf16[2,2,2,128,512]{4,3,2,1,0:T(8,128)(2,1)S(1)} %copy-done, f32[2,2,2,128,256]{4,3,2,1,0:T(8,128)S(1)} %near.1.near_ref), custom_call_target="tpu_custom_call" | custom-call | tf_op jit(solution)/shard_map/far/pallas_call | solution.py:408
  (13 shorter events, 0.0 us)
Async XLA Ops:
  2.9 11.5 %collective-permute-start = (bf16[2,2,128,256]{3,2,1,0:T(8,128)(2,1)}, bf16[2,2,128,256]{3,2,1,0:T(8,128)(2,1)S(1)}, u32[]{:S(2)}, u32[]{:S(2)}) collective-permute-start(bf16[2,2,128,256]{3,2,1,0:T(8,128)(2,1)} %get-tuple-element.15.cross_ref), channel_id=1, source_target_pairs={{0,8},{1,2},{2,1},{3,4},{4,3},{5,6},{6,5},{7,15},{8,0},{9,10},{10,... | collective-permute-start | bytes 786440 | tf_op jit(solution)/shard_map/ppermute | solution.py:43
  3.4 23.7 %all-to-all-start = ((bf16[32,2,16,256]{3,2,1,0:T(8,128)(2,1)}), bf16[32,2,16,256]{3,2,1,0:T(8,128)(2,1)S(1)}, u32[]{:S(2)}, u32[]{:S(2)}) async-start(bf16[32,2,16,256]{3,2,1,0:T(8,128)(2,1)} %bitcast.8), calls=%async_computation | async-start | bytes 1048576 | tf_op jit(solution)/shard_map/all_to_all | solution.py:357
  10.8 21.0 %collective-permute-start.4 = (bf16[2,128,256]{2,1,0:T(8,128)(2,1)}, bf16[2,128,256]{2,1,0:T(8,128)(2,1)S(1)}, u32[]{:S(2)}, u32[]{:S(2)}) collective-permute-start(bf16[2,128,256]{2,1,0:T(8,128)(2,1)} %get-tuple-element.19), channel_id=1, source_target_pairs={{0,9},{1,8},{2,11},{3,10},{4,13},{5,12},{6,15},{7,14},{8,1},{9,0},... | collective-permute-start | bytes 393224 | tf_op jit(solution)/shard_map/ppermute | solution.py:53
  12.4 19.4 %collective-permute-start.5 = (bf16[2,128,256]{2,1,0:T(8,128)(2,1)}, bf16[2,128,256]{2,1,0:T(8,128)(2,1)S(1)}, u32[]{:S(2)}, u32[]{:S(2)}) collective-permute-start(bf16[2,128,256]{2,1,0:T(8,128)(2,1)} %get-tuple-element.20), channel_id=1, source_target_pairs={{0,1},{1,0},{2,3},{3,2},{4,5},{5,4},{6,7},{7,6},{8,17},{9,16},{10,... | collective-permute-start | bytes 393224 | tf_op jit(solution)/shard_map/ppermute | solution.py:53
  12.7 14.4 %copy-start.11 = (f32[16,2,64]{2,1,0:T(2,128)S(1)}, f32[16,2,64]{2,1,0:T(2,128)}, u32[]{:S(2)}) copy-start(f32[16,2,64]{2,1,0:T(2,128)} %param.11) | copy-start | bytes 24580
  12.7 19.7 %collective-permute-start.1 = (bf16[2,2,128,256]{3,2,1,0:T(8,128)(2,1)}, bf16[2,2,128,256]{3,2,1,0:T(8,128)(2,1)S(1)}, u32[]{:S(2)}, u32[]{:S(2)}) collective-permute-start(bf16[2,2,128,256]{3,2,1,0:T(8,128)(2,1)} %get-tuple-element.14.near_ref), channel_id=1, source_target_pairs={{0,1},{1,0},{2,3},{3,2},{4,5},{5,4},{6,7},{7,6},{8,9},{9,8},{10,11... | collective-permute-start | bytes 786440 | tf_op jit(solution)/shard_map/ppermute | solution.py:43
  14.4 0.7 %copy-start.5 = (bf16[2,2,128,256]{3,2,1,0:T(8,128)(2,1)}, bf16[2,2,128,256]{3,2,1,0:T(8,128)(2,1)S(1)}, u32[]{:S(2)}) copy-start(bf16[2,2,128,256]{3,2,1,0:T(8,128)(2,1)S(1)} %collective-permute-done.from_cross_ref) | copy-start | bytes 786436
  17.1 16.1 %collective-permute-start.2 = (bf16[2,3,128,256]{3,2,1,0:T(8,128)(2,1)}, bf16[2,3,128,256]{3,2,1,0:T(8,128)(2,1)S(1)}, u32[]{:S(2)}, u32[]{:S(2)}) collective-permute-start(bf16[2,3,128,256]{3,2,1,0:T(8,128)(2,1)} %get-tuple-element.16), channel_id=1, source_target_pairs={{0,8},{1,9},{2,10},{3,11},{4,12},{5,13},{6,14},{7,15},{8,0},{9,1},... | collective-permute-start | bytes 1179656 | tf_op jit(solution)/shard_map/ppermute | solution.py:53
  17.9 16.9 %collective-permute-start.3 = (bf16[2,3,128,256]{3,2,1,0:T(8,128)(2,1)}, bf16[2,3,128,256]{3,2,1,0:T(8,128)(2,1)S(1)}, u32[]{:S(2)}, u32[]{:S(2)}) collective-permute-start(bf16[2,3,128,256]{3,2,1,0:T(8,128)(2,1)} %get-tuple-element.17), channel_id=1, source_target_pairs={{0,1},{1,0},{2,3},{3,2},{4,5},{5,4},{6,7},{7,6},{8,16},{9,17},{10,... | collective-permute-start | bytes 1179656 | tf_op jit(solution)/shard_map/ppermute | solution.py:53
  29.2 19.0 %all-to-all-start.1 = ((bf16[32,2,16,256]{3,2,1,0:T(8,128)(2,1)}), bf16[32,2,16,256]{3,2,1,0:T(8,128)(2,1)S(1)}, u32[]{:S(2)}, u32[]{:S(2)}) async-start(bf16[32,2,16,256]{3,2,1,0:T(8,128)(2,1)} %bitcast.3), calls=%async_computation.1 | async-start | bytes 1048576 | tf_op jit(solution)/shard_map/all_to_all | solution.py:357
  31.8 16.4 %copy-start = (bf16[2,2,2,128,512]{4,3,2,1,0:T(8,128)(2,1)S(1)}, bf16[2,2,2,128,512]{4,3,2,1,0:T(8,128)(2,1)}, u32[]{:S(2)}) copy-start(bf16[2,2,2,128,512]{4,3,2,1,0:T(8,128)(2,1)} %disaggregate_ref.1) | copy-start | bytes 3145732
  31.8 16.3 %copy-start.1 = (s32[2,2]{1,0:T(2,128)S(1)}, s32[2,2]{1,0:T(2,128)}, u32[]{:S(2)}) copy-start(s32[2,2]{1,0:T(2,128)} %live_ref.3) | copy-start | bytes 52
  31.8 0.6 %copy-start.9 = (bf16[2,128,256]{2,1,0:T(8,128)(2,1)}, bf16[2,128,256]{2,1,0:T(8,128)(2,1)S(1)}, u32[]{:S(2)}) copy-start(bf16[2,128,256]{2,1,0:T(8,128)(2,1)S(1)} %collective-permute-done.5.corner_cross_ref) | copy-start | bytes 393220
  32.5 0.7 %copy-start.7 = (bf16[2,2,128,256]{3,2,1,0:T(8,128)(2,1)}, bf16[2,2,128,256]{3,2,1,0:T(8,128)(2,1)S(1)}, u32[]{:S(2)}) copy-start(bf16[2,2,128,256]{3,2,1,0:T(8,128)(2,1)S(1)} %collective-permute-done.1.from_near_ref) | copy-start | bytes 786436
  34.8 1.7 %copy-start.2 = (bf16[2,2,2,9,128,128]{5,4,3,2,1,0:T(8,128)(2,1)S(1)}, bf16[2,2,2,9,128,128]{5,4,3,2,1,0:T(8,128)(2,1)}, u32[]{:S(2)}) copy-start(bf16[2,2,2,9,128,128]{5,4,3,2,1,0:T(8,128)(2,1)} %blocks_ref.1) | copy-start | bytes 7077892
  36.4 0.9 %copy-start.3 = (bf16[2,2,128,256]{3,2,1,0:T(8,128)(2,1)S(1)}, bf16[2,2,128,256]{3,2,1,0:T(8,128)(2,1)}, u32[]{:S(2)}) copy-start(bf16[2,2,128,256]{3,2,1,0:T(8,128)(2,1)} %get-tuple-element.14.near_ref) | copy-start | bytes 786436
  37.4 0.9 %copy-start.4 = (bf16[2,2,128,256]{3,2,1,0:T(8,128)(2,1)S(1)}, bf16[2,2,128,256]{3,2,1,0:T(8,128)(2,1)}, u32[]{:S(2)}) copy-start(bf16[2,2,128,256]{3,2,1,0:T(8,128)(2,1)} %get-tuple-element.15.cross_ref) | copy-start | bytes 786436
  38.3 0.9 %copy-start.6 = (bf16[2,2,128,256]{3,2,1,0:T(8,128)(2,1)S(1)}, bf16[2,2,128,256]{3,2,1,0:T(8,128)(2,1)}, u32[]{:S(2)}) copy-start(bf16[2,2,128,256]{3,2,1,0:T(8,128)(2,1)} %copy-done.5) | copy-start | bytes 786436
  39.3 0.9 %copy-start.8 = (bf16[2,2,128,256]{3,2,1,0:T(8,128)(2,1)S(1)}, bf16[2,2,128,256]{3,2,1,0:T(8,128)(2,1)}, u32[]{:S(2)}) copy-start(bf16[2,2,128,256]{3,2,1,0:T(8,128)(2,1)} %copy-done.7) | copy-start | bytes 786436
  40.2 0.9 %copy-start.10 = (bf16[2,128,256]{2,1,0:T(8,128)(2,1)S(1)}, bf16[2,128,256]{2,1,0:T(8,128)(2,1)}, u32[]{:S(2)}) copy-start(bf16[2,128,256]{2,1,0:T(8,128)(2,1)} %copy-done.9) | copy-start | bytes 393220

commit v7 on v6

--- a/solution.py
+++ b/solution.py
@@ -68,50 +68,44 @@
     live_ref, unknowns_ref, aggregate_ref, out_ref, near_ref, cross_ref, corner_near_ref,
     corner_cross_ref, leaves_ref,
 ):
-    rows, cols, _, narrow, sides = out_ref.shape
+    parts, _, narrow, sides = out_ref.shape
     deep, wide, size = unknowns_ref.shape[1:4]
 
-    @pl.when(pl.program_id(0) == 0)
-    def _():
-        for u in range(deep):
-            for v in range(wide):
-                keep = live_ref[u, v].astype(jnp.float32).astype(jnp.bfloat16)
-                at = (u * wide + v) * size
-                for c in range(2):
-                    leaves_ref[at : at + size, c * sides : (c + 1) * sides] = (
-                        unknowns_ref[c, u, v] * keep
-                    )
+    for u in range(deep):
+        for v in range(wide):
+            keep = live_ref[u, v].astype(jnp.float32).astype(jnp.bfloat16)
+            at = (u * wide + v) * size
+            for c in range(2):
+                leaves_ref[at : at + size, c * sides : (c + 1) * sides] = (
+                    unknowns_ref[c, u, v] * keep
+                )
 
     left = [
         jnp.concatenate([aggregate_ref[c, u, v] for u in range(deep) for v in range(wide)], axis=1)
         for c in range(2)
     ]
     real, imag = complex_dot(left[0], left[1], leaves_ref[...])
-    for row in range(rows):
-        for col in range(cols):
-            at = (col * rows + row) * narrow
-            out_ref[row, col, 0] = real[at : at + narrow].astype(jnp.bfloat16)
-            out_ref[row, col, 1] = imag[at : at + narrow].astype(jnp.bfloat16)
-
-    @pl.when(pl.program_id(0) == 0)
-    def _():
-        odd = lax.rem(lax.axis_index("dir"), 2)
-        row_odd = lax.rem(lax.axis_index("sect"), 2)
-
-        def leaf(u, v, c):
-            at = pl.multiple_of((u * wide + v) * size, size)
-            return leaves_ref[pl.ds(at, size), c * sides : (c + 1) * sides]
-
-        for c in range(2):
-            for u in range(deep):
-                near_ref[c, u] = leaf(u, 1 - odd, c)
-                cross_ref[c, u] = leaf(u, odd, c)
-            corner_near_ref[c] = leaf(1 - row_odd, 1 - odd, c)
-            corner_cross_ref[c] = leaf(row_odd, 1 - odd, c)
+    for part in range(parts):
+        out_ref[part, 0] = real[part * narrow : (part + 1) * narrow].astype(jnp.bfloat16)
+        out_ref[part, 1] = imag[part * narrow : (part + 1) * narrow].astype(jnp.bfloat16)
+
+    odd = lax.rem(lax.axis_index("dir"), 2)
+    row_odd = lax.rem(lax.axis_index("sect"), 2)
+
+    def leaf(u, v, c):
+        at = pl.multiple_of((u * wide + v) * size, size)
+        return leaves_ref[pl.ds(at, size), c * sides : (c + 1) * sides]
+
+    for c in range(2):
+        for u in range(deep):
+            near_ref[c, u] = leaf(u, 1 - odd, c)
+            cross_ref[c, u] = leaf(u, odd, c)
+        corner_near_ref[c] = leaf(1 - row_odd, 1 - odd, c)
+        corner_cross_ref[c] = leaf(row_odd, 1 - odd, c)
 
 
 def translate_kernel(from_ref, coef_ref, out_ref, turned_ref, wide_ref, held_ref):
-    box_rows, box_cols, _, narrow, sides = from_ref.shape
+    box_cols, box_rows, _, narrow, sides = from_ref.shape
     lanes = min(128, sides)
 
     turned_ref[...] = coef_ref[...].T
@@ -136,23 +130,29 @@
             totals = [None] * box_rows
             for source in range(box_rows):
                 held = {
-                    step: [held_ref[source, col + step, k] for k in range(3)]
+                    step: [held_ref[col + step, source, k] for k in range(3)]
                     for step in range(-REACH, REACH + 1)
                     if 0 <= col + step < box_cols
                 }
-                for index, (row_step, step) in enumerate(far_offsets):
-                    target = source - row_step
-                    if 0 <= target < box_rows and step in held:
-                        terms = [wide_ref[index, k] * held[step][k] for k in range(3)]
-                        old = totals[target]
-                        totals[target] = terms if old is None else [a + b for a, b in zip(old, terms)]
+                for target in range(max(0, source - REACH), min(box_rows, source + REACH + 1)):
+                    sums = None
+                    for index, (row_step, step) in enumerate(far_offsets):
+                        if row_step == source - target and step in held:
+                            terms = [wide_ref[index, k] * held[step][k] for k in range(3)]
+                            sums = terms if sums is None else [x + y for x, y in zip(sums, terms)]
+                    if sums is None:
+                        continue
+                    a, b, c = sums
+                    term = [x.astype(jnp.bfloat16).astype(jnp.float32) for x in (a - b, c - a - b)]
+                    old = totals[target]
+                    totals[target] = term if old is None else [x + y for x, y in zip(old, term)]
             for target, total in enumerate(totals):
-                if total is None:
-                    out_ref[target, col, :, :, across] = jnp.zeros((2, narrow, lanes), jnp.bfloat16)
-                else:
-                    a, b, c = total
-                    out_ref[target, col, 0, :, across] = (a - b).astype(jnp.bfloat16)
-                    out_ref[target, col, 1, :, across] = (c - a - b).astype(jnp.bfloat16)
+                for c in range(2):
+                    out_ref[col, target, c, :, across] = (
+                        jnp.zeros((narrow, lanes), jnp.bfloat16)
+                        if total is None
+                        else total[c].astype(jnp.bfloat16)
+                    )
         return carry
 
     lax.fori_loop(0, sides // lanes, tile, 0, unroll=True)
@@ -258,14 +258,12 @@
     live_ref, incoming_ref, disaggregate_ref, near_ref, out_ref, live_here, right_ref, made_ref, live_sem,
     in_sem, out_sem,
 ):
-    rows, cols, _, narrow, sides = incoming_ref.shape
+    parts, _, narrow, sides = incoming_ref.shape
     deep, wide = live_ref.shape
 
-    def arrival(row, c):
+    def arrival(c):
         return pltpu.make_async_copy(
-            incoming_ref.at[row, :, c],
-            right_ref.at[:, row, :, c * sides : (c + 1) * sides],
-            in_sem.at[row, c],
+            incoming_ref.at[:, c], right_ref.at[:, :, c * sides : (c + 1) * sides], in_sem.at[c]
         )
 
     def departure(u, v):
@@ -273,15 +271,14 @@
             made_ref.at[:, u, v], out_ref.at[:, u, v], out_sem.at[u, v]
         )
 
-    places = [(row, c) for row in range(rows) for c in range(2)]
     live_copy = pltpu.make_async_copy(live_ref, live_here, live_sem)
     live_copy.start()
-    for place in places:
-        arrival(*place).start()
+    for c in range(2):
+        arrival(c).start()
     live_copy.wait()
-    for place in places:
-        arrival(*place).wait()
-    right = right_ref[...].reshape(cols * rows * narrow, 2 * sides)
+    for c in range(2):
+        arrival(c).wait()
+    right = right_ref[...].reshape(parts * narrow, 2 * sides)
     for u in range(deep):
         for v in range(wide):
             live = live_here[u : u + 1, v : v + 1].astype(jnp.float32)
@@ -302,31 +299,16 @@
     held = translate.shape[2]
     bf16, f32 = jnp.bfloat16, jnp.float32
     tiled = narrow % 16 == 0
-    steps = 1
-    rows, cols = (sect_count, dir_count) if tiled else (1, steps)
-    block = total_dirs // (rows * cols)
+    parts = dir_count * sect_count if tiled else 1
+    block = total_dirs // parts
 
     column = jax.ShapeDtypeStruct((2, deep, size, sides), bf16)
     corner = jax.ShapeDtypeStruct((2, size, sides), bf16)
-    blocks = jax.ShapeDtypeStruct((rows, cols, 2, block, sides), bf16)
-    whole = [
-        pl.BlockSpec(a.shape, lambda i, n=len(a.shape): (0,) * n) for a in (unknowns, column, corner)
-    ]
+    blocks = jax.ShapeDtypeStruct((parts, 2, block, sides), bf16)
     patterns, col_near, col_cross, corner_near, corner_cross = pl.pallas_call(
         pattern_kernel,
-        grid=(steps,),
-        in_specs=[
-            pl.BlockSpec(memory_space=pltpu.SMEM),
-            whole[0],
-            pl.BlockSpec((2, deep, wide, total_dirs // steps, size), lambda i: (0, 0, 0, i, 0)),
-        ],
-        out_specs=[
-            pl.BlockSpec((rows, cols // steps, 2, block, sides), lambda i: (0, i, 0, 0, 0)),
-            whole[1],
-            whole[1],
-            whole[2],
-            whole[2],
-        ],
+        in_specs=[pl.BlockSpec(memory_space=pltpu.SMEM), VMEM, VMEM],
+        out_specs=[VMEM] * 5,
         out_shape=[blocks, column, column, corner, corner],
         scratch_shapes=[pltpu.VMEM((deep * wide * size, 2 * sides), bf16)],
         compiler_params=params(),
@@ -353,11 +335,11 @@
     )(col_near, col_cross, from_cross)
 
     def spread(array):
-        flat = array.reshape(rows * cols, 2, block, sides)
-        return lax.all_to_all(flat, ("sect", "dir"), split_axis=0, concat_axis=0, tiled=True).reshape(array.shape)
+        flat = array.reshape(parts, 2, block, sides)
+        return lax.all_to_all(flat, ("dir", "sect"), split_axis=0, concat_axis=0, tiled=True)
 
     if tiled:
-        own = spread(patterns)
+        own = spread(patterns).reshape(dir_count, sect_count, 2, block, sides)
         own, _, _ = lax.optimization_barrier((own, row_near, row_cross))
         lanes = min(128, sides)
         incoming = pl.pallas_call(
@@ -368,7 +350,7 @@
             scratch_shapes=[
                 pltpu.VMEM((held, 2 * len(far_offsets)), f32),
                 pltpu.VMEM((len(far_offsets), 3, narrow, lanes), f32),
-                pltpu.VMEM((rows, cols, 3, narrow, lanes), f32),
+                pltpu.VMEM((dir_count, sect_count, 3, narrow, lanes), f32),
             ],
             compiler_params=params(16),
             cost_estimate=cost(8),
@@ -376,16 +358,14 @@
         )(own, translate.reshape(2 * len(far_offsets), held))
         returned = spread(incoming)
     else:
-        split = (2, dir_count, sect_count, narrow, sides)
-        base = patterns[0].transpose(1, 0, 2, 3).reshape(split).transpose(0, 2, 1, 3, 4)
+        base = patterns.reshape(2, dir_count, sect_count, narrow, sides).transpose(0, 2, 1, 3, 4)
         base = base.reshape(2, total_dirs, sides)[None, None]
         own = lax.all_to_all(base, "sect", split_axis=3, concat_axis=0, tiled=True)
         own = lax.all_to_all(own, "dir", split_axis=3, concat_axis=1, tiled=True)
         coefs = lax.dynamic_slice_in_dim(translate, lax.axis_index("sect") * narrow, narrow, 2)
         incoming = translate_grid(own, coefs)
         returned = lax.all_to_all(incoming, "sect", split_axis=0, concat_axis=3, tiled=True)
-        returned = lax.all_to_all(returned, "dir", split_axis=1, concat_axis=3, tiled=True)[0, 0]
-        returned = returned.reshape(2, cols, block, sides).transpose(1, 0, 2, 3)[None]
+        returned = lax.all_to_all(returned, "dir", split_axis=1, concat_axis=3, tiled=True)[0]
 
     row_near = swap_rows(row_near, 0)
     row_cross = swap_rows(row_cross, 1)
@@ -412,10 +392,10 @@
         out_shape=field,
         scratch_shapes=[
             pltpu.VMEM(leaf_live.shape, jnp.int32),
-            pltpu.VMEM((cols, rows, block, 2 * sides), bf16),
+            pltpu.VMEM((parts, block, 2 * sides), bf16),
             pltpu.VMEM(unknowns.shape, f32),
             pltpu.SemaphoreType.DMA,
-            pltpu.SemaphoreType.DMA((rows, 2)),
+            pltpu.SemaphoreType.DMA((2,)),
             pltpu.SemaphoreType.DMA((deep, wide)),
         ],
         compiler_params=params(16),

time: 50.4 us -> 49.6 us (0.984)
  waiting for transfers between devices: 14.6 us -> 13 us
  starting transfers between devices: 15.4 us -> 16.1 us
    all_to_all x2, waiting for transfers between devices: 13 us -> 11.1 us  [spread(): lax.all_to_all(flat, ('dir', 'sect'), split_axis=0, concat_axis=0, tiled=...]
    all_to_all x2, starting transfers between devices: 9.98 us -> 10.6 us  [spread(): lax.all_to_all(flat, ('dir', 'sect'), split_axis=0, concat_axis=0, tiled=...]
  transfers between devices with their start and end apart: 8 -> 8, of which waited for: 3 -> 3; matrix products, arithmetic and copies ran while one was open for 0% -> 0% of each run, Pallas kernels for 13% -> 14%
where the time goes in v7:
time: 49.6 us; the launch traced here: 49.1 us
  starting transfers between devices  16.1 us (32%)
  waiting for transfers between devices  13 us (26%)
  Pallas kernels  11.5 us (23%)
  local copies, waits for them, and re-layouts  8.41 us (17%)
    all_to_all x2, waiting for transfers between devices, spread(): lax.all_to_all(flat, ('dir', 'sect'), split_axis=0, concat_axis=0, tiled=...  11.1 us
    all_to_all x2, starting transfers between devices, spread(): lax.all_to_all(flat, ('dir', 'sect'), split_axis=0, concat_axis=0, tiled=...  10.6 us
    unnamed x24, local copies, waits for them, and re-layouts  8.41 us
    ppermute x4, starting transfers between devices, swap_rows(): return lax.ppermute(array, ('sect', 'dir'), sends)  3.31 us
    pallas_call x1, Pallas kernels, shards(): pl.pallas_call(pattern_kernel, in_specs=[pl.BlockSpec(memory_space=pltpu....  2.94 us
    pallas_call x1, Pallas kernels, shards(): pl.pallas_call(near_kernel, grid=(deep * wide,), in_specs=[VMEM] * 8 + [p...  2.66 us
    pallas_call x1, Pallas kernels, shards(): pl.pallas_call(translate_kernel, in_specs=[VMEM] * 2, out_specs=VMEM, out...  2.28 us
    ppermute x2, starting transfers between devices, swap_cols(): return lax.ppermute(array, ('sect', 'dir'), sends)  2.12 us
  transfers between devices with their start and end apart: 8, of which 3 were waited for; matrix products, arithmetic and copies ran while one was open for 0% of the time, Pallas kernels for 14%

profile of v7, /device:TPU:0, one launch (start us, length us, event | category | flops | bytes accessed | tf_op | source)
XLA Modules:
  0.0 49.1 jit_solution(15577039347699871234)
XLA Ops:
  0.0 2.9 %patterns.1 = (bf16[32,2,16,256]{3,2,1,0:T(8,128)(2,1)}, bf16[2,2,128,256]{3,2,1,0:T(8,128)(2,1)}, bf16[2,2,128,256]{3,2,1,0:T(8,128)(2,1)}, bf16[2,128,256]{2,1,0:T(8,128)(2,1)}, bf16[2,128,256]{2,1,0:T(8,128)(2,1)}) custom-call(s32[2,2]{1,0:T(2,128)} %live_ref.3, bf16[2,2,2,128,256]{4,3,2,1,0:T(8,128)(2,1)} %unknowns_ref.1, ...), custom_call_target="tpu_custom_call" | custom-call | tf_op jit(solution)/shard_map/patterns/pallas_call | solution.py:308
  2.9 0.5 collective-permute-start
  3.4 7.4 %all-to-all-start = ((bf16[32,2,16,256]{3,2,1,0:T(8,128)(2,1)}), bf16[32,2,16,256]{3,2,1,0:T(8,128)(2,1)S(1)}, u32[]{:S(2)}, u32[]{:S(2)}) async-start(bf16[32,2,16,256]{3,2,1,0:T(8,128)(2,1)} %get-tuple-element.13), calls=%async_computation | async-start | bytes 1048576 | tf_op jit(solution)/shard_map/all_to_all | solution.py:339
  10.8 1.6 %collective-permute-start.4 = (bf16[2,128,256]{2,1,0:T(8,128)(2,1)}, bf16[2,128,256]{2,1,0:T(8,128)(2,1)S(1)}, u32[]{:S(2)}, u32[]{:S(2)}) collective-permute-start(bf16[2,128,256]{2,1,0:T(8,128)(2,1)} %get-tuple-element.19), channel_id=1, source_target_pairs={{0,9},{1,8},{2,11},{3,10},{4,13},{5,12},{6,15},{7,14},{8,1},{9,0},... | collective-permute-start | bytes 393224 | tf_op jit(solution)/shard_map/ppermute | solution.py:53
  12.4 0.4 collective-permute-start.5
  12.7 1.7 %collective-permute-start.1 = (bf16[2,2,128,256]{3,2,1,0:T(8,128)(2,1)}, bf16[2,2,128,256]{3,2,1,0:T(8,128)(2,1)S(1)}, u32[]{:S(2)}, u32[]{:S(2)}) collective-permute-start(bf16[2,2,128,256]{3,2,1,0:T(8,128)(2,1)} %get-tuple-element.14.near_ref), channel_id=1, source_target_pairs={{0,1},{1,0},{2,3},{3,2},{4,5},{5,4},{6,7},{7,6},{8,9},{9,8},{10,11... | collective-permute-start | bytes 786440 | tf_op jit(solution)/shard_map/ppermute | solution.py:43
  14.4 0.0 collective-permute-done.from_cross_ref
  14.4 0.7 %copy-done.5 = bf16[2,2,128,256]{3,2,1,0:T(8,128)(2,1)} copy-done((bf16[2,2,128,256]{3,2,1,0:T(8,128)(2,1)}, bf16[2,2,128,256]{3,2,1,0:T(8,128)(2,1)S(1)}, u32[]{:S(2)}) %copy-start.5) | copy-done | bytes 262168
  15.1 2.0 %rows.1 = (bf16[2,3,128,256]{3,2,1,0:T(8,128)(2,1)}, bf16[2,3,128,256]{3,2,1,0:T(8,128)(2,1)}) custom-call(bf16[2,2,128,256]{3,2,1,0:T(8,128)(2,1)} %get-tuple-element.14.near_ref, bf16[2,2,128,256]{3,2,1,0:T(8,128)(2,1)} %get-tuple-element.15.cross_ref, bf16[2,2,128,256]{3,2,1,0:T(8,128)(2,1)} %copy-done.5), custom_call_target="tpu_custom_call" | custom-call | flops 9200000000 | bytes 29520000 | tf_op jit(solution)/shard_map/rows/pallas_call | solution.py:323
  17.1 0.8 %collective-permute-start.2 = (bf16[2,3,128,256]{3,2,1,0:T(8,128)(2,1)}, bf16[2,3,128,256]{3,2,1,0:T(8,128)(2,1)S(1)}, u32[]{:S(2)}, u32[]{:S(2)}) collective-permute-start(bf16[2,3,128,256]{3,2,1,0:T(8,128)(2,1)} %get-tuple-element.16), channel_id=1, source_target_pairs={{0,8},{1,9},{2,10},{3,11},{4,12},{5,13},{6,14},{7,15},{8,0},{9,1},... | collective-permute-start | bytes 1179656 | tf_op jit(solution)/shard_map/ppermute | solution.py:53
  17.9 0.6 %collective-permute-start.3 = (bf16[2,3,128,256]{3,2,1,0:T(8,128)(2,1)}, bf16[2,3,128,256]{3,2,1,0:T(8,128)(2,1)S(1)}, u32[]{:S(2)}, u32[]{:S(2)}) collective-permute-start(bf16[2,3,128,256]{3,2,1,0:T(8,128)(2,1)} %get-tuple-element.17), channel_id=1, source_target_pairs={{0,1},{1,0},{2,3},{3,2},{4,5},{5,4},{6,7},{7,6},{8,16},{9,17},{10,... | collective-permute-start | bytes 1179656 | tf_op jit(solution)/shard_map/ppermute | solution.py:53
  18.4 7.9 %all-to-all-done = bf16[32,2,16,256]{3,2,1,0:T(8,128)(2,1)S(1)} async-done(((bf16[32,2,16,256]{3,2,1,0:T(8,128)(2,1)}), bf16[32,2,16,256]{3,2,1,0:T(8,128)(2,1)S(1)}, u32[]{:S(2)}, u32[]{:S(2)}) %all-to-all-start) | async-done | bytes 524320 | tf_op jit(solution)/shard_map/all_to_all | solution.py:339
  26.3 2.3 %translations.1 = bf16[8,4,2,16,256]{4,3,2,1,0:T(8,128)(2,1)} custom-call(bf16[8,4,2,16,256]{4,3,2,1,0:T(8,128)(2,1)S(1)} %bitcast.3, f32[32,64]{1,0:T(8,128)S(1)} %bitcast.4), custom_call_target="tpu_custom_call" | custom-call | flops 9200000000 | bytes 29520000 | tf_op jit(solution)/shard_map/translations/pallas_call | solution.py:345
  28.6 3.3 %all-to-all-start.1 = ((bf16[32,2,16,256]{3,2,1,0:T(8,128)(2,1)}), bf16[32,2,16,256]{3,2,1,0:T(8,128)(2,1)S(1)}, u32[]{:S(2)}, u32[]{:S(2)}) async-start(bf16[32,2,16,256]{3,2,1,0:T(8,128)(2,1)} %bitcast.2), calls=%async_computation.1 | async-start | bytes 1048576 | tf_op jit(solution)/shard_map/all_to_all | solution.py:339
  31.9 0.0 copy-start
  31.9 0.0 copy-start.1
  31.9 0.0 collective-permute-done.4.corner_near_ref
  31.9 0.0 collective-permute-done.5.corner_cross_ref
  31.9 0.6 %copy-done.9 = bf16[2,128,256]{2,1,0:T(8,128)(2,1)} copy-done((bf16[2,128,256]{2,1,0:T(8,128)(2,1)}, bf16[2,128,256]{2,1,0:T(8,128)(2,1)S(1)}, u32[]{:S(2)}) %copy-start.9) | copy-done | bytes 131096
  32.6 0.0 collective-permute-done.1.from_near_ref
  32.6 0.7 %copy-done.7 = bf16[2,2,128,256]{3,2,1,0:T(8,128)(2,1)} copy-done((bf16[2,2,128,256]{3,2,1,0:T(8,128)(2,1)}, bf16[2,2,128,256]{3,2,1,0:T(8,128)(2,1)S(1)}, u32[]{:S(2)}) %copy-start.7) | copy-done | bytes 262168
  33.3 0.0 collective-permute-done.2.row_near_ref
  33.3 1.9 %collective-permute-done.3.row_cross_ref = bf16[2,3,128,256]{3,2,1,0:T(8,128)(2,1)S(1)} collective-permute-done((bf16[2,3,128,256]{3,2,1,0:T(8,128)(2,1)}, bf16[2,3,128,256]{3,2,1,0:T(8,128)(2,1)S(1)}, u32[]{:S(2)}, u32[]{:S(2)}) %collective-permute-start.3) | collective-permute-done | bytes 393248 | tf_op jit(solution)/shard_map/ppermute | solution.py:53
  35.2 1.7 %copy-done.2 = bf16[2,2,2,9,128,128]{5,4,3,2,1,0:T(8,128)(2,1)S(1)} copy-done((bf16[2,2,2,9,128,128]{5,4,3,2,1,0:T(8,128)(2,1)S(1)}, bf16[2,2,2,9,128,128]{5,4,3,2,1,0:T(8,128)(2,1)}, u32[]{:S(2)}) %copy-start.2) | copy-done | bytes 2359320
  36.8 0.9 %copy-done.3 = bf16[2,2,128,256]{3,2,1,0:T(8,128)(2,1)S(1)} copy-done((bf16[2,2,128,256]{3,2,1,0:T(8,128)(2,1)S(1)}, bf16[2,2,128,256]{3,2,1,0:T(8,128)(2,1)}, u32[]{:S(2)}) %copy-start.3) | copy-done | bytes 262168
  37.8 0.9 %copy-done.4 = bf16[2,2,128,256]{3,2,1,0:T(8,128)(2,1)S(1)} copy-done((bf16[2,2,128,256]{3,2,1,0:T(8,128)(2,1)S(1)}, bf16[2,2,128,256]{3,2,1,0:T(8,128)(2,1)}, u32[]{:S(2)}) %copy-start.4) | copy-done | bytes 262168
  38.7 0.9 %copy-done.6 = bf16[2,2,128,256]{3,2,1,0:T(8,128)(2,1)S(1)} copy-done((bf16[2,2,128,256]{3,2,1,0:T(8,128)(2,1)S(1)}, bf16[2,2,128,256]{3,2,1,0:T(8,128)(2,1)}, u32[]{:S(2)}) %copy-start.6) | copy-done | bytes 262168
  39.7 0.9 %copy-done.8 = bf16[2,2,128,256]{3,2,1,0:T(8,128)(2,1)S(1)} copy-done((bf16[2,2,128,256]{3,2,1,0:T(8,128)(2,1)S(1)}, bf16[2,2,128,256]{3,2,1,0:T(8,128)(2,1)}, u32[]{:S(2)}) %copy-start.8) | copy-done | bytes 262168
  40.6 0.9 %copy-done.10 = bf16[2,128,256]{2,1,0:T(8,128)(2,1)S(1)} copy-done((bf16[2,128,256]{2,1,0:T(8,128)(2,1)S(1)}, bf16[2,128,256]{2,1,0:T(8,128)(2,1)}, u32[]{:S(2)}) %copy-start.10) | copy-done | bytes 131096
  41.5 2.7 %near.1.near_ref = f32[2,2,2,128,256]{4,3,2,1,0:T(8,128)S(1)} custom-call(bf16[2,2,128,256]{3,2,1,0:T(8,128)(2,1)S(1)} %copy-done.3, bf16[2,2,128,256]{3,2,1,0:T(8,128)(2,1)S(1)} %copy-done.4, bf16[2,2,128,256]{3,2,1,0:T(8,128)(2,1)S(1)} %copy-done.6, bf16[2,2,128,256]{3,2,1,0:T(8,128)(2,1)S(1)} %copy-done.8, ...), custom_call_target="tpu_custom_call" | custom-call | flops 13799999488 | bytes 44280000 | tf_op jit(solution)/shard_map/near/pallas_call | solution.py:373
  44.2 3.2 %all-to-all-done.1.incoming_ref = bf16[32,2,16,256]{3,2,1,0:T(8,128)(2,1)S(1)} async-done(((bf16[32,2,16,256]{3,2,1,0:T(8,128)(2,1)}), bf16[32,2,16,256]{3,2,1,0:T(8,128)(2,1)S(1)}, u32[]{:S(2)}, u32[]{:S(2)}) %all-to-all-start.1) | async-done | bytes 524320 | tf_op jit(solution)/shard_map/all_to_all | solution.py:339
  47.4 1.7 %far.1 = f32[2,2,2,128,256]{4,3,2,1,0:T(8,128)} custom-call(s32[2,2]{1,0:T(2,128)S(1)} %copy-done.1, bf16[32,2,16,256]{3,2,1,0:T(8,128)(2,1)S(1)} %all-to-all-done.1.incoming_ref, bf16[2,2,2,128,512]{4,3,2,1,0:T(8,128)(2,1)S(1)} %copy-done, f32[2,2,2,128,256]{4,3,2,1,0:T(8,128)S(1)} %near.1.near_ref), custom_call_target="tpu_custom_call" | custom-call | tf_op jit(solution)/shard_map/far/pallas_call | solution.py:388
  (13 shorter events, 0.0 us)
Async XLA Ops:
  2.9 11.5 %collective-permute-start = (bf16[2,2,128,256]{3,2,1,0:T(8,128)(2,1)}, bf16[2,2,128,256]{3,2,1,0:T(8,128)(2,1)S(1)}, u32[]{:S(2)}, u32[]{:S(2)}) collective-permute-start(bf16[2,2,128,256]{3,2,1,0:T(8,128)(2,1)} %get-tuple-element.15.cross_ref), channel_id=1, source_target_pairs={{0,8},{1,2},{2,1},{3,4},{4,3},{5,6},{6,5},{7,15},{8,0},{9,10},{10,... | collective-permute-start | bytes 786440 | tf_op jit(solution)/shard_map/ppermute | solution.py:43
  3.4 22.9 %all-to-all-start = ((bf16[32,2,16,256]{3,2,1,0:T(8,128)(2,1)}), bf16[32,2,16,256]{3,2,1,0:T(8,128)(2,1)S(1)}, u32[]{:S(2)}, u32[]{:S(2)}) async-start(bf16[32,2,16,256]{3,2,1,0:T(8,128)(2,1)} %get-tuple-element.13), calls=%async_computation | async-start | bytes 1048576 | tf_op jit(solution)/shard_map/all_to_all | solution.py:339
  10.8 21.1 %collective-permute-start.4 = (bf16[2,128,256]{2,1,0:T(8,128)(2,1)}, bf16[2,128,256]{2,1,0:T(8,128)(2,1)S(1)}, u32[]{:S(2)}, u32[]{:S(2)}) collective-permute-start(bf16[2,128,256]{2,1,0:T(8,128)(2,1)} %get-tuple-element.19), channel_id=1, source_target_pairs={{0,9},{1,8},{2,11},{3,10},{4,13},{5,12},{6,15},{7,14},{8,1},{9,0},... | collective-permute-start | bytes 393224 | tf_op jit(solution)/shard_map/ppermute | solution.py:53
  12.4 19.5 %collective-permute-start.5 = (bf16[2,128,256]{2,1,0:T(8,128)(2,1)}, bf16[2,128,256]{2,1,0:T(8,128)(2,1)S(1)}, u32[]{:S(2)}, u32[]{:S(2)}) collective-permute-start(bf16[2,128,256]{2,1,0:T(8,128)(2,1)} %get-tuple-element.20), channel_id=1, source_target_pairs={{0,1},{1,0},{2,3},{3,2},{4,5},{5,4},{6,7},{7,6},{8,17},{9,16},{10,... | collective-permute-start | bytes 393224 | tf_op jit(solution)/shard_map/ppermute | solution.py:53
  12.7 13.6 %copy-start.11 = (f32[16,2,64]{2,1,0:T(2,128)S(1)}, f32[16,2,64]{2,1,0:T(2,128)}, u32[]{:S(2)}) copy-start(f32[16,2,64]{2,1,0:T(2,128)} %param.11) | copy-start | bytes 24580
  12.7 19.8 %collective-permute-start.1 = (bf16[2,2,128,256]{3,2,1,0:T(8,128)(2,1)}, bf16[2,2,128,256]{3,2,1,0:T(8,128)(2,1)S(1)}, u32[]{:S(2)}, u32[]{:S(2)}) collective-permute-start(bf16[2,2,128,256]{3,2,1,0:T(8,128)(2,1)} %get-tuple-element.14.near_ref), channel_id=1, source_target_pairs={{0,1},{1,0},{2,3},{3,2},{4,5},{5,4},{6,7},{7,6},{8,9},{9,8},{10,11... | collective-permute-start | bytes 786440 | tf_op jit(solution)/shard_map/ppermute | solution.py:43
  14.4 0.7 %copy-start.5 = (bf16[2,2,128,256]{3,2,1,0:T(8,128)(2,1)}, bf16[2,2,128,256]{3,2,1,0:T(8,128)(2,1)S(1)}, u32[]{:S(2)}) copy-start(bf16[2,2,128,256]{3,2,1,0:T(8,128)(2,1)S(1)} %collective-permute-done.from_cross_ref) | copy-start | bytes 786436
  17.1 16.2 %collective-permute-start.2 = (bf16[2,3,128,256]{3,2,1,0:T(8,128)(2,1)}, bf16[2,3,128,256]{3,2,1,0:T(8,128)(2,1)S(1)}, u32[]{:S(2)}, u32[]{:S(2)}) collective-permute-start(bf16[2,3,128,256]{3,2,1,0:T(8,128)(2,1)} %get-tuple-element.16), channel_id=1, source_target_pairs={{0,8},{1,9},{2,10},{3,11},{4,12},{5,13},{6,14},{7,15},{8,0},{9,1},... | collective-permute-start | bytes 1179656 | tf_op jit(solution)/shard_map/ppermute | solution.py:53
  17.9 17.3 %collective-permute-start.3 = (bf16[2,3,128,256]{3,2,1,0:T(8,128)(2,1)}, bf16[2,3,128,256]{3,2,1,0:T(8,128)(2,1)S(1)}, u32[]{:S(2)}, u32[]{:S(2)}) collective-permute-start(bf16[2,3,128,256]{3,2,1,0:T(8,128)(2,1)} %get-tuple-element.17), channel_id=1, source_target_pairs={{0,1},{1,0},{2,3},{3,2},{4,5},{5,4},{6,7},{7,6},{8,16},{9,17},{10,... | collective-permute-start | bytes 1179656 | tf_op jit(solution)/shard_map/ppermute | solution.py:53
  28.6 18.8 %all-to-all-start.1 = ((bf16[32,2,16,256]{3,2,1,0:T(8,128)(2,1)}), bf16[32,2,16,256]{3,2,1,0:T(8,128)(2,1)S(1)}, u32[]{:S(2)}, u32[]{:S(2)}) async-start(bf16[32,2,16,256]{3,2,1,0:T(8,128)(2,1)} %bitcast.2), calls=%async_computation.1 | async-start | bytes 1048576 | tf_op jit(solution)/shard_map/all_to_all | solution.py:339
  31.9 15.5 %copy-start = (bf16[2,2,2,128,512]{4,3,2,1,0:T(8,128)(2,1)S(1)}, bf16[2,2,2,128,512]{4,3,2,1,0:T(8,128)(2,1)}, u32[]{:S(2)}) copy-start(bf16[2,2,2,128,512]{4,3,2,1,0:T(8,128)(2,1)} %disaggregate_ref.1) | copy-start | bytes 3145732
  31.9 15.5 %copy-start.1 = (s32[2,2]{1,0:T(2,128)S(1)}, s32[2,2]{1,0:T(2,128)}, u32[]{:S(2)}) copy-start(s32[2,2]{1,0:T(2,128)} %live_ref.3) | copy-start | bytes 52
  31.9 0.6 %copy-start.9 = (bf16[2,128,256]{2,1,0:T(8,128)(2,1)}, bf16[2,128,256]{2,1,0:T(8,128)(2,1)S(1)}, u32[]{:S(2)}) copy-start(bf16[2,128,256]{2,1,0:T(8,128)(2,1)S(1)} %collective-permute-done.5.corner_cross_ref) | copy-start | bytes 393220
  32.6 0.7 %copy-start.7 = (bf16[2,2,128,256]{3,2,1,0:T(8,128)(2,1)}, bf16[2,2,128,256]{3,2,1,0:T(8,128)(2,1)S(1)}, u32[]{:S(2)}) copy-start(bf16[2,2,128,256]{3,2,1,0:T(8,128)(2,1)S(1)} %collective-permute-done.1.from_near_ref) | copy-start | bytes 786436
  35.2 1.7 %copy-start.2 = (bf16[2,2,2,9,128,128]{5,4,3,2,1,0:T(8,128)(2,1)S(1)}, bf16[2,2,2,9,128,128]{5,4,3,2,1,0:T(8,128)(2,1)}, u32[]{:S(2)}) copy-start(bf16[2,2,2,9,128,128]{5,4,3,2,1,0:T(8,128)(2,1)} %blocks_ref.1) | copy-start | bytes 7077892
  36.8 0.9 %copy-start.3 = (bf16[2,2,128,256]{3,2,1,0:T(8,128)(2,1)S(1)}, bf16[2,2,128,256]{3,2,1,0:T(8,128)(2,1)}, u32[]{:S(2)}) copy-start(bf16[2,2,128,256]{3,2,1,0:T(8,128)(2,1)} %get-tuple-element.14.near_ref) | copy-start | bytes 786436
  37.8 0.9 %copy-start.4 = (bf16[2,2,128,256]{3,2,1,0:T(8,128)(2,1)S(1)}, bf16[2,2,128,256]{3,2,1,0:T(8,128)(2,1)}, u32[]{:S(2)}) copy-start(bf16[2,2,128,256]{3,2,1,0:T(8,128)(2,1)} %get-tuple-element.15.cross_ref) | copy-start | bytes 786436
  38.7 0.9 %copy-start.6 = (bf16[2,2,128,256]{3,2,1,0:T(8,128)(2,1)S(1)}, bf16[2,2,128,256]{3,2,1,0:T(8,128)(2,1)}, u32[]{:S(2)}) copy-start(bf16[2,2,128,256]{3,2,1,0:T(8,128)(2,1)} %copy-done.5) | copy-start | bytes 786436
  39.7 0.9 %copy-start.8 = (bf16[2,2,128,256]{3,2,1,0:T(8,128)(2,1)S(1)}, bf16[2,2,128,256]{3,2,1,0:T(8,128)(2,1)}, u32[]{:S(2)}) copy-start(bf16[2,2,128,256]{3,2,1,0:T(8,128)(2,1)} %copy-done.7) | copy-start | bytes 786436
  40.6 0.9 %copy-start.10 = (bf16[2,128,256]{2,1,0:T(8,128)(2,1)S(1)}, bf16[2,128,256]{2,1,0:T(8,128)(2,1)}, u32[]{:S(2)}) copy-start(bf16[2,128,256]{2,1,0:T(8,128)(2,1)} %copy-done.9) | copy-start | bytes 393220

commit v8 on v7

--- a/solution.py
+++ b/solution.py
@@ -256,15 +256,10 @@
 
 def far_kernel(
     live_ref, incoming_ref, disaggregate_ref, near_ref, out_ref, live_here, right_ref, made_ref, live_sem,
-    in_sem, out_sem,
+    out_sem,
 ):
     parts, _, narrow, sides = incoming_ref.shape
     deep, wide = live_ref.shape
-
-    def arrival(c):
-        return pltpu.make_async_copy(
-            incoming_ref.at[:, c], right_ref.at[:, :, c * sides : (c + 1) * sides], in_sem.at[c]
-        )
 
     def departure(u, v):
         return pltpu.make_async_copy(
@@ -274,10 +269,8 @@
     live_copy = pltpu.make_async_copy(live_ref, live_here, live_sem)
     live_copy.start()
     for c in range(2):
-        arrival(c).start()
+        right_ref[:, :, c * sides : (c + 1) * sides] = incoming_ref[:, c]
     live_copy.wait()
-    for c in range(2):
-        arrival(c).wait()
     right = right_ref[...].reshape(parts * narrow, 2 * sides)
     for u in range(deep):
         for v in range(wide):
@@ -387,7 +380,7 @@
     )
     return pl.pallas_call(
         far_kernel,
-        in_specs=[ANY, ANY, VMEM, VMEM],
+        in_specs=[ANY, VMEM, VMEM, VMEM],
         out_specs=ANY,
         out_shape=field,
         scratch_shapes=[
@@ -395,7 +388,6 @@
             pltpu.VMEM((parts, block, 2 * sides), bf16),
             pltpu.VMEM(unknowns.shape, f32),
             pltpu.SemaphoreType.DMA,
-            pltpu.SemaphoreType.DMA((2,)),
             pltpu.SemaphoreType.DMA((deep, wide)),
         ],
         compiler_params=params(16),

time: 49.6 us -> 49.5 us (level)
  no operation moved by 1% of the time
where the time goes in v8:
time: 49.5 us; the launch traced here: 49.1 us
  starting transfers between devices  16.1 us (33%)
  waiting for transfers between devices  13 us (26%)
  Pallas kernels  11.5 us (23%)
  local copies, waits for them, and re-layouts  8.41 us (17%)
    all_to_all x2, waiting for transfers between devices, spread(): lax.all_to_all(flat, ('dir', 'sect'), split_axis=0, concat_axis=0, tiled=...  11.1 us
    all_to_all x2, starting transfers between devices, spread(): lax.all_to_all(flat, ('dir', 'sect'), split_axis=0, concat_axis=0, tiled=...  10.6 us
    unnamed x24, local copies, waits for them, and re-layouts  8.41 us
    ppermute x4, starting transfers between devices, swap_rows(): return lax.ppermute(array, ('sect', 'dir'), sends)  3.31 us
    pallas_call x1, Pallas kernels, shards(): pl.pallas_call(pattern_kernel, in_specs=[pl.BlockSpec(memory_space=pltpu....  2.94 us
    pallas_call x1, Pallas kernels, shards(): pl.pallas_call(near_kernel, grid=(deep * wide,), in_specs=[VMEM] * 8 + [p...  2.66 us
    pallas_call x1, Pallas kernels, shards(): pl.pallas_call(translate_kernel, in_specs=[VMEM] * 2, out_specs=VMEM, out...  2.28 us
    ppermute x2, starting transfers between devices, swap_cols(): return lax.ppermute(array, ('sect', 'dir'), sends)  2.12 us
  transfers between devices with their start and end apart: 8, of which 3 were waited for; matrix products, arithmetic and copies ran while one was open for 0% of the time, Pallas kernels for 14%

profile of v8, /device:TPU:0, one launch (start us, length us, event | category | flops | bytes accessed | tf_op | source)
XLA Modules:
  0.0 49.1 jit_solution(14698500004281678710)
XLA Ops:
  0.0 2.9 %patterns.1 = (bf16[32,2,16,256]{3,2,1,0:T(8,128)(2,1)}, bf16[2,2,128,256]{3,2,1,0:T(8,128)(2,1)}, bf16[2,2,128,256]{3,2,1,0:T(8,128)(2,1)}, bf16[2,128,256]{2,1,0:T(8,128)(2,1)}, bf16[2,128,256]{2,1,0:T(8,128)(2,1)}) custom-call(s32[2,2]{1,0:T(2,128)} %live_ref.3, bf16[2,2,2,128,256]{4,3,2,1,0:T(8,128)(2,1)} %unknowns_ref.1, ...), custom_call_target="tpu_custom_call" | custom-call | tf_op jit(solution)/shard_map/patterns/pallas_call | solution.py:301
  2.9 0.5 collective-permute-start
  3.4 7.4 %all-to-all-start = ((bf16[32,2,16,256]{3,2,1,0:T(8,128)(2,1)}), bf16[32,2,16,256]{3,2,1,0:T(8,128)(2,1)S(1)}, u32[]{:S(2)}, u32[]{:S(2)}) async-start(bf16[32,2,16,256]{3,2,1,0:T(8,128)(2,1)} %get-tuple-element.13), calls=%async_computation | async-start | bytes 1048576 | tf_op jit(solution)/shard_map/all_to_all | solution.py:332
  10.8 1.6 %collective-permute-start.4 = (bf16[2,128,256]{2,1,0:T(8,128)(2,1)}, bf16[2,128,256]{2,1,0:T(8,128)(2,1)S(1)}, u32[]{:S(2)}, u32[]{:S(2)}) collective-permute-start(bf16[2,128,256]{2,1,0:T(8,128)(2,1)} %get-tuple-element.19), channel_id=1, source_target_pairs={{0,9},{1,8},{2,11},{3,10},{4,13},{5,12},{6,15},{7,14},{8,1},{9,0},... | collective-permute-start | bytes 393224 | tf_op jit(solution)/shard_map/ppermute | solution.py:53
  12.4 0.4 collective-permute-start.5
  12.7 1.7 %collective-permute-start.1 = (bf16[2,2,128,256]{3,2,1,0:T(8,128)(2,1)}, bf16[2,2,128,256]{3,2,1,0:T(8,128)(2,1)S(1)}, u32[]{:S(2)}, u32[]{:S(2)}) collective-permute-start(bf16[2,2,128,256]{3,2,1,0:T(8,128)(2,1)} %get-tuple-element.14.near_ref), channel_id=1, source_target_pairs={{0,1},{1,0},{2,3},{3,2},{4,5},{5,4},{6,7},{7,6},{8,9},{9,8},{10,11... | collective-permute-start | bytes 786440 | tf_op jit(solution)/shard_map/ppermute | solution.py:43
  14.4 0.0 collective-permute-done.from_cross_ref
  14.4 0.7 %copy-done.5 = bf16[2,2,128,256]{3,2,1,0:T(8,128)(2,1)} copy-done((bf16[2,2,128,256]{3,2,1,0:T(8,128)(2,1)}, bf16[2,2,128,256]{3,2,1,0:T(8,128)(2,1)S(1)}, u32[]{:S(2)}) %copy-start.5) | copy-done | bytes 262168
  15.1 2.0 %rows.1 = (bf16[2,3,128,256]{3,2,1,0:T(8,128)(2,1)}, bf16[2,3,128,256]{3,2,1,0:T(8,128)(2,1)}) custom-call(bf16[2,2,128,256]{3,2,1,0:T(8,128)(2,1)} %get-tuple-element.14.near_ref, bf16[2,2,128,256]{3,2,1,0:T(8,128)(2,1)} %get-tuple-element.15.cross_ref, bf16[2,2,128,256]{3,2,1,0:T(8,128)(2,1)} %copy-done.5), custom_call_target="tpu_custom_call" | custom-call | flops 9200000000 | bytes 29520000 | tf_op jit(solution)/shard_map/rows/pallas_call | solution.py:316
  17.1 0.8 %collective-permute-start.2 = (bf16[2,3,128,256]{3,2,1,0:T(8,128)(2,1)}, bf16[2,3,128,256]{3,2,1,0:T(8,128)(2,1)S(1)}, u32[]{:S(2)}, u32[]{:S(2)}) collective-permute-start(bf16[2,3,128,256]{3,2,1,0:T(8,128)(2,1)} %get-tuple-element.16), channel_id=1, source_target_pairs={{0,8},{1,9},{2,10},{3,11},{4,12},{5,13},{6,14},{7,15},{8,0},{9,1},... | collective-permute-start | bytes 1179656 | tf_op jit(solution)/shard_map/ppermute | solution.py:53
  17.9 0.6 %collective-permute-start.3 = (bf16[2,3,128,256]{3,2,1,0:T(8,128)(2,1)}, bf16[2,3,128,256]{3,2,1,0:T(8,128)(2,1)S(1)}, u32[]{:S(2)}, u32[]{:S(2)}) collective-permute-start(bf16[2,3,128,256]{3,2,1,0:T(8,128)(2,1)} %get-tuple-element.17), channel_id=1, source_target_pairs={{0,1},{1,0},{2,3},{3,2},{4,5},{5,4},{6,7},{7,6},{8,16},{9,17},{10,... | collective-permute-start | bytes 1179656 | tf_op jit(solution)/shard_map/ppermute | solution.py:53
  18.4 7.9 %all-to-all-done = bf16[32,2,16,256]{3,2,1,0:T(8,128)(2,1)S(1)} async-done(((bf16[32,2,16,256]{3,2,1,0:T(8,128)(2,1)}), bf16[32,2,16,256]{3,2,1,0:T(8,128)(2,1)S(1)}, u32[]{:S(2)}, u32[]{:S(2)}) %all-to-all-start) | async-done | bytes 524320 | tf_op jit(solution)/shard_map/all_to_all | solution.py:332
  26.3 2.3 %translations.1 = bf16[8,4,2,16,256]{4,3,2,1,0:T(8,128)(2,1)} custom-call(bf16[8,4,2,16,256]{4,3,2,1,0:T(8,128)(2,1)S(1)} %bitcast.3, f32[32,64]{1,0:T(8,128)S(1)} %bitcast.4), custom_call_target="tpu_custom_call" | custom-call | flops 9200000000 | bytes 29520000 | tf_op jit(solution)/shard_map/translations/pallas_call | solution.py:338
  28.6 3.3 %all-to-all-start.1 = ((bf16[32,2,16,256]{3,2,1,0:T(8,128)(2,1)}), bf16[32,2,16,256]{3,2,1,0:T(8,128)(2,1)S(1)}, u32[]{:S(2)}, u32[]{:S(2)}) async-start(bf16[32,2,16,256]{3,2,1,0:T(8,128)(2,1)} %bitcast.2), calls=%async_computation.1 | async-start | bytes 1048576 | tf_op jit(solution)/shard_map/all_to_all | solution.py:332
  31.9 0.0 copy-start
  31.9 0.0 copy-start.1
  31.9 0.0 collective-permute-done.4.corner_near_ref
  31.9 0.0 collective-permute-done.5.corner_cross_ref
  31.9 0.6 %copy-done.9 = bf16[2,128,256]{2,1,0:T(8,128)(2,1)} copy-done((bf16[2,128,256]{2,1,0:T(8,128)(2,1)}, bf16[2,128,256]{2,1,0:T(8,128)(2,1)S(1)}, u32[]{:S(2)}) %copy-start.9) | copy-done | bytes 131096
  32.6 0.0 collective-permute-done.1.from_near_ref
  32.6 0.7 %copy-done.7 = bf16[2,2,128,256]{3,2,1,0:T(8,128)(2,1)} copy-done((bf16[2,2,128,256]{3,2,1,0:T(8,128)(2,1)}, bf16[2,2,128,256]{3,2,1,0:T(8,128)(2,1)S(1)}, u32[]{:S(2)}) %copy-start.7) | copy-done | bytes 262168
  33.3 0.0 collective-permute-done.2.row_near_ref
  33.3 1.9 %collective-permute-done.3.row_cross_ref = bf16[2,3,128,256]{3,2,1,0:T(8,128)(2,1)S(1)} collective-permute-done((bf16[2,3,128,256]{3,2,1,0:T(8,128)(2,1)}, bf16[2,3,128,256]{3,2,1,0:T(8,128)(2,1)S(1)}, u32[]{:S(2)}, u32[]{:S(2)}) %collective-permute-start.3) | collective-permute-done | bytes 393248 | tf_op jit(solution)/shard_map/ppermute | solution.py:53
  35.2 1.7 %copy-done.2 = bf16[2,2,2,9,128,128]{5,4,3,2,1,0:T(8,128)(2,1)S(1)} copy-done((bf16[2,2,2,9,128,128]{5,4,3,2,1,0:T(8,128)(2,1)S(1)}, bf16[2,2,2,9,128,128]{5,4,3,2,1,0:T(8,128)(2,1)}, u32[]{:S(2)}) %copy-start.2) | copy-done | bytes 2359320
  36.8 0.9 %copy-done.3 = bf16[2,2,128,256]{3,2,1,0:T(8,128)(2,1)S(1)} copy-done((bf16[2,2,128,256]{3,2,1,0:T(8,128)(2,1)S(1)}, bf16[2,2,128,256]{3,2,1,0:T(8,128)(2,1)}, u32[]{:S(2)}) %copy-start.3) | copy-done | bytes 262168
  37.8 0.9 %copy-done.4 = bf16[2,2,128,256]{3,2,1,0:T(8,128)(2,1)S(1)} copy-done((bf16[2,2,128,256]{3,2,1,0:T(8,128)(2,1)S(1)}, bf16[2,2,128,256]{3,2,1,0:T(8,128)(2,1)}, u32[]{:S(2)}) %copy-start.4) | copy-done | bytes 262168
  38.7 0.9 %copy-done.6 = bf16[2,2,128,256]{3,2,1,0:T(8,128)(2,1)S(1)} copy-done((bf16[2,2,128,256]{3,2,1,0:T(8,128)(2,1)S(1)}, bf16[2,2,128,256]{3,2,1,0:T(8,128)(2,1)}, u32[]{:S(2)}) %copy-start.6) | copy-done | bytes 262168
  39.7 0.9 %copy-done.8 = bf16[2,2,128,256]{3,2,1,0:T(8,128)(2,1)S(1)} copy-done((bf16[2,2,128,256]{3,2,1,0:T(8,128)(2,1)S(1)}, bf16[2,2,128,256]{3,2,1,0:T(8,128)(2,1)}, u32[]{:S(2)}) %copy-start.8) | copy-done | bytes 262168
  40.6 0.9 %copy-done.10 = bf16[2,128,256]{2,1,0:T(8,128)(2,1)S(1)} copy-done((bf16[2,128,256]{2,1,0:T(8,128)(2,1)S(1)}, bf16[2,128,256]{2,1,0:T(8,128)(2,1)}, u32[]{:S(2)}) %copy-start.10) | copy-done | bytes 131096
  41.5 2.7 %near.1.near_ref = f32[2,2,2,128,256]{4,3,2,1,0:T(8,128)S(1)} custom-call(bf16[2,2,128,256]{3,2,1,0:T(8,128)(2,1)S(1)} %copy-done.3, bf16[2,2,128,256]{3,2,1,0:T(8,128)(2,1)S(1)} %copy-done.4, bf16[2,2,128,256]{3,2,1,0:T(8,128)(2,1)S(1)} %copy-done.6, bf16[2,2,128,256]{3,2,1,0:T(8,128)(2,1)S(1)} %copy-done.8, ...), custom_call_target="tpu_custom_call" | custom-call | flops 13799999488 | bytes 44280000 | tf_op jit(solution)/shard_map/near/pallas_call | solution.py:366
  44.2 3.2 %all-to-all-done.1.incoming_ref = bf16[32,2,16,256]{3,2,1,0:T(8,128)(2,1)S(1)} async-done(((bf16[32,2,16,256]{3,2,1,0:T(8,128)(2,1)}), bf16[32,2,16,256]{3,2,1,0:T(8,128)(2,1)S(1)}, u32[]{:S(2)}, u32[]{:S(2)}) %all-to-all-start.1) | async-done | bytes 524320 | tf_op jit(solution)/shard_map/all_to_all | solution.py:332
  47.4 1.6 %far.1 = f32[2,2,2,128,256]{4,3,2,1,0:T(8,128)} custom-call(s32[2,2]{1,0:T(2,128)S(1)} %copy-done.1, bf16[32,2,16,256]{3,2,1,0:T(8,128)(2,1)S(1)} %all-to-all-done.1.incoming_ref, bf16[2,2,2,128,512]{4,3,2,1,0:T(8,128)(2,1)S(1)} %copy-done, f32[2,2,2,128,256]{4,3,2,1,0:T(8,128)S(1)} %near.1.near_ref), custom_call_target="tpu_custom_call" | custom-call | tf_op jit(solution)/shard_map/far/pallas_call | solution.py:381
  (13 shorter events, 0.0 us)
Async XLA Ops:
  2.9 11.5 %collective-permute-start = (bf16[2,2,128,256]{3,2,1,0:T(8,128)(2,1)}, bf16[2,2,128,256]{3,2,1,0:T(8,128)(2,1)S(1)}, u32[]{:S(2)}, u32[]{:S(2)}) collective-permute-start(bf16[2,2,128,256]{3,2,1,0:T(8,128)(2,1)} %get-tuple-element.15.cross_ref), channel_id=1, source_target_pairs={{0,8},{1,2},{2,1},{3,4},{4,3},{5,6},{6,5},{7,15},{8,0},{9,10},{10,... | collective-permute-start | bytes 786440 | tf_op jit(solution)/shard_map/ppermute | solution.py:43
  3.4 22.9 %all-to-all-start = ((bf16[32,2,16,256]{3,2,1,0:T(8,128)(2,1)}), bf16[32,2,16,256]{3,2,1,0:T(8,128)(2,1)S(1)}, u32[]{:S(2)}, u32[]{:S(2)}) async-start(bf16[32,2,16,256]{3,2,1,0:T(8,128)(2,1)} %get-tuple-element.13), calls=%async_computation | async-start | bytes 1048576 | tf_op jit(solution)/shard_map/all_to_all | solution.py:332
  10.8 21.1 %collective-permute-start.4 = (bf16[2,128,256]{2,1,0:T(8,128)(2,1)}, bf16[2,128,256]{2,1,0:T(8,128)(2,1)S(1)}, u32[]{:S(2)}, u32[]{:S(2)}) collective-permute-start(bf16[2,128,256]{2,1,0:T(8,128)(2,1)} %get-tuple-element.19), channel_id=1, source_target_pairs={{0,9},{1,8},{2,11},{3,10},{4,13},{5,12},{6,15},{7,14},{8,1},{9,0},... | collective-permute-start | bytes 393224 | tf_op jit(solution)/shard_map/ppermute | solution.py:53
  12.4 19.5 %collective-permute-start.5 = (bf16[2,128,256]{2,1,0:T(8,128)(2,1)}, bf16[2,128,256]{2,1,0:T(8,128)(2,1)S(1)}, u32[]{:S(2)}, u32[]{:S(2)}) collective-permute-start(bf16[2,128,256]{2,1,0:T(8,128)(2,1)} %get-tuple-element.20), channel_id=1, source_target_pairs={{0,1},{1,0},{2,3},{3,2},{4,5},{5,4},{6,7},{7,6},{8,17},{9,16},{10,... | collective-permute-start | bytes 393224 | tf_op jit(solution)/shard_map/ppermute | solution.py:53
  12.7 13.6 %copy-start.11 = (f32[16,2,64]{2,1,0:T(2,128)S(1)}, f32[16,2,64]{2,1,0:T(2,128)}, u32[]{:S(2)}) copy-start(f32[16,2,64]{2,1,0:T(2,128)} %param.11) | copy-start | bytes 24580
  12.7 19.8 %collective-permute-start.1 = (bf16[2,2,128,256]{3,2,1,0:T(8,128)(2,1)}, bf16[2,2,128,256]{3,2,1,0:T(8,128)(2,1)S(1)}, u32[]{:S(2)}, u32[]{:S(2)}) collective-permute-start(bf16[2,2,128,256]{3,2,1,0:T(8,128)(2,1)} %get-tuple-element.14.near_ref), channel_id=1, source_target_pairs={{0,1},{1,0},{2,3},{3,2},{4,5},{5,4},{6,7},{7,6},{8,9},{9,8},{10,11... | collective-permute-start | bytes 786440 | tf_op jit(solution)/shard_map/ppermute | solution.py:43
  14.4 0.7 %copy-start.5 = (bf16[2,2,128,256]{3,2,1,0:T(8,128)(2,1)}, bf16[2,2,128,256]{3,2,1,0:T(8,128)(2,1)S(1)}, u32[]{:S(2)}) copy-start(bf16[2,2,128,256]{3,2,1,0:T(8,128)(2,1)S(1)} %collective-permute-done.from_cross_ref) | copy-start | bytes 786436
  17.1 16.2 %collective-permute-start.2 = (bf16[2,3,128,256]{3,2,1,0:T(8,128)(2,1)}, bf16[2,3,128,256]{3,2,1,0:T(8,128)(2,1)S(1)}, u32[]{:S(2)}, u32[]{:S(2)}) collective-permute-start(bf16[2,3,128,256]{3,2,1,0:T(8,128)(2,1)} %get-tuple-element.16), channel_id=1, source_target_pairs={{0,8},{1,9},{2,10},{3,11},{4,12},{5,13},{6,14},{7,15},{8,0},{9,1},... | collective-permute-start | bytes 1179656 | tf_op jit(solution)/shard_map/ppermute | solution.py:53
  17.9 17.3 %collective-permute-start.3 = (bf16[2,3,128,256]{3,2,1,0:T(8,128)(2,1)}, bf16[2,3,128,256]{3,2,1,0:T(8,128)(2,1)S(1)}, u32[]{:S(2)}, u32[]{:S(2)}) collective-permute-start(bf16[2,3,128,256]{3,2,1,0:T(8,128)(2,1)} %get-tuple-element.17), channel_id=1, source_target_pairs={{0,1},{1,0},{2,3},{3,2},{4,5},{5,4},{6,7},{7,6},{8,16},{9,17},{10,... | collective-permute-start | bytes 1179656 | tf_op jit(solution)/shard_map/ppermute | solution.py:53
  28.6 18.8 %all-to-all-start.1 = ((bf16[32,2,16,256]{3,2,1,0:T(8,128)(2,1)}), bf16[32,2,16,256]{3,2,1,0:T(8,128)(2,1)S(1)}, u32[]{:S(2)}, u32[]{:S(2)}) async-start(bf16[32,2,16,256]{3,2,1,0:T(8,128)(2,1)} %bitcast.2), calls=%async_computation.1 | async-start | bytes 1048576 | tf_op jit(solution)/shard_map/all_to_all | solution.py:332
  31.9 15.5 %copy-start = (bf16[2,2,2,128,512]{4,3,2,1,0:T(8,128)(2,1)S(1)}, bf16[2,2,2,128,512]{4,3,2,1,0:T(8,128)(2,1)}, u32[]{:S(2)}) copy-start(bf16[2,2,2,128,512]{4,3,2,1,0:T(8,128)(2,1)} %disaggregate_ref.1) | copy-start | bytes 3145732
  31.9 15.5 %copy-start.1 = (s32[2,2]{1,0:T(2,128)S(1)}, s32[2,2]{1,0:T(2,128)}, u32[]{:S(2)}) copy-start(s32[2,2]{1,0:T(2,128)} %live_ref.3) | copy-start | bytes 52
  31.9 0.6 %copy-start.9 = (bf16[2,128,256]{2,1,0:T(8,128)(2,1)}, bf16[2,128,256]{2,1,0:T(8,128)(2,1)S(1)}, u32[]{:S(2)}) copy-start(bf16[2,128,256]{2,1,0:T(8,128)(2,1)S(1)} %collective-permute-done.5.corner_cross_ref) | copy-start | bytes 393220
  32.6 0.7 %copy-start.7 = (bf16[2,2,128,256]{3,2,1,0:T(8,128)(2,1)}, bf16[2,2,128,256]{3,2,1,0:T(8,128)(2,1)S(1)}, u32[]{:S(2)}) copy-start(bf16[2,2,128,256]{3,2,1,0:T(8,128)(2,1)S(1)} %collective-permute-done.1.from_near_ref) | copy-start | bytes 786436
  35.2 1.7 %copy-start.2 = (bf16[2,2,2,9,128,128]{5,4,3,2,1,0:T(8,128)(2,1)S(1)}, bf16[2,2,2,9,128,128]{5,4,3,2,1,0:T(8,128)(2,1)}, u32[]{:S(2)}) copy-start(bf16[2,2,2,9,128,128]{5,4,3,2,1,0:T(8,128)(2,1)} %blocks_ref.1) | copy-start | bytes 7077892
  36.8 0.9 %copy-start.3 = (bf16[2,2,128,256]{3,2,1,0:T(8,128)(2,1)S(1)}, bf16[2,2,128,256]{3,2,1,0:T(8,128)(2,1)}, u32[]{:S(2)}) copy-start(bf16[2,2,128,256]{3,2,1,0:T(8,128)(2,1)} %get-tuple-element.14.near_ref) | copy-start | bytes 786436
  37.8 0.9 %copy-start.4 = (bf16[2,2,128,256]{3,2,1,0:T(8,128)(2,1)S(1)}, bf16[2,2,128,256]{3,2,1,0:T(8,128)(2,1)}, u32[]{:S(2)}) copy-start(bf16[2,2,128,256]{3,2,1,0:T(8,128)(2,1)} %get-tuple-element.15.cross_ref) | copy-start | bytes 786436
  38.7 0.9 %copy-start.6 = (bf16[2,2,128,256]{3,2,1,0:T(8,128)(2,1)S(1)}, bf16[2,2,128,256]{3,2,1,0:T(8,128)(2,1)}, u32[]{:S(2)}) copy-start(bf16[2,2,128,256]{3,2,1,0:T(8,128)(2,1)} %copy-done.5) | copy-start | bytes 786436
  39.7 0.9 %copy-start.8 = (bf16[2,2,128,256]{3,2,1,0:T(8,128)(2,1)S(1)}, bf16[2,2,128,256]{3,2,1,0:T(8,128)(2,1)}, u32[]{:S(2)}) copy-start(bf16[2,2,128,256]{3,2,1,0:T(8,128)(2,1)} %copy-done.7) | copy-start | bytes 786436
  40.6 0.9 %copy-start.10 = (bf16[2,128,256]{2,1,0:T(8,128)(2,1)S(1)}, bf16[2,128,256]{2,1,0:T(8,128)(2,1)}, u32[]{:S(2)}) copy-start(bf16[2,128,256]{2,1,0:T(8,128)(2,1)} %copy-done.9) | copy-start | bytes 393220

commit v9 on v8

--- a/solution.py
+++ b/solution.py
@@ -104,10 +104,8 @@
         corner_cross_ref[c] = leaf(row_odd, 1 - odd, c)
 
 
-def translate_kernel(from_ref, coef_ref, out_ref, turned_ref, wide_ref, held_ref):
-    box_cols, box_rows, _, narrow, sides = from_ref.shape
-    lanes = min(128, sides)
-
+def coefficient_kernel(coef_ref, wide_ref, turned_ref):
+    _, _, narrow, lanes = wide_ref.shape
     turned_ref[...] = coef_ref[...].T
     first = pl.multiple_of(lax.axis_index("sect") * narrow, narrow)
     coefs = turned_ref[pl.ds(first, narrow)]
@@ -118,6 +116,11 @@
         wide_ref[index, 0] = real
         wide_ref[index, 1] = imag
         wide_ref[index, 2] = real + imag
+
+
+def translate_kernel(from_ref, wide_ref, out_ref, held_ref):
+    box_cols, box_rows, _, narrow, sides = from_ref.shape
+    lanes = min(128, sides)
 
     def tile(place, carry):
         across = pl.ds(pl.multiple_of(place * lanes, lanes), lanes)
@@ -333,22 +336,30 @@
 
     if tiled:
         own = spread(patterns).reshape(dir_count, sect_count, 2, block, sides)
-        own, _, _ = lax.optimization_barrier((own, row_near, row_cross))
         lanes = min(128, sides)
+        coefs, _ = lax.optimization_barrier((translate, row_cross))
+        wide_coefs = pl.pallas_call(
+            coefficient_kernel,
+            in_specs=[VMEM],
+            out_specs=VMEM,
+            out_shape=jax.ShapeDtypeStruct((len(far_offsets), 3, narrow, lanes), f32),
+            scratch_shapes=[pltpu.VMEM((held, 2 * len(far_offsets)), f32)],
+            compiler_params=params(16),
+            name="coefficients",
+        )(coefs.reshape(2 * len(far_offsets), held))
+        own, _, _, wide_coefs = lax.optimization_barrier((own, row_near, row_cross, wide_coefs))
         incoming = pl.pallas_call(
             translate_kernel,
             in_specs=[VMEM] * 2,
             out_specs=VMEM,
             out_shape=jax.ShapeDtypeStruct(own.shape, bf16),
             scratch_shapes=[
-                pltpu.VMEM((held, 2 * len(far_offsets)), f32),
-                pltpu.VMEM((len(far_offsets), 3, narrow, lanes), f32),
                 pltpu.VMEM((dir_count, sect_count, 3, narrow, lanes), f32),
             ],
             compiler_params=params(16),
             cost_estimate=cost(8),
             name="translations",
-        )(own, translate.reshape(2 * len(far_offsets), held))
+        )(own, wide_coefs)
         returned = spread(incoming)
     else:
         base = patterns.reshape(2, dir_count, sect_count, narrow, sides).transpose(0, 2, 1, 3, 4)

time: 49.5 us -> 49.3 us (level)
  waiting for transfers between devices: 13 us -> 12.4 us
    all_to_all x2, waiting for transfers between devices: 11.1 us -> 10 us  [spread(): lax.all_to_all(flat, ('dir', 'sect'), split_axis=0, concat_axis=0, tiled=...]
    ppermute x4, waiting for transfers between devices: 1.89 us -> 2.41 us  [swap_rows(): return lax.ppermute(array, ('sect', 'dir'), sends)]
where the time goes in v9:
time: 49.3 us; the launch traced here: 48.8 us
  starting transfers between devices  16.4 us (33%)
  waiting for transfers between devices  12.4 us (25%)
  Pallas kernels  11.5 us (23%)
  local copies, waits for them, and re-layouts  8.41 us (17%)
    all_to_all x2, starting transfers between devices, spread(): lax.all_to_all(flat, ('dir', 'sect'), split_axis=0, concat_axis=0, tiled=...  10.6 us
    all_to_all x2, waiting for transfers between devices, spread(): lax.all_to_all(flat, ('dir', 'sect'), split_axis=0, concat_axis=0, tiled=...  10 us
    unnamed x24, local copies, waits for them, and re-layouts  8.41 us
    ppermute x4, starting transfers between devices, swap_rows(): return lax.ppermute(array, ('sect', 'dir'), sends)  3.62 us
    pallas_call x1, Pallas kernels, shards(): pl.pallas_call(pattern_kernel, in_specs=[pl.BlockSpec(memory_space=pltpu....  2.94 us
    pallas_call x1, Pallas kernels, shards(): pl.pallas_call(near_kernel, grid=(deep * wide,), in_specs=[VMEM] * 8 + [p...  2.66 us
    ppermute x4, waiting for transfers between devices, swap_rows(): return lax.ppermute(array, ('sect', 'dir'), sends)  2.41 us
    ppermute x2, starting transfers between devices, swap_cols(): return lax.ppermute(array, ('sect', 'dir'), sends)  2.12 us
  transfers between devices with their start and end apart: 8, of which 3 were waited for; matrix products, arithmetic and copies ran while one was open for 0% of the time, Pallas kernels for 14%

profile of v9, /device:TPU:0, one launch (start us, length us, event | category | flops | bytes accessed | tf_op | source)
XLA Modules:
  0.0 48.8 jit_solution(67504229334575728)
XLA Ops:
  0.0 2.9 %patterns.1 = (bf16[32,2,16,256]{3,2,1,0:T(8,128)(2,1)}, bf16[2,2,128,256]{3,2,1,0:T(8,128)(2,1)}, bf16[2,2,128,256]{3,2,1,0:T(8,128)(2,1)}, bf16[2,128,256]{2,1,0:T(8,128)(2,1)}, bf16[2,128,256]{2,1,0:T(8,128)(2,1)}) custom-call(s32[2,2]{1,0:T(2,128)} %live_ref.3, bf16[2,2,2,128,256]{4,3,2,1,0:T(8,128)(2,1)} %unknowns_ref.1, ...), custom_call_target="tpu_custom_call" | custom-call | tf_op jit(solution)/shard_map/patterns/pallas_call | solution.py:304
  2.9 0.5 collective-permute-start
  3.4 7.4 %all-to-all-start = ((bf16[32,2,16,256]{3,2,1,0:T(8,128)(2,1)}), bf16[32,2,16,256]{3,2,1,0:T(8,128)(2,1)S(1)}, u32[]{:S(2)}, u32[]{:S(2)}) async-start(bf16[32,2,16,256]{3,2,1,0:T(8,128)(2,1)} %get-tuple-element.15), calls=%async_computation | async-start | bytes 1048576 | tf_op jit(solution)/shard_map/all_to_all | solution.py:335
  10.8 1.6 %collective-permute-start.4 = (bf16[2,128,256]{2,1,0:T(8,128)(2,1)}, bf16[2,128,256]{2,1,0:T(8,128)(2,1)S(1)}, u32[]{:S(2)}, u32[]{:S(2)}) collective-permute-start(bf16[2,128,256]{2,1,0:T(8,128)(2,1)} %get-tuple-element.23), channel_id=1, source_target_pairs={{0,9},{1,8},{2,11},{3,10},{4,13},{5,12},{6,15},{7,14},{8,1},{9,0},... | collective-permute-start | bytes 393224 | tf_op jit(solution)/shard_map/ppermute | solution.py:53
  12.4 0.4 collective-permute-start.5
  12.7 1.7 %collective-permute-start.1 = (bf16[2,2,128,256]{3,2,1,0:T(8,128)(2,1)}, bf16[2,2,128,256]{3,2,1,0:T(8,128)(2,1)S(1)}, u32[]{:S(2)}, u32[]{:S(2)}) collective-permute-start(bf16[2,2,128,256]{3,2,1,0:T(8,128)(2,1)} %get-tuple-element.16.near_ref), channel_id=1, source_target_pairs={{0,1},{1,0},{2,3},{3,2},{4,5},{5,4},{6,7},{7,6},{8,9},{9,8},{10,11... | collective-permute-start | bytes 786440 | tf_op jit(solution)/shard_map/ppermute | solution.py:43
  14.4 0.0 collective-permute-done.from_cross_ref
  14.4 0.7 %copy-done.6 = bf16[2,2,128,256]{3,2,1,0:T(8,128)(2,1)} copy-done((bf16[2,2,128,256]{3,2,1,0:T(8,128)(2,1)}, bf16[2,2,128,256]{3,2,1,0:T(8,128)(2,1)S(1)}, u32[]{:S(2)}) %copy-start.6) | copy-done | bytes 262168
  15.1 2.0 %rows.1 = (bf16[2,3,128,256]{3,2,1,0:T(8,128)(2,1)}, bf16[2,3,128,256]{3,2,1,0:T(8,128)(2,1)}) custom-call(bf16[2,2,128,256]{3,2,1,0:T(8,128)(2,1)} %get-tuple-element.16.near_ref, bf16[2,2,128,256]{3,2,1,0:T(8,128)(2,1)} %get-tuple-element.17.cross_ref, bf16[2,2,128,256]{3,2,1,0:T(8,128)(2,1)} %copy-done.6), custom_call_target="tpu_custom_call" | custom-call | flops 9200000000 | bytes 29520000 | tf_op jit(solution)/shard_map/rows/pallas_call | solution.py:319
  17.1 0.8 %collective-permute-start.3 = (bf16[2,3,128,256]{3,2,1,0:T(8,128)(2,1)}, bf16[2,3,128,256]{3,2,1,0:T(8,128)(2,1)S(1)}, u32[]{:S(2)}, u32[]{:S(2)}) collective-permute-start(bf16[2,3,128,256]{3,2,1,0:T(8,128)(2,1)} %get-tuple-element.19), channel_id=1, source_target_pairs={{0,1},{1,0},{2,3},{3,2},{4,5},{5,4},{6,7},{7,6},{8,16},{9,17},{10,... | collective-permute-start | bytes 1179656 | tf_op jit(solution)/shard_map/ppermute | solution.py:53
  17.9 0.3 coefficients.1.wide_ref
  18.1 0.9 %collective-permute-start.2 = (bf16[2,3,128,256]{3,2,1,0:T(8,128)(2,1)}, bf16[2,3,128,256]{3,2,1,0:T(8,128)(2,1)S(1)}, u32[]{:S(2)}, u32[]{:S(2)}) collective-permute-start(bf16[2,3,128,256]{3,2,1,0:T(8,128)(2,1)} %get-tuple-element.18), channel_id=1, source_target_pairs={{0,8},{1,9},{2,10},{3,11},{4,12},{5,13},{6,14},{7,15},{8,0},{9,1},... | collective-permute-start | bytes 1179656 | tf_op jit(solution)/shard_map/ppermute | solution.py:53
  19.0 7.3 %all-to-all-done = bf16[32,2,16,256]{3,2,1,0:T(8,128)(2,1)S(1)} async-done(((bf16[32,2,16,256]{3,2,1,0:T(8,128)(2,1)}), bf16[32,2,16,256]{3,2,1,0:T(8,128)(2,1)S(1)}, u32[]{:S(2)}, u32[]{:S(2)}) %all-to-all-start) | async-done | bytes 524320 | tf_op jit(solution)/shard_map/all_to_all | solution.py:335
  26.3 2.0 %translations.1 = bf16[8,4,2,16,256]{4,3,2,1,0:T(8,128)(2,1)} custom-call(bf16[8,4,2,16,256]{4,3,2,1,0:T(8,128)(2,1)S(1)} %bitcast.3, f32[16,3,16,128]{3,2,1,0:T(8,128)S(1)} %coefficients.1.wide_ref), custom_call_target="tpu_custom_call" | custom-call | flops 9200000000 | bytes 29520000 | tf_op jit(solution)/shard_map/translations/pallas_call | solution.py:351
  28.4 3.3 %all-to-all-start.1 = ((bf16[32,2,16,256]{3,2,1,0:T(8,128)(2,1)}), bf16[32,2,16,256]{3,2,1,0:T(8,128)(2,1)S(1)}, u32[]{:S(2)}, u32[]{:S(2)}) async-start(bf16[32,2,16,256]{3,2,1,0:T(8,128)(2,1)} %bitcast.2), calls=%async_computation.1 | async-start | bytes 1048576 | tf_op jit(solution)/shard_map/all_to_all | solution.py:335
  31.6 0.0 copy-start
  31.6 0.0 copy-start.2
  31.7 0.0 collective-permute-done.4.corner_near_ref
  31.7 0.6 %copy-done.10 = bf16[2,128,256]{2,1,0:T(8,128)(2,1)} copy-done((bf16[2,128,256]{2,1,0:T(8,128)(2,1)}, bf16[2,128,256]{2,1,0:T(8,128)(2,1)S(1)}, u32[]{:S(2)}) %copy-start.10) | copy-done | bytes 131096
  32.3 0.0 collective-permute-done.1.from_near_ref
  32.3 0.7 %copy-done.8 = bf16[2,2,128,256]{3,2,1,0:T(8,128)(2,1)} copy-done((bf16[2,2,128,256]{3,2,1,0:T(8,128)(2,1)}, bf16[2,2,128,256]{3,2,1,0:T(8,128)(2,1)S(1)}, u32[]{:S(2)}) %copy-start.8) | copy-done | bytes 262168
  33.0 0.0 collective-permute-done.2.row_near_ref
  33.0 2.4 %collective-permute-done.3.row_cross_ref = bf16[2,3,128,256]{3,2,1,0:T(8,128)(2,1)S(1)} collective-permute-done((bf16[2,3,128,256]{3,2,1,0:T(8,128)(2,1)}, bf16[2,3,128,256]{3,2,1,0:T(8,128)(2,1)S(1)}, u32[]{:S(2)}, u32[]{:S(2)}) %collective-permute-start.3) | collective-permute-done | bytes 393248 | tf_op jit(solution)/shard_map/ppermute | solution.py:53
  35.4 1.7 %copy-done.3 = bf16[2,2,2,9,128,128]{5,4,3,2,1,0:T(8,128)(2,1)S(1)} copy-done((bf16[2,2,2,9,128,128]{5,4,3,2,1,0:T(8,128)(2,1)S(1)}, bf16[2,2,2,9,128,128]{5,4,3,2,1,0:T(8,128)(2,1)}, u32[]{:S(2)}) %copy-start.3) | copy-done | bytes 2359320
  37.1 0.9 %copy-done.4 = bf16[2,2,128,256]{3,2,1,0:T(8,128)(2,1)S(1)} copy-done((bf16[2,2,128,256]{3,2,1,0:T(8,128)(2,1)S(1)}, bf16[2,2,128,256]{3,2,1,0:T(8,128)(2,1)}, u32[]{:S(2)}) %copy-start.4) | copy-done | bytes 262168
  38.0 0.9 %copy-done.5 = bf16[2,2,128,256]{3,2,1,0:T(8,128)(2,1)S(1)} copy-done((bf16[2,2,128,256]{3,2,1,0:T(8,128)(2,1)S(1)}, bf16[2,2,128,256]{3,2,1,0:T(8,128)(2,1)}, u32[]{:S(2)}) %copy-start.5) | copy-done | bytes 262168
  39.0 0.9 %copy-done.7 = bf16[2,2,128,256]{3,2,1,0:T(8,128)(2,1)S(1)} copy-done((bf16[2,2,128,256]{3,2,1,0:T(8,128)(2,1)S(1)}, bf16[2,2,128,256]{3,2,1,0:T(8,128)(2,1)}, u32[]{:S(2)}) %copy-start.7) | copy-done | bytes 262168
  39.9 0.9 %copy-done.9 = bf16[2,2,128,256]{3,2,1,0:T(8,128)(2,1)S(1)} copy-done((bf16[2,2,128,256]{3,2,1,0:T(8,128)(2,1)S(1)}, bf16[2,2,128,256]{3,2,1,0:T(8,128)(2,1)}, u32[]{:S(2)}) %copy-start.9) | copy-done | bytes 262168
  40.9 0.9 %copy-done.11 = bf16[2,128,256]{2,1,0:T(8,128)(2,1)S(1)} copy-done((bf16[2,128,256]{2,1,0:T(8,128)(2,1)S(1)}, bf16[2,128,256]{2,1,0:T(8,128)(2,1)}, u32[]{:S(2)}) %copy-start.11) | copy-done | bytes 131096
  41.8 2.7 %near.1.near_ref = f32[2,2,2,128,256]{4,3,2,1,0:T(8,128)S(1)} custom-call(bf16[2,2,128,256]{3,2,1,0:T(8,128)(2,1)S(1)} %copy-done.4, bf16[2,2,128,256]{3,2,1,0:T(8,128)(2,1)S(1)} %copy-done.5, bf16[2,2,128,256]{3,2,1,0:T(8,128)(2,1)S(1)} %copy-done.7, bf16[2,2,128,256]{3,2,1,0:T(8,128)(2,1)S(1)} %copy-done.9, ...), custom_call_target="tpu_custom_call" | custom-call | flops 13799999488 | bytes 44280000 | tf_op jit(solution)/shard_map/near/pallas_call | solution.py:377
  44.5 2.7 %all-to-all-done.1.incoming_ref = bf16[32,2,16,256]{3,2,1,0:T(8,128)(2,1)S(1)} async-done(((bf16[32,2,16,256]{3,2,1,0:T(8,128)(2,1)}), bf16[32,2,16,256]{3,2,1,0:T(8,128)(2,1)S(1)}, u32[]{:S(2)}, u32[]{:S(2)}) %all-to-all-start.1) | async-done | bytes 524320 | tf_op jit(solution)/shard_map/all_to_all | solution.py:335
  47.2 1.6 %far.1 = f32[2,2,2,128,256]{4,3,2,1,0:T(8,128)} custom-call(s32[2,2]{1,0:T(2,128)S(1)} %copy-done.2, bf16[32,2,16,256]{3,2,1,0:T(8,128)(2,1)S(1)} %all-to-all-done.1.incoming_ref, bf16[2,2,2,128,512]{4,3,2,1,0:T(8,128)(2,1)S(1)} %copy-done, f32[2,2,2,128,256]{4,3,2,1,0:T(8,128)S(1)} %near.1.near_ref), custom_call_target="tpu_custom_call" | custom-call | tf_op jit(solution)/shard_map/far/pallas_call | solution.py:392
  (14 shorter events, 0.0 us)
Async XLA Ops:
  2.9 11.5 %collective-permute-start = (bf16[2,2,128,256]{3,2,1,0:T(8,128)(2,1)}, bf16[2,2,128,256]{3,2,1,0:T(8,128)(2,1)S(1)}, u32[]{:S(2)}, u32[]{:S(2)}) collective-permute-start(bf16[2,2,128,256]{3,2,1,0:T(8,128)(2,1)} %get-tuple-element.17.cross_ref), channel_id=1, source_target_pairs={{0,8},{1,2},{2,1},{3,4},{4,3},{5,6},{6,5},{7,15},{8,0},{9,10},{10,... | collective-permute-start | bytes 786440 | tf_op jit(solution)/shard_map/ppermute | solution.py:43
  3.4 22.9 %all-to-all-start = ((bf16[32,2,16,256]{3,2,1,0:T(8,128)(2,1)}), bf16[32,2,16,256]{3,2,1,0:T(8,128)(2,1)S(1)}, u32[]{:S(2)}, u32[]{:S(2)}) async-start(bf16[32,2,16,256]{3,2,1,0:T(8,128)(2,1)} %get-tuple-element.15), calls=%async_computation | async-start | bytes 1048576 | tf_op jit(solution)/shard_map/all_to_all | solution.py:335
  10.8 20.9 %collective-permute-start.4 = (bf16[2,128,256]{2,1,0:T(8,128)(2,1)}, bf16[2,128,256]{2,1,0:T(8,128)(2,1)S(1)}, u32[]{:S(2)}, u32[]{:S(2)}) collective-permute-start(bf16[2,128,256]{2,1,0:T(8,128)(2,1)} %get-tuple-element.23), channel_id=1, source_target_pairs={{0,9},{1,8},{2,11},{3,10},{4,13},{5,12},{6,15},{7,14},{8,1},{9,0},... | collective-permute-start | bytes 393224 | tf_op jit(solution)/shard_map/ppermute | solution.py:53
  12.4 19.3 %collective-permute-start.5 = (bf16[2,128,256]{2,1,0:T(8,128)(2,1)}, bf16[2,128,256]{2,1,0:T(8,128)(2,1)S(1)}, u32[]{:S(2)}, u32[]{:S(2)}) collective-permute-start(bf16[2,128,256]{2,1,0:T(8,128)(2,1)} %get-tuple-element.24), channel_id=1, source_target_pairs={{0,1},{1,0},{2,3},{3,2},{4,5},{5,4},{6,7},{7,6},{8,17},{9,16},{10,... | collective-permute-start | bytes 393224 | tf_op jit(solution)/shard_map/ppermute | solution.py:53
  12.7 5.1 %copy-start.1 = (f32[16,2,64]{2,1,0:T(2,128)S(1)}, f32[16,2,64]{2,1,0:T(2,128)}, u32[]{:S(2)}) copy-start(f32[16,2,64]{2,1,0:T(2,128)} %param.11) | copy-start | bytes 24580
  12.7 19.6 %collective-permute-start.1 = (bf16[2,2,128,256]{3,2,1,0:T(8,128)(2,1)}, bf16[2,2,128,256]{3,2,1,0:T(8,128)(2,1)S(1)}, u32[]{:S(2)}, u32[]{:S(2)}) collective-permute-start(bf16[2,2,128,256]{3,2,1,0:T(8,128)(2,1)} %get-tuple-element.16.near_ref), channel_id=1, source_target_pairs={{0,1},{1,0},{2,3},{3,2},{4,5},{5,4},{6,7},{7,6},{8,9},{9,8},{10,11... | collective-permute-start | bytes 786440 | tf_op jit(solution)/shard_map/ppermute | solution.py:43
  14.4 0.7 %copy-start.6 = (bf16[2,2,128,256]{3,2,1,0:T(8,128)(2,1)}, bf16[2,2,128,256]{3,2,1,0:T(8,128)(2,1)S(1)}, u32[]{:S(2)}) copy-start(bf16[2,2,128,256]{3,2,1,0:T(8,128)(2,1)S(1)} %collective-permute-done.from_cross_ref) | copy-start | bytes 786436
  17.1 18.4 %collective-permute-start.3 = (bf16[2,3,128,256]{3,2,1,0:T(8,128)(2,1)}, bf16[2,3,128,256]{3,2,1,0:T(8,128)(2,1)S(1)}, u32[]{:S(2)}, u32[]{:S(2)}) collective-permute-start(bf16[2,3,128,256]{3,2,1,0:T(8,128)(2,1)} %get-tuple-element.19), channel_id=1, source_target_pairs={{0,1},{1,0},{2,3},{3,2},{4,5},{5,4},{6,7},{7,6},{8,16},{9,17},{10,... | collective-permute-start | bytes 1179656 | tf_op jit(solution)/shard_map/ppermute | solution.py:53
  18.1 14.9 %collective-permute-start.2 = (bf16[2,3,128,256]{3,2,1,0:T(8,128)(2,1)}, bf16[2,3,128,256]{3,2,1,0:T(8,128)(2,1)S(1)}, u32[]{:S(2)}, u32[]{:S(2)}) collective-permute-start(bf16[2,3,128,256]{3,2,1,0:T(8,128)(2,1)} %get-tuple-element.18), channel_id=1, source_target_pairs={{0,8},{1,9},{2,10},{3,11},{4,12},{5,13},{6,14},{7,15},{8,0},{9,1},... | collective-permute-start | bytes 1179656 | tf_op jit(solution)/shard_map/ppermute | solution.py:53
  28.4 18.8 %all-to-all-start.1 = ((bf16[32,2,16,256]{3,2,1,0:T(8,128)(2,1)}), bf16[32,2,16,256]{3,2,1,0:T(8,128)(2,1)S(1)}, u32[]{:S(2)}, u32[]{:S(2)}) async-start(bf16[32,2,16,256]{3,2,1,0:T(8,128)(2,1)} %bitcast.2), calls=%async_computation.1 | async-start | bytes 1048576 | tf_op jit(solution)/shard_map/all_to_all | solution.py:335
  31.6 15.5 %copy-start = (bf16[2,2,2,128,512]{4,3,2,1,0:T(8,128)(2,1)S(1)}, bf16[2,2,2,128,512]{4,3,2,1,0:T(8,128)(2,1)}, u32[]{:S(2)}) copy-start(bf16[2,2,2,128,512]{4,3,2,1,0:T(8,128)(2,1)} %disaggregate_ref.1) | copy-start | bytes 3145732
  31.6 15.5 %copy-start.2 = (s32[2,2]{1,0:T(2,128)S(1)}, s32[2,2]{1,0:T(2,128)}, u32[]{:S(2)}) copy-start(s32[2,2]{1,0:T(2,128)} %live_ref.3) | copy-start | bytes 52
  31.7 0.6 %copy-start.10 = (bf16[2,128,256]{2,1,0:T(8,128)(2,1)}, bf16[2,128,256]{2,1,0:T(8,128)(2,1)S(1)}, u32[]{:S(2)}) copy-start(bf16[2,128,256]{2,1,0:T(8,128)(2,1)S(1)} %collective-permute-done.5.corner_cross_ref) | copy-start | bytes 393220
  32.3 0.7 %copy-start.8 = (bf16[2,2,128,256]{3,2,1,0:T(8,128)(2,1)}, bf16[2,2,128,256]{3,2,1,0:T(8,128)(2,1)S(1)}, u32[]{:S(2)}) copy-start(bf16[2,2,128,256]{3,2,1,0:T(8,128)(2,1)S(1)} %collective-permute-done.1.from_near_ref) | copy-start | bytes 786436
  35.4 1.7 %copy-start.3 = (bf16[2,2,2,9,128,128]{5,4,3,2,1,0:T(8,128)(2,1)S(1)}, bf16[2,2,2,9,128,128]{5,4,3,2,1,0:T(8,128)(2,1)}, u32[]{:S(2)}) copy-start(bf16[2,2,2,9,128,128]{5,4,3,2,1,0:T(8,128)(2,1)} %blocks_ref.1) | copy-start | bytes 7077892
  37.1 0.9 %copy-start.4 = (bf16[2,2,128,256]{3,2,1,0:T(8,128)(2,1)S(1)}, bf16[2,2,128,256]{3,2,1,0:T(8,128)(2,1)}, u32[]{:S(2)}) copy-start(bf16[2,2,128,256]{3,2,1,0:T(8,128)(2,1)} %get-tuple-element.16.near_ref) | copy-start | bytes 786436
  38.0 0.9 %copy-start.5 = (bf16[2,2,128,256]{3,2,1,0:T(8,128)(2,1)S(1)}, bf16[2,2,128,256]{3,2,1,0:T(8,128)(2,1)}, u32[]{:S(2)}) copy-start(bf16[2,2,128,256]{3,2,1,0:T(8,128)(2,1)} %get-tuple-element.17.cross_ref) | copy-start | bytes 786436
  39.0 0.9 %copy-start.7 = (bf16[2,2,128,256]{3,2,1,0:T(8,128)(2,1)S(1)}, bf16[2,2,128,256]{3,2,1,0:T(8,128)(2,1)}, u32[]{:S(2)}) copy-start(bf16[2,2,128,256]{3,2,1,0:T(8,128)(2,1)} %copy-done.6) | copy-start | bytes 786436
  39.9 0.9 %copy-start.9 = (bf16[2,2,128,256]{3,2,1,0:T(8,128)(2,1)S(1)}, bf16[2,2,128,256]{3,2,1,0:T(8,128)(2,1)}, u32[]{:S(2)}) copy-start(bf16[2,2,128,256]{3,2,1,0:T(8,128)(2,1)} %copy-done.8) | copy-start | bytes 786436
  40.9 0.9 %copy-start.11 = (bf16[2,128,256]{2,1,0:T(8,128)(2,1)S(1)}, bf16[2,128,256]{2,1,0:T(8,128)(2,1)}, u32[]{:S(2)}) copy-start(bf16[2,128,256]{2,1,0:T(8,128)(2,1)} %copy-done.10) | copy-start | bytes 393220

commit v10 on v9

--- a/solution.py
+++ b/solution.py
@@ -118,9 +118,13 @@
         wide_ref[index, 2] = real + imag
 
 
-def translate_kernel(from_ref, wide_ref, out_ref, held_ref):
+def translate_kernel(from_ref, wide_ref, out_ref, held_ref, made_ref, sem):
     box_cols, box_rows, _, narrow, sides = from_ref.shape
     lanes = min(128, sides)
+
+    def departure(place):
+        across = pl.ds(pl.multiple_of(place * lanes, lanes), lanes)
+        return pltpu.make_async_copy(made_ref.at[..., across], out_ref.at[..., across], sem.at[place])
 
     def tile(place, carry):
         across = pl.ds(pl.multiple_of(place * lanes, lanes), lanes)
@@ -151,14 +155,17 @@
                     totals[target] = term if old is None else [x + y for x, y in zip(old, term)]
             for target, total in enumerate(totals):
                 for c in range(2):
-                    out_ref[col, target, c, :, across] = (
+                    made_ref[col, target, c, :, across] = (
                         jnp.zeros((narrow, lanes), jnp.bfloat16)
                         if total is None
                         else total[c].astype(jnp.bfloat16)
                     )
+        departure(place).start()
         return carry
 
     lax.fori_loop(0, sides // lanes, tile, 0, unroll=True)
+    for place in range(sides // lanes):
+        departure(place).wait()
 
 
 def translate_grid(sources, coefs):
@@ -351,10 +358,12 @@
         incoming = pl.pallas_call(
             translate_kernel,
             in_specs=[VMEM] * 2,
-            out_specs=VMEM,
+            out_specs=ANY,
             out_shape=jax.ShapeDtypeStruct(own.shape, bf16),
             scratch_shapes=[
                 pltpu.VMEM((dir_count, sect_count, 3, narrow, lanes), f32),
+                pltpu.VMEM(own.shape, bf16),
+                pltpu.SemaphoreType.DMA((sides // lanes,)),
             ],
             compiler_params=params(16),
             cost_estimate=cost(8),

time: 49.3 us -> 49.2 us (level)
  no operation moved by 1% of the time
where the time goes in v10:
time: 49.2 us; the launch traced here: 48.8 us
  starting transfers between devices  16.4 us (33%)
  waiting for transfers between devices  12.4 us (25%)
  Pallas kernels  11.4 us (23%)
  local copies, waits for them, and re-layouts  8.41 us (17%)
    all_to_all x2, starting transfers between devices, spread(): lax.all_to_all(flat, ('dir', 'sect'), split_axis=0, concat_axis=0, tiled=...  10.6 us
    all_to_all x2, waiting for transfers between devices, spread(): lax.all_to_all(flat, ('dir', 'sect'), split_axis=0, concat_axis=0, tiled=...  9.78 us
    unnamed x24, local copies, waits for them, and re-layouts  8.41 us
    ppermute x4, starting transfers between devices, swap_rows(): return lax.ppermute(array, ('sect', 'dir'), sends)  3.62 us
    pallas_call x1, Pallas kernels, shards(): pl.pallas_call(pattern_kernel, in_specs=[pl.BlockSpec(memory_space=pltpu....  2.94 us
    pallas_call x1, Pallas kernels, shards(): pl.pallas_call(near_kernel, grid=(deep * wide,), in_specs=[VMEM] * 8 + [p...  2.66 us
    ppermute x4, waiting for transfers between devices, swap_rows(): return lax.ppermute(array, ('sect', 'dir'), sends)  2.65 us
    ppermute x2, starting transfers between devices, swap_cols(): return lax.ppermute(array, ('sect', 'dir'), sends)  2.12 us
  transfers between devices with their start and end apart: 8, of which 3 were waited for; matrix products, arithmetic and copies ran while one was open for 0% of the time, Pallas kernels for 14%

profile of v10, /device:TPU:0, one launch (start us, length us, event | category | flops | bytes accessed | tf_op | source)
XLA Modules:
  0.0 48.8 jit_solution(15186125470412260827)
XLA Ops:
  0.0 2.9 %patterns.1 = (bf16[32,2,16,256]{3,2,1,0:T(8,128)(2,1)}, bf16[2,2,128,256]{3,2,1,0:T(8,128)(2,1)}, bf16[2,2,128,256]{3,2,1,0:T(8,128)(2,1)}, bf16[2,128,256]{2,1,0:T(8,128)(2,1)}, bf16[2,128,256]{2,1,0:T(8,128)(2,1)}) custom-call(s32[2,2]{1,0:T(2,128)} %live_ref.3, bf16[2,2,2,128,256]{4,3,2,1,0:T(8,128)(2,1)} %unknowns_ref.1, ...), custom_call_target="tpu_custom_call" | custom-call | tf_op jit(solution)/shard_map/patterns/pallas_call | solution.py:311
  2.9 0.5 collective-permute-start
  3.4 7.4 %all-to-all-start = ((bf16[32,2,16,256]{3,2,1,0:T(8,128)(2,1)}), bf16[32,2,16,256]{3,2,1,0:T(8,128)(2,1)S(1)}, u32[]{:S(2)}, u32[]{:S(2)}) async-start(bf16[32,2,16,256]{3,2,1,0:T(8,128)(2,1)} %get-tuple-element.15), calls=%async_computation | async-start | bytes 1048576 | tf_op jit(solution)/shard_map/all_to_all | solution.py:342
  10.8 1.6 %collective-permute-start.4 = (bf16[2,128,256]{2,1,0:T(8,128)(2,1)}, bf16[2,128,256]{2,1,0:T(8,128)(2,1)S(1)}, u32[]{:S(2)}, u32[]{:S(2)}) collective-permute-start(bf16[2,128,256]{2,1,0:T(8,128)(2,1)} %get-tuple-element.23), channel_id=1, source_target_pairs={{0,9},{1,8},{2,11},{3,10},{4,13},{5,12},{6,15},{7,14},{8,1},{9,0},... | collective-permute-start | bytes 393224 | tf_op jit(solution)/shard_map/ppermute | solution.py:53
  12.4 0.4 collective-permute-start.5
  12.7 1.7 %collective-permute-start.1 = (bf16[2,2,128,256]{3,2,1,0:T(8,128)(2,1)}, bf16[2,2,128,256]{3,2,1,0:T(8,128)(2,1)S(1)}, u32[]{:S(2)}, u32[]{:S(2)}) collective-permute-start(bf16[2,2,128,256]{3,2,1,0:T(8,128)(2,1)} %get-tuple-element.16.near_ref), channel_id=1, source_target_pairs={{0,1},{1,0},{2,3},{3,2},{4,5},{5,4},{6,7},{7,6},{8,9},{9,8},{10,11... | collective-permute-start | bytes 786440 | tf_op jit(solution)/shard_map/ppermute | solution.py:43
  14.4 0.0 collective-permute-done.from_cross_ref
  14.4 0.7 %copy-done.6 = bf16[2,2,128,256]{3,2,1,0:T(8,128)(2,1)} copy-done((bf16[2,2,128,256]{3,2,1,0:T(8,128)(2,1)}, bf16[2,2,128,256]{3,2,1,0:T(8,128)(2,1)S(1)}, u32[]{:S(2)}) %copy-start.6) | copy-done | bytes 262168
  15.1 2.0 %rows.1 = (bf16[2,3,128,256]{3,2,1,0:T(8,128)(2,1)}, bf16[2,3,128,256]{3,2,1,0:T(8,128)(2,1)}) custom-call(bf16[2,2,128,256]{3,2,1,0:T(8,128)(2,1)} %get-tuple-element.16.near_ref, bf16[2,2,128,256]{3,2,1,0:T(8,128)(2,1)} %get-tuple-element.17.cross_ref, bf16[2,2,128,256]{3,2,1,0:T(8,128)(2,1)} %copy-done.6), custom_call_target="tpu_custom_call" | custom-call | flops 9200000000 | bytes 29520000 | tf_op jit(solution)/shard_map/rows/pallas_call | solution.py:326
  17.1 0.8 %collective-permute-start.3 = (bf16[2,3,128,256]{3,2,1,0:T(8,128)(2,1)}, bf16[2,3,128,256]{3,2,1,0:T(8,128)(2,1)S(1)}, u32[]{:S(2)}, u32[]{:S(2)}) collective-permute-start(bf16[2,3,128,256]{3,2,1,0:T(8,128)(2,1)} %get-tuple-element.19), channel_id=1, source_target_pairs={{0,1},{1,0},{2,3},{3,2},{4,5},{5,4},{6,7},{7,6},{8,16},{9,17},{10,... | collective-permute-start | bytes 1179656 | tf_op jit(solution)/shard_map/ppermute | solution.py:53
  17.9 0.3 coefficients.1.wide_ref
  18.1 0.9 %collective-permute-start.2 = (bf16[2,3,128,256]{3,2,1,0:T(8,128)(2,1)}, bf16[2,3,128,256]{3,2,1,0:T(8,128)(2,1)S(1)}, u32[]{:S(2)}, u32[]{:S(2)}) collective-permute-start(bf16[2,3,128,256]{3,2,1,0:T(8,128)(2,1)} %get-tuple-element.18), channel_id=1, source_target_pairs={{0,8},{1,9},{2,10},{3,11},{4,12},{5,13},{6,14},{7,15},{8,0},{9,1},... | collective-permute-start | bytes 1179656 | tf_op jit(solution)/shard_map/ppermute | solution.py:53
  19.0 7.3 %all-to-all-done = bf16[32,2,16,256]{3,2,1,0:T(8,128)(2,1)S(1)} async-done(((bf16[32,2,16,256]{3,2,1,0:T(8,128)(2,1)}), bf16[32,2,16,256]{3,2,1,0:T(8,128)(2,1)S(1)}, u32[]{:S(2)}, u32[]{:S(2)}) %all-to-all-start) | async-done | bytes 524320 | tf_op jit(solution)/shard_map/all_to_all | solution.py:342
  26.3 2.0 %translations.1 = bf16[8,4,2,16,256]{4,3,2,1,0:T(8,128)(2,1)} custom-call(bf16[8,4,2,16,256]{4,3,2,1,0:T(8,128)(2,1)S(1)} %bitcast.3, f32[16,3,16,128]{3,2,1,0:T(8,128)S(1)} %coefficients.1.wide_ref), custom_call_target="tpu_custom_call" | custom-call | flops 9200000000 | bytes 29520000 | tf_op jit(solution)/shard_map/translations/pallas_call | solution.py:358
  28.3 3.3 %all-to-all-start.1 = ((bf16[32,2,16,256]{3,2,1,0:T(8,128)(2,1)}), bf16[32,2,16,256]{3,2,1,0:T(8,128)(2,1)S(1)}, u32[]{:S(2)}, u32[]{:S(2)}) async-start(bf16[32,2,16,256]{3,2,1,0:T(8,128)(2,1)} %bitcast.2), calls=%async_computation.1 | async-start | bytes 1048576 | tf_op jit(solution)/shard_map/all_to_all | solution.py:342
  31.6 0.0 copy-start
  31.6 0.0 copy-start.2
  31.6 0.0 collective-permute-done.4.corner_near_ref
  31.6 0.6 %copy-done.10 = bf16[2,128,256]{2,1,0:T(8,128)(2,1)} copy-done((bf16[2,128,256]{2,1,0:T(8,128)(2,1)}, bf16[2,128,256]{2,1,0:T(8,128)(2,1)S(1)}, u32[]{:S(2)}) %copy-start.10) | copy-done | bytes 131096
  32.3 0.0 collective-permute-done.1.from_near_ref
  32.3 0.7 %copy-done.8 = bf16[2,2,128,256]{3,2,1,0:T(8,128)(2,1)} copy-done((bf16[2,2,128,256]{3,2,1,0:T(8,128)(2,1)}, bf16[2,2,128,256]{3,2,1,0:T(8,128)(2,1)S(1)}, u32[]{:S(2)}) %copy-start.8) | copy-done | bytes 262168
  33.0 0.0 collective-permute-done.2.row_near_ref
  33.0 2.6 %collective-permute-done.3.row_cross_ref = bf16[2,3,128,256]{3,2,1,0:T(8,128)(2,1)S(1)} collective-permute-done((bf16[2,3,128,256]{3,2,1,0:T(8,128)(2,1)}, bf16[2,3,128,256]{3,2,1,0:T(8,128)(2,1)S(1)}, u32[]{:S(2)}, u32[]{:S(2)}) %collective-permute-start.3) | collective-permute-done | bytes 393248 | tf_op jit(solution)/shard_map/ppermute | solution.py:53
  35.6 1.7 %copy-done.3 = bf16[2,2,2,9,128,128]{5,4,3,2,1,0:T(8,128)(2,1)S(1)} copy-done((bf16[2,2,2,9,128,128]{5,4,3,2,1,0:T(8,128)(2,1)S(1)}, bf16[2,2,2,9,128,128]{5,4,3,2,1,0:T(8,128)(2,1)}, u32[]{:S(2)}) %copy-start.3) | copy-done | bytes 2359320
  37.3 0.9 %copy-done.4 = bf16[2,2,128,256]{3,2,1,0:T(8,128)(2,1)S(1)} copy-done((bf16[2,2,128,256]{3,2,1,0:T(8,128)(2,1)S(1)}, bf16[2,2,128,256]{3,2,1,0:T(8,128)(2,1)}, u32[]{:S(2)}) %copy-start.4) | copy-done | bytes 262168
  38.2 0.9 %copy-done.5 = bf16[2,2,128,256]{3,2,1,0:T(8,128)(2,1)S(1)} copy-done((bf16[2,2,128,256]{3,2,1,0:T(8,128)(2,1)S(1)}, bf16[2,2,128,256]{3,2,1,0:T(8,128)(2,1)}, u32[]{:S(2)}) %copy-start.5) | copy-done | bytes 262168
  39.2 0.9 %copy-done.7 = bf16[2,2,128,256]{3,2,1,0:T(8,128)(2,1)S(1)} copy-done((bf16[2,2,128,256]{3,2,1,0:T(8,128)(2,1)S(1)}, bf16[2,2,128,256]{3,2,1,0:T(8,128)(2,1)}, u32[]{:S(2)}) %copy-start.7) | copy-done | bytes 262168
  40.1 0.9 %copy-done.9 = bf16[2,2,128,256]{3,2,1,0:T(8,128)(2,1)S(1)} copy-done((bf16[2,2,128,256]{3,2,1,0:T(8,128)(2,1)S(1)}, bf16[2,2,128,256]{3,2,1,0:T(8,128)(2,1)}, u32[]{:S(2)}) %copy-start.9) | copy-done | bytes 262168
  41.1 0.9 %copy-done.11 = bf16[2,128,256]{2,1,0:T(8,128)(2,1)S(1)} copy-done((bf16[2,128,256]{2,1,0:T(8,128)(2,1)S(1)}, bf16[2,128,256]{2,1,0:T(8,128)(2,1)}, u32[]{:S(2)}) %copy-start.11) | copy-done | bytes 131096
  42.0 2.7 %near.1.near_ref = f32[2,2,2,128,256]{4,3,2,1,0:T(8,128)S(1)} custom-call(bf16[2,2,128,256]{3,2,1,0:T(8,128)(2,1)S(1)} %copy-done.4, bf16[2,2,128,256]{3,2,1,0:T(8,128)(2,1)S(1)} %copy-done.5, bf16[2,2,128,256]{3,2,1,0:T(8,128)(2,1)S(1)} %copy-done.7, bf16[2,2,128,256]{3,2,1,0:T(8,128)(2,1)S(1)} %copy-done.9, ...), custom_call_target="tpu_custom_call" | custom-call | flops 13799999488 | bytes 44280000 | tf_op jit(solution)/shard_map/near/pallas_call | solution.py:386
  44.7 2.5 %all-to-all-done.1.incoming_ref = bf16[32,2,16,256]{3,2,1,0:T(8,128)(2,1)S(1)} async-done(((bf16[32,2,16,256]{3,2,1,0:T(8,128)(2,1)}), bf16[32,2,16,256]{3,2,1,0:T(8,128)(2,1)S(1)}, u32[]{:S(2)}, u32[]{:S(2)}) %all-to-all-start.1) | async-done | bytes 524320 | tf_op jit(solution)/shard_map/all_to_all | solution.py:342
  47.1 1.6 %far.1 = f32[2,2,2,128,256]{4,3,2,1,0:T(8,128)} custom-call(s32[2,2]{1,0:T(2,128)S(1)} %copy-done.2, bf16[32,2,16,256]{3,2,1,0:T(8,128)(2,1)S(1)} %all-to-all-done.1.incoming_ref, bf16[2,2,2,128,512]{4,3,2,1,0:T(8,128)(2,1)S(1)} %copy-done, f32[2,2,2,128,256]{4,3,2,1,0:T(8,128)S(1)} %near.1.near_ref), custom_call_target="tpu_custom_call" | custom-call | tf_op jit(solution)/shard_map/far/pallas_call | solution.py:401
  (14 shorter events, 0.0 us)
Async XLA Ops:
  2.9 11.5 %collective-permute-start = (bf16[2,2,128,256]{3,2,1,0:T(8,128)(2,1)}, bf16[2,2,128,256]{3,2,1,0:T(8,128)(2,1)S(1)}, u32[]{:S(2)}, u32[]{:S(2)}) collective-permute-start(bf16[2,2,128,256]{3,2,1,0:T(8,128)(2,1)} %get-tuple-element.17.cross_ref), channel_id=1, source_target_pairs={{0,8},{1,2},{2,1},{3,4},{4,3},{5,6},{6,5},{7,15},{8,0},{9,10},{10,... | collective-permute-start | bytes 786440 | tf_op jit(solution)/shard_map/ppermute | solution.py:43
  3.4 22.9 %all-to-all-start = ((bf16[32,2,16,256]{3,2,1,0:T(8,128)(2,1)}), bf16[32,2,16,256]{3,2,1,0:T(8,128)(2,1)S(1)}, u32[]{:S(2)}, u32[]{:S(2)}) async-start(bf16[32,2,16,256]{3,2,1,0:T(8,128)(2,1)} %get-tuple-element.15), calls=%async_computation | async-start | bytes 1048576 | tf_op jit(solution)/shard_map/all_to_all | solution.py:342
  10.8 20.8 %collective-permute-start.4 = (bf16[2,128,256]{2,1,0:T(8,128)(2,1)}, bf16[2,128,256]{2,1,0:T(8,128)(2,1)S(1)}, u32[]{:S(2)}, u32[]{:S(2)}) collective-permute-start(bf16[2,128,256]{2,1,0:T(8,128)(2,1)} %get-tuple-element.23), channel_id=1, source_target_pairs={{0,9},{1,8},{2,11},{3,10},{4,13},{5,12},{6,15},{7,14},{8,1},{9,0},... | collective-permute-start | bytes 393224 | tf_op jit(solution)/shard_map/ppermute | solution.py:53
  12.4 19.2 %collective-permute-start.5 = (bf16[2,128,256]{2,1,0:T(8,128)(2,1)}, bf16[2,128,256]{2,1,0:T(8,128)(2,1)S(1)}, u32[]{:S(2)}, u32[]{:S(2)}) collective-permute-start(bf16[2,128,256]{2,1,0:T(8,128)(2,1)} %get-tuple-element.24), channel_id=1, source_target_pairs={{0,1},{1,0},{2,3},{3,2},{4,5},{5,4},{6,7},{7,6},{8,17},{9,16},{10,... | collective-permute-start | bytes 393224 | tf_op jit(solution)/shard_map/ppermute | solution.py:53
  12.7 5.1 %copy-start.1 = (f32[16,2,64]{2,1,0:T(2,128)S(1)}, f32[16,2,64]{2,1,0:T(2,128)}, u32[]{:S(2)}) copy-start(f32[16,2,64]{2,1,0:T(2,128)} %param.11) | copy-start | bytes 24580
  12.7 19.5 %collective-permute-start.1 = (bf16[2,2,128,256]{3,2,1,0:T(8,128)(2,1)}, bf16[2,2,128,256]{3,2,1,0:T(8,128)(2,1)S(1)}, u32[]{:S(2)}, u32[]{:S(2)}) collective-permute-start(bf16[2,2,128,256]{3,2,1,0:T(8,128)(2,1)} %get-tuple-element.16.near_ref), channel_id=1, source_target_pairs={{0,1},{1,0},{2,3},{3,2},{4,5},{5,4},{6,7},{7,6},{8,9},{9,8},{10,11... | collective-permute-start | bytes 786440 | tf_op jit(solution)/shard_map/ppermute | solution.py:43
  14.4 0.7 %copy-start.6 = (bf16[2,2,128,256]{3,2,1,0:T(8,128)(2,1)}, bf16[2,2,128,256]{3,2,1,0:T(8,128)(2,1)S(1)}, u32[]{:S(2)}) copy-start(bf16[2,2,128,256]{3,2,1,0:T(8,128)(2,1)S(1)} %collective-permute-done.from_cross_ref) | copy-start | bytes 786436
  17.1 18.5 %collective-permute-start.3 = (bf16[2,3,128,256]{3,2,1,0:T(8,128)(2,1)}, bf16[2,3,128,256]{3,2,1,0:T(8,128)(2,1)S(1)}, u32[]{:S(2)}, u32[]{:S(2)}) collective-permute-start(bf16[2,3,128,256]{3,2,1,0:T(8,128)(2,1)} %get-tuple-element.19), channel_id=1, source_target_pairs={{0,1},{1,0},{2,3},{3,2},{4,5},{5,4},{6,7},{7,6},{8,16},{9,17},{10,... | collective-permute-start | bytes 1179656 | tf_op jit(solution)/shard_map/ppermute | solution.py:53
  18.1 14.8 %collective-permute-start.2 = (bf16[2,3,128,256]{3,2,1,0:T(8,128)(2,1)}, bf16[2,3,128,256]{3,2,1,0:T(8,128)(2,1)S(1)}, u32[]{:S(2)}, u32[]{:S(2)}) collective-permute-start(bf16[2,3,128,256]{3,2,1,0:T(8,128)(2,1)} %get-tuple-element.18), channel_id=1, source_target_pairs={{0,8},{1,9},{2,10},{3,11},{4,12},{5,13},{6,14},{7,15},{8,0},{9,1},... | collective-permute-start | bytes 1179656 | tf_op jit(solution)/shard_map/ppermute | solution.py:53
  28.3 18.8 %all-to-all-start.1 = ((bf16[32,2,16,256]{3,2,1,0:T(8,128)(2,1)}), bf16[32,2,16,256]{3,2,1,0:T(8,128)(2,1)S(1)}, u32[]{:S(2)}, u32[]{:S(2)}) async-start(bf16[32,2,16,256]{3,2,1,0:T(8,128)(2,1)} %bitcast.2), calls=%async_computation.1 | async-start | bytes 1048576 | tf_op jit(solution)/shard_map/all_to_all | solution.py:342
  31.6 15.5 %copy-start = (bf16[2,2,2,128,512]{4,3,2,1,0:T(8,128)(2,1)S(1)}, bf16[2,2,2,128,512]{4,3,2,1,0:T(8,128)(2,1)}, u32[]{:S(2)}) copy-start(bf16[2,2,2,128,512]{4,3,2,1,0:T(8,128)(2,1)} %disaggregate_ref.1) | copy-start | bytes 3145732
  31.6 15.5 %copy-start.2 = (s32[2,2]{1,0:T(2,128)S(1)}, s32[2,2]{1,0:T(2,128)}, u32[]{:S(2)}) copy-start(s32[2,2]{1,0:T(2,128)} %live_ref.3) | copy-start | bytes 52
  31.6 0.6 %copy-start.10 = (bf16[2,128,256]{2,1,0:T(8,128)(2,1)}, bf16[2,128,256]{2,1,0:T(8,128)(2,1)S(1)}, u32[]{:S(2)}) copy-start(bf16[2,128,256]{2,1,0:T(8,128)(2,1)S(1)} %collective-permute-done.5.corner_cross_ref) | copy-start | bytes 393220
  32.3 0.7 %copy-start.8 = (bf16[2,2,128,256]{3,2,1,0:T(8,128)(2,1)}, bf16[2,2,128,256]{3,2,1,0:T(8,128)(2,1)S(1)}, u32[]{:S(2)}) copy-start(bf16[2,2,128,256]{3,2,1,0:T(8,128)(2,1)S(1)} %collective-permute-done.1.from_near_ref) | copy-start | bytes 786436
  35.6 1.7 %copy-start.3 = (bf16[2,2,2,9,128,128]{5,4,3,2,1,0:T(8,128)(2,1)S(1)}, bf16[2,2,2,9,128,128]{5,4,3,2,1,0:T(8,128)(2,1)}, u32[]{:S(2)}) copy-start(bf16[2,2,2,9,128,128]{5,4,3,2,1,0:T(8,128)(2,1)} %blocks_ref.1) | copy-start | bytes 7077892
  37.3 0.9 %copy-start.4 = (bf16[2,2,128,256]{3,2,1,0:T(8,128)(2,1)S(1)}, bf16[2,2,128,256]{3,2,1,0:T(8,128)(2,1)}, u32[]{:S(2)}) copy-start(bf16[2,2,128,256]{3,2,1,0:T(8,128)(2,1)} %get-tuple-element.16.near_ref) | copy-start | bytes 786436
  38.2 0.9 %copy-start.5 = (bf16[2,2,128,256]{3,2,1,0:T(8,128)(2,1)S(1)}, bf16[2,2,128,256]{3,2,1,0:T(8,128)(2,1)}, u32[]{:S(2)}) copy-start(bf16[2,2,128,256]{3,2,1,0:T(8,128)(2,1)} %get-tuple-element.17.cross_ref) | copy-start | bytes 786436
  39.2 0.9 %copy-start.7 = (bf16[2,2,128,256]{3,2,1,0:T(8,128)(2,1)S(1)}, bf16[2,2,128,256]{3,2,1,0:T(8,128)(2,1)}, u32[]{:S(2)}) copy-start(bf16[2,2,128,256]{3,2,1,0:T(8,128)(2,1)} %copy-done.6) | copy-start | bytes 786436
  40.1 0.9 %copy-start.9 = (bf16[2,2,128,256]{3,2,1,0:T(8,128)(2,1)S(1)}, bf16[2,2,128,256]{3,2,1,0:T(8,128)(2,1)}, u32[]{:S(2)}) copy-start(bf16[2,2,128,256]{3,2,1,0:T(8,128)(2,1)} %copy-done.8) | copy-start | bytes 786436
  41.1 0.9 %copy-start.11 = (bf16[2,128,256]{2,1,0:T(8,128)(2,1)S(1)}, bf16[2,128,256]{2,1,0:T(8,128)(2,1)}, u32[]{:S(2)}) copy-start(bf16[2,128,256]{2,1,0:T(8,128)(2,1)} %copy-done.10) | copy-start | bytes 393220
